TPU v7x, 128 devices: a whole 4x4x4 slice. The times are simulated.
128 devices in a mesh: batch: 128 (over y, x, z, core).
Axes of the slice: x: 4, y: 4, z: 4, core: 2. Of those that a mesh axis runs over, the one named last changes fastest.
Arguments:
- features: bfloat16 [131072, 1024], P('batch'), may hold values from -24 to 24
- head: bfloat16 [1024, 256], replicated, may hold values from -0.1875 to 0.1875
- partner: int32 [131072], P('batch'), may hold values from 0 to 131071, as said below
Outputs:
- feature_grad: bfloat16 [131072, 1024], P('batch')
- head_grad: float32 [1024, 256], P('batch')
Inputs may be any that keep to these rules, and one draw needn't show every extreme that they name: `partner`: partner_i differs from i and lies in a block 1 to 4 blocks away from i's block, circularly.
All inputs are finite; a program needn't handle non-finite values.
Results may differ from a plain program's by a relative error of at most 0.0058.
Values may be sent and summed in bfloat16 or wider, within the bound.
No kernel may reach another device: no remote copies, remote signals or barrier semaphores. Data moves between devices by JAX's collectives and lax.ppermute only.
A program may use at most 64 MiB of HBM per device.

v0:
```python
import jax
import jax.numpy as jnp
from jax import lax
from jax.sharding import PartitionSpec as P

ROUNDS = 4


def passed_along(x, axis, by):
    size = lax.axis_size(axis)
    return lax.ppermute(x, axis, [(i, (i + by) % size) for i in range(size)])


def tile_coef(z_a, ids_a, part_a, z_b, ids_b, part_b, total):
    scores = jnp.dot(z_a, z_b.T, preferred_element_type=jnp.float32)
    positive = (part_a[:, None] == ids_b[None, :]) | (part_b[None, :] == ids_a[:, None])
    signs = jnp.where(positive, 1.0, -1.0).astype(jnp.float32)
    logits = 10.0 * scores - 10.0
    coef = -signs * jax.nn.sigmoid(-signs * logits) * (20.0 / total)
    return jnp.where(ids_a[:, None] != ids_b[None, :], coef, 0.0).astype(jnp.bfloat16)


def per_device(features, head, partner):
    rows = features.shape[0]
    count = lax.axis_size("batch")
    owner = lax.axis_index("batch")
    total = float(rows * count)
    raw = jnp.dot(features, head, preferred_element_type=jnp.float32)
    scale = lax.rsqrt(jnp.sum(raw * raw, axis=1, keepdims=True) + 1e-06)
    unit = raw * scale
    embed = unit.astype(jnp.bfloat16)
    local = jnp.arange(rows, dtype=jnp.int32)
    my_ids = owner * rows + local
    coef = tile_coef(embed, my_ids, partner, embed, my_ids, partner, total)
    grad = jnp.dot(coef, embed, preferred_element_type=jnp.float32)
    for step in range(1, ROUNDS + 1):
        other_z, other_p = passed_along((embed, partner), "batch", step)
        other_ids = (owner - step) % count * rows + local
        coef = tile_coef(embed, my_ids, partner, other_z, other_ids, other_p, total)
        grad = grad + jnp.dot(coef, other_z, preferred_element_type=jnp.float32)
        backward = jnp.dot(coef.T, embed, preferred_element_type=jnp.float32).astype(jnp.bfloat16)
        returned = passed_along(backward, "batch", -step)
        grad = grad + returned.astype(jnp.float32)
    raw_grad = ((grad - unit * jnp.sum(unit * grad, axis=1, keepdims=True)) * scale).astype(
        jnp.bfloat16
    )
    feature_grad = jnp.dot(raw_grad, head.T, preferred_element_type=jnp.float32).astype(
        jnp.bfloat16
    )
    head_grad = lax.psum_scatter(
        lax.dot_general(
            features, raw_grad, (((0,), (0,)), ((), ())), preferred_element_type=jnp.float32
        ),
        "batch",
        scatter_dimension=0,
        tiled=True,
    )
    return (feature_grad, head_grad)


def solution(mesh):
    in_specs = (P("batch", None), P(), P("batch"))
    out_specs = (P("batch", None), P("batch", None))
    return jax.shard_map(
        per_device, mesh=mesh, in_specs=in_specs, out_specs=out_specs, check_vma=False
    )
```

profile of v0, /device:TPU:1, one launch (start us, length us, event | category | flops | bytes accessed | tf_op | source)
XLA Modules:
  0.0 744.3 jit_solution(14218663807094003303)
XLA Ops:
  7.2 0.0 copy-start
  7.2 0.0 copy-start.5
  7.2 0.0 reduce-scatter.4.cloned.1.call-start
  7.2 1.5 copy-done
  8.8 1.8 multiply_reduce_fusion.1
  10.6 0.9 multiply_convert_fusion.1
  11.5 4.4 collective-permute-start.10
  15.9 1.1 collective-permute-start.7
  17.0 0.0 copy-done.5
  17.0 3.6 collective-permute-start.9
  20.6 0.5 collective-permute-start.6
  21.1 0.6 collective-permute-start.4
  21.7 5.2 fusion.3
  26.9 14.7 %collective-permute-done.9 = s32[1024]{0:T(1024)S(1)} collective-permute-done((s32[1024]{0:T(1024)S(1)}, s32[1024]{0:T(1024)S(1)}, u32[]{:S(2)}, u32[]{:S(2)}) %collective-permute-start.9) | collective-permute-done | bytes 4128 | tf_op jit(solution)/shard_map/ppermute | solution.py:11
  41.6 2.7 collective-permute-start.3
  44.3 0.0 collective-permute-done.10
  44.3 2.2 collective-permute-start.1
  46.6 3.7 select_convert_fusion
  50.3 1.8 convolution_convert_fusion.1
  52.1 0.0 collective-permute-done.6
  52.1 0.1 collective-permute-start
  52.2 0.0 collective-permute-done.7
  52.2 3.5 collective-permute-start.11
  55.6 3.7 select_convert_fusion.1
  59.4 1.8 convolution_convert_fusion.2
  61.1 0.0 collective-permute-done.3
  61.2 4.1 collective-permute-start.8
  65.3 0.0 collective-permute-done.4
  65.3 3.7 select_convert_fusion.2
  69.0 1.8 convolution_convert_fusion.3
  70.8 11.6 %collective-permute-start.5 = (bf16[1024,256]{0,1:T(8,128)(2,1)S(1)}, bf16[1024,256]{0,1:T(8,128)(2,1)S(1)}, u32[]{:S(2)}, u32[]{:S(2)}) collective-permute-start(bf16[1024,256]{0,1:T(8,128)(2,1)S(1)} %convolution_convert_fusion.3), channel_id=1, source_target_pairs={{0,126},{1,127},{2,0},{3,1},{4,2},{5,3},{6,4},{7,5},{8,6},{9,7},{1... | collective-permute-start | bytes 1572872 | tf_op jit(solution)/shard_map/ppermute | solution.py:11
  82.4 0.0 collective-permute-done
  82.4 0.0 collective-permute-done.1
  82.4 3.6 select_convert_fusion.3
  86.0 1.8 convolution_convert_fusion.4
  87.8 0.3 collective-permute-start.2
  88.1 1.8 fusion.16
  89.9 1.8 fusion.15
  91.7 0.0 copy-start.4
  91.7 1.9 fusion.14
  93.6 0.0 collective-permute-done.11
  93.7 0.0 collective-permute-done.8
  93.7 3.6 collective-permute-done.5
  97.3 0.0 collective-permute-done.2
  97.3 0.0 copy-done.4
  97.3 1.3 multiply_reduce_fusion
  98.6 0.2 multiply_convert_fusion
  98.8 0.0 copy-start.1
  98.8 0.8 copy-done.1
  99.7 1.7 convolution_bitcast_fusion
  101.4 0.0 copy-start.2
  101.4 0.0 copy-start.3
  101.4 2.6 copy.19
  104.0 0.0 reduce-scatter.4.cloned.1.call-update
  104.0 0.0 copy-done.2
  104.0 0.0 copy-done.3
  104.0 2.1 convolution_convert_fusion
  106.1 631.4 %reduce-scatter.4.cloned.1.call-done = f32[8,256]{1,0:T(8,128)} async-done(((f32[1024,256]{1,0:T(8,128)}), f32[8,256]{1,0:T(8,128)}) %reduce-scatter.4.cloned.1.call-update) | async-done | bytes 8208
  (6 shorter events, 0.0 us)
Async XLA Ops:
  7.2 1.6 copy-start
  7.2 9.9 %copy-start.5 = (s32[1024]{0:T(1024)S(1)}, s32[1024]{0:T(1024)}, u32[]{:S(2)}) copy-start(s32[1024]{0:T(1024)} %param.5) | copy-start | bytes 12292
  7.2 730.3 %reduce-scatter.4.cloned.1.call-start = ((), (), s32[]{:S(2)}) async-start(), calls=%async_computation.1 | async-start | bytes 1056768
  11.5 32.9 %collective-permute-start.10 = (bf16[1024,256]{0,1:T(8,128)(2,1)}, bf16[1024,256]{0,1:T(8,128)(2,1)}, u32[]{:S(2)}, u32[]{:S(2)}) collective-permute-start(bf16[1024,256]{0,1:T(8,128)(2,1)} %multiply_convert_fusion.1), channel_id=1, source_target_pairs={{0,4},{1,5},{2,6},{3,7},{4,8},{5,9},{6,10},{7,11},{8,12},{9,13},{1... | collective-permute-start | bytes 1572872 | tf_op jit(solution)/shard_map/ppermute | solution.py:11
  15.9 36.3 %collective-permute-start.7 = (bf16[1024,256]{0,1:T(8,128)(2,1)}, bf16[1024,256]{0,1:T(8,128)(2,1)}, u32[]{:S(2)}, u32[]{:S(2)}) collective-permute-start(bf16[1024,256]{0,1:T(8,128)(2,1)} %multiply_convert_fusion.1), channel_id=1, source_target_pairs={{0,3},{1,4},{2,5},{3,6},{4,7},{5,8},{6,9},{7,10},{8,11},{9,12},{10... | collective-permute-start | bytes 1572872 | tf_op jit(solution)/shard_map/ppermute | solution.py:11
  17.0 24.6 %collective-permute-start.9 = (s32[1024]{0:T(1024)S(1)}, s32[1024]{0:T(1024)S(1)}, u32[]{:S(2)}, u32[]{:S(2)}) collective-permute-start(s32[1024]{0:T(1024)S(1)} %copy-done.5), channel_id=1, source_target_pairs={{0,4},{1,5},{2,6},{3,7},{4,8},{5,9},{6,10},{7,11},{8,12},{9,13},{1... | collective-permute-start | bytes 12296 | tf_op jit(solution)/shard_map/ppermute | solution.py:11
  20.6 31.4 %collective-permute-start.6 = (s32[1024]{0:T(1024)S(1)}, s32[1024]{0:T(1024)S(1)}, u32[]{:S(2)}, u32[]{:S(2)}) collective-permute-start(s32[1024]{0:T(1024)S(1)} %copy-done.5), channel_id=1, source_target_pairs={{0,3},{1,4},{2,5},{3,6},{4,7},{5,8},{6,9},{7,10},{8,11},{9,12},{10... | collective-permute-start | bytes 12296 | tf_op jit(solution)/shard_map/ppermute | solution.py:11
  21.1 44.2 %collective-permute-start.4 = (bf16[1024,256]{0,1:T(8,128)(2,1)}, bf16[1024,256]{0,1:T(8,128)(2,1)}, u32[]{:S(2)}, u32[]{:S(2)}) collective-permute-start(bf16[1024,256]{0,1:T(8,128)(2,1)} %multiply_convert_fusion.1), channel_id=1, source_target_pairs={{0,2},{1,3},{2,4},{3,5},{4,6},{5,7},{6,8},{7,9},{8,10},{9,11},{10,... | collective-permute-start | bytes 1572872 | tf_op jit(solution)/shard_map/ppermute | solution.py:11
  41.6 19.5 %collective-permute-start.3 = (s32[1024]{0:T(1024)S(1)}, s32[1024]{0:T(1024)S(1)}, u32[]{:S(2)}, u32[]{:S(2)}) collective-permute-start(s32[1024]{0:T(1024)S(1)} %copy-done.5), channel_id=1, source_target_pairs={{0,2},{1,3},{2,4},{3,5},{4,6},{5,7},{6,8},{7,9},{8,10},{9,11},{10,... | collective-permute-start | bytes 12296 | tf_op jit(solution)/shard_map/ppermute | solution.py:11
  44.3 38.0 %collective-permute-start.1 = (bf16[1024,256]{0,1:T(8,128)(2,1)}, bf16[1024,256]{0,1:T(8,128)(2,1)S(1)}, u32[]{:S(2)}, u32[]{:S(2)}) collective-permute-start(bf16[1024,256]{0,1:T(8,128)(2,1)} %multiply_convert_fusion.1), channel_id=1, source_target_pairs={{0,1},{1,2},{2,3},{3,4},{4,5},{5,6},{6,7},{7,8},{8,9},{9,10},{10,1... | collective-permute-start | bytes 1572872 | tf_op jit(solution)/shard_map/ppermute | solution.py:11
  52.1 30.3 %collective-permute-start = (s32[1024]{0:T(1024)S(1)}, s32[1024]{0:T(1024)S(1)}, u32[]{:S(2)}, u32[]{:S(2)}) collective-permute-start(s32[1024]{0:T(1024)S(1)} %copy-done.5), channel_id=1, source_target_pairs={{0,1},{1,2},{2,3},{3,4},{4,5},{5,6},{6,7},{7,8},{8,9},{9,10},{10,1... | collective-permute-start | bytes 12296 | tf_op jit(solution)/shard_map/ppermute | solution.py:11
  52.2 41.5 %collective-permute-start.11 = (bf16[1024,256]{0,1:T(8,128)(2,1)S(1)}, bf16[1024,256]{0,1:T(8,128)(2,1)S(1)}, u32[]{:S(2)}, u32[]{:S(2)}) collective-permute-start(bf16[1024,256]{0,1:T(8,128)(2,1)S(1)} %convolution_convert_fusion.1), channel_id=1, source_target_pairs={{0,124},{1,125},{2,126},{3,127},{4,0},{5,1},{6,2},{7,3},{8,4},{9,5... | collective-permute-start | bytes 1572872 | tf_op jit(solution)/shard_map/ppermute | solution.py:11
  61.2 32.5 %collective-permute-start.8 = (bf16[1024,256]{0,1:T(8,128)(2,1)S(1)}, bf16[1024,256]{0,1:T(8,128)(2,1)S(1)}, u32[]{:S(2)}, u32[]{:S(2)}) collective-permute-start(bf16[1024,256]{0,1:T(8,128)(2,1)S(1)} %convolution_convert_fusion.2), channel_id=1, source_target_pairs={{0,125},{1,126},{2,127},{3,0},{4,1},{5,2},{6,3},{7,4},{8,5},{9,6},... | collective-permute-start | bytes 1572872 | tf_op jit(solution)/shard_map/ppermute | solution.py:11
  70.8 26.5 %collective-permute-start.5 = (bf16[1024,256]{0,1:T(8,128)(2,1)S(1)}, bf16[1024,256]{0,1:T(8,128)(2,1)S(1)}, u32[]{:S(2)}, u32[]{:S(2)}) collective-permute-start(bf16[1024,256]{0,1:T(8,128)(2,1)S(1)} %convolution_convert_fusion.3), channel_id=1, source_target_pairs={{0,126},{1,127},{2,0},{3,1},{4,2},{5,3},{6,4},{7,5},{8,6},{9,7},{1... | collective-permute-start | bytes 1572872 | tf_op jit(solution)/shard_map/ppermute | solution.py:11
  87.8 9.5 %collective-permute-start.2 = (bf16[1024,256]{0,1:T(8,128)(2,1)S(1)}, bf16[1024,256]{0,1:T(8,128)(2,1)S(1)}, u32[]{:S(2)}, u32[]{:S(2)}) collective-permute-start(bf16[1024,256]{0,1:T(8,128)(2,1)S(1)} %convolution_convert_fusion.4), channel_id=1, source_target_pairs={{0,127},{1,0},{2,1},{3,2},{4,3},{5,4},{6,5},{7,6},{8,7},{9,8},{10,... | collective-permute-start | bytes 1572872 | tf_op jit(solution)/shard_map/ppermute | solution.py:11
  91.7 5.6 copy-start.4
  98.8 0.8 copy-start.1
  101.4 2.7 copy-start.2
  101.4 2.7 copy-start.3
Sparse Core Ops, SparseCore 0:
  104.1 633.2 reduce-scatter.3
where the time goes:
time: 751 us; the launch traced here: 744 us
  waiting for transfers between devices  650 us (87%)
  matrix products  39.4 us (5%)
  starting transfers between devices  34.8 us (5%)
  between operations  14.3 us (2%)
    unnamed x2, waiting for transfers between devices  631 us
    ppermute x12, starting transfers between devices, passed_along(): return lax.ppermute(x, axis, [(i, (i + by) % size) for i in range(size)])  34.8 us
    ppermute x12, waiting for transfers between devices, passed_along(): return lax.ppermute(x, axis, [(i, (i + by) % size) for i in range(size)])  18.3 us
  transfers between devices with their start and end apart: 13, of which 3 were waited for; matrix products, arithmetic and copies ran while one was open for 5% of the time, Pallas kernels for 0%

commit v1 on v0

--- a/solution.py
+++ b/solution.py
@@ -47,14 +47,11 @@
     feature_grad = jnp.dot(raw_grad, head.T, preferred_element_type=jnp.float32).astype(
         jnp.bfloat16
     )
-    head_grad = lax.psum_scatter(
-        lax.dot_general(
-            features, raw_grad, (((0,), (0,)), ((), ())), preferred_element_type=jnp.float32
-        ),
-        "batch",
-        scatter_dimension=0,
-        tiled=True,
-    )
+    partial = lax.dot_general(
+        features, raw_grad, (((0,), (0,)), ((), ())), preferred_element_type=jnp.float32
+    ).astype(jnp.bfloat16)
+    parts = lax.all_to_all(partial.reshape(count, -1, partial.shape[1]), "batch", 0, 0)
+    head_grad = jnp.sum(parts.astype(jnp.float32), axis=0)
     return (feature_grad, head_grad)
 
 

time: 751 us -> 121 us (0.16)
  waiting for transfers between devices: 650 us -> 28.8 us
  between operations: 14.3 us -> 0.87 us
  starting transfers between devices: 34.8 us -> 45.9 us
    unnamed x2 -> x0, waiting for transfers between devices: 631 us -> none
    all_to_all x0 -> x1, starting transfers between devices: none -> 11.1 us  [per_device(): lax.all_to_all(partial.reshape(count, -1, partial.shape[1]), 'batch', 0, 0)]
    all_to_all x0 -> x1, waiting for transfers between devices: none -> 10.4 us  [per_device(): lax.all_to_all(partial.reshape(count, -1, partial.shape[1]), 'batch', 0, 0)]
  transfers between devices with their start and end apart: 13 -> 13, of which waited for: 3 -> 3; matrix products, arithmetic and copies ran while one was open for 5% -> 30% of each run, Pallas kernels for 0% -> 0%
where the time goes in v1:
time: 121 us; the launch traced here: 120 us
  starting transfers between devices  45.9 us (38%)
  matrix products  39.5 us (33%)
  waiting for transfers between devices  28.8 us (24%)
  local copies, waits for them, and re-layouts  3.41 us (3%)
  other arithmetic  1.89 us (2%)
    ppermute x12, starting transfers between devices, passed_along(): return lax.ppermute(x, axis, [(i, (i + by) % size) for i in range(size)])  34.8 us
    ppermute x12, waiting for transfers between devices, passed_along(): return lax.ppermute(x, axis, [(i, (i + by) % size) for i in range(size)])  18.3 us
    dot_general x4, matrix products, tile_coef(): scores = jnp.dot(z_a, z_b.T, preferred_element_type=jnp.float32)  14.7 us
    all_to_all x1, starting transfers between devices, per_device(): lax.all_to_all(partial.reshape(count, -1, partial.shape[1]), 'batch', 0, 0)  11.1 us
    all_to_all x1, waiting for transfers between devices, per_device(): lax.all_to_all(partial.reshape(count, -1, partial.shape[1]), 'batch', 0, 0)  10.4 us
    dot_general x4, matrix products, per_device(): jnp.dot(coef.T, embed, preferred_element_type=jnp.float32)  7.07 us
    dot_general x4, matrix products, per_device(): grad = grad + jnp.dot(coef, other_z, preferred_element_type=jnp.float32)  6.81 us
    dot_general x1, matrix products, per_device(): grad = jnp.dot(coef, embed, preferred_element_type=jnp.float32)  5.19 us
  transfers between devices with their start and end apart: 13, of which 3 were waited for; matrix products, arithmetic and copies ran while one was open for 30% of the time, Pallas kernels for 0%

profile of v1, /device:TPU:1, one launch (start us, length us, event | category | flops | bytes accessed | tf_op | source)
XLA Modules:
  0.0 120.3 jit_solution(15637582268924997170)
XLA Ops:
  0.6 0.0 copy-start
  0.6 1.6 %copy-done = bf16[1024,1024]{1,0:T(8,128)(2,1)S(1)} copy-done((bf16[1024,1024]{1,0:T(8,128)(2,1)S(1)}, bf16[1024,1024]{1,0:T(8,128)(2,1)}, u32[]{:S(2)}) %copy-start) | copy-done | bytes 2097176
  2.2 0.0 copy-start.4
  2.2 1.8 %multiply_reduce_fusion.1 = (f32[1024]{0:T(1024)S(1)}, f32[1024,256]{0,1:T(8,128)S(1)}) fusion(bf16[1024,1024]{1,0:T(8,128)(2,1)S(1)} %copy-done, bf16[1024,256]{1,0:T(8,128)(2,1)} %param.4), kind=kOutput, calls=%fused_computation.24 | convolution fusion | flops 537394176 | bytes 3674112 | tf_op jit(solution)/shard_map/dot_general | solution.py:28
  4.1 0.9 multiply_convert_fusion.1
  5.0 4.4 %collective-permute-start.10 = (bf16[1024,256]{0,1:T(8,128)(2,1)}, bf16[1024,256]{0,1:T(8,128)(2,1)}, u32[]{:S(2)}, u32[]{:S(2)}) collective-permute-start(bf16[1024,256]{0,1:T(8,128)(2,1)} %multiply_convert_fusion.1), channel_id=1, source_target_pairs={{0,4},{1,5},{2,6},{3,7},{4,8},{5,9},{6,10},{7,11},{8,12},{9,13},{1... | collective-permute-start | bytes 1572872 | tf_op jit(solution)/shard_map/ppermute | solution.py:11
  9.4 1.1 collective-permute-start.7
  10.5 0.0 copy-done.4
  10.5 3.6 %collective-permute-start.9 = (s32[1024]{0:T(1024)S(1)}, s32[1024]{0:T(1024)S(1)}, u32[]{:S(2)}, u32[]{:S(2)}) collective-permute-start(s32[1024]{0:T(1024)S(1)} %copy-done.4), channel_id=1, source_target_pairs={{0,4},{1,5},{2,6},{3,7},{4,8},{5,9},{6,10},{7,11},{8,12},{9,13},{1... | collective-permute-start | bytes 12296 | tf_op jit(solution)/shard_map/ppermute | solution.py:11
  14.1 0.5 collective-permute-start.6
  14.6 0.6 collective-permute-start.4
  15.2 5.2 %fusion.3 = f32[1024,256]{0,1:T(8,128)} fusion(bf16[1024,256]{0,1:T(8,128)(2,1)} %multiply_convert_fusion.1, s32[1024]{0:T(1024)S(1)} %copy-done.4, s32[1024]{0:T(1024)S(1)} %iota_add_fusion.4), kind=kOutput, calls=%fused_computation.10 | convolution fusion | flops 1090519040 | bytes 1581056 | tf_op jit(solution)/shard_map/dot_general | solution.py:35
  20.4 14.7 %collective-permute-done.9 = s32[1024]{0:T(1024)S(1)} collective-permute-done((s32[1024]{0:T(1024)S(1)}, s32[1024]{0:T(1024)S(1)}, u32[]{:S(2)}, u32[]{:S(2)}) %collective-permute-start.9) | collective-permute-done | bytes 4128 | tf_op jit(solution)/shard_map/ppermute | solution.py:11
  35.1 2.7 %collective-permute-start.3 = (s32[1024]{0:T(1024)S(1)}, s32[1024]{0:T(1024)S(1)}, u32[]{:S(2)}, u32[]{:S(2)}) collective-permute-start(s32[1024]{0:T(1024)S(1)} %copy-done.4), channel_id=1, source_target_pairs={{0,2},{1,3},{2,4},{3,5},{4,6},{5,7},{6,8},{7,9},{8,10},{9,11},{10,... | collective-permute-start | bytes 12296 | tf_op jit(solution)/shard_map/ppermute | solution.py:11
  37.8 0.0 collective-permute-done.10
  37.8 2.2 %collective-permute-start.1 = (bf16[1024,256]{0,1:T(8,128)(2,1)}, bf16[1024,256]{0,1:T(8,128)(2,1)S(1)}, u32[]{:S(2)}, u32[]{:S(2)}) collective-permute-start(bf16[1024,256]{0,1:T(8,128)(2,1)} %multiply_convert_fusion.1), channel_id=1, source_target_pairs={{0,1},{1,2},{2,3},{3,4},{4,5},{5,6},{6,7},{7,8},{8,9},{9,10},{10,1... | collective-permute-start | bytes 1572872 | tf_op jit(solution)/shard_map/ppermute | solution.py:11
  40.1 3.7 %select_convert_fusion = bf16[1024,1024]{1,0:T(8,128)(2,1)S(1)} fusion(bf16[1024,256]{0,1:T(8,128)(2,1)} %multiply_convert_fusion.1, bf16[1024,256]{0,1:T(8,128)(2,1)} %collective-permute-done.10, s32[1024]{0:T(1024)S(1)} %collective-permute-done.9, s32[1024]{0:T(1024)S(1)} %iota_add_fusion, s32[1024]{0:T(1024)S(1)} %copy-done.4, s32[1024]{0:T(1024)S(1)} %iota_add_fusion.4), kind=kOutput, calls=%fused_computation | convolution fusion | flops 553648128 | bytes 3162112 | tf_op jit(solution)/shard_map/dot_general | solution.py:15
  43.8 1.8 %convolution_convert_fusion.1 = bf16[1024,256]{0,1:T(8,128)(2,1)S(1)} fusion(bf16[1024,256]{0,1:T(8,128)(2,1)} %multiply_convert_fusion.1, bf16[1024,1024]{1,0:T(8,128)(2,1)S(1)} %select_convert_fusion), kind=kOutput, calls=%fused_computation.15 | convolution fusion | flops 537133056 | bytes 3145728 | tf_op jit(solution)/shard_map/dot_general | solution.py:41
  45.6 0.0 collective-permute-done.6
  45.6 0.1 collective-permute-start
  45.7 0.0 collective-permute-done.7
  45.7 3.5 %collective-permute-start.11 = (bf16[1024,256]{0,1:T(8,128)(2,1)S(1)}, bf16[1024,256]{0,1:T(8,128)(2,1)S(1)}, u32[]{:S(2)}, u32[]{:S(2)}) collective-permute-start(bf16[1024,256]{0,1:T(8,128)(2,1)S(1)} %convolution_convert_fusion.1), channel_id=1, source_target_pairs={{0,124},{1,125},{2,126},{3,127},{4,0},{5,1},{6,2},{7,3},{8,4},{9,5... | collective-permute-start | bytes 1572872 | tf_op jit(solution)/shard_map/ppermute | solution.py:11
  49.1 3.7 %select_convert_fusion.1 = bf16[1024,1024]{1,0:T(8,128)(2,1)S(1)} fusion(bf16[1024,256]{0,1:T(8,128)(2,1)} %multiply_convert_fusion.1, bf16[1024,256]{0,1:T(8,128)(2,1)} %collective-permute-done.7, s32[1024]{0:T(1024)S(1)} %collective-permute-done.6, s32[1024]{0:T(1024)S(1)} %iota_add_fusion.1, s32[1024]{0:T(1024)S(1)} %copy-done.4, s32[1024]{0:T(1024)S(1)} %iota_add_fusion.4), kind=kOutput, calls=%fused_computation.1 | convolution fusion | flops 553648128 | bytes 3162112 | tf_op jit(solution)/shard_map/dot_general | solution.py:15
  52.9 1.8 %convolution_convert_fusion.2 = bf16[1024,256]{0,1:T(8,128)(2,1)S(1)} fusion(bf16[1024,256]{0,1:T(8,128)(2,1)} %multiply_convert_fusion.1, bf16[1024,1024]{1,0:T(8,128)(2,1)S(1)} %select_convert_fusion.1), kind=kOutput, calls=%fused_computation.16 | convolution fusion | flops 537133056 | bytes 3145728 | tf_op jit(solution)/shard_map/dot_general | solution.py:41
  54.6 0.0 collective-permute-done.3
  54.7 4.1 %collective-permute-start.8 = (bf16[1024,256]{0,1:T(8,128)(2,1)S(1)}, bf16[1024,256]{0,1:T(8,128)(2,1)S(1)}, u32[]{:S(2)}, u32[]{:S(2)}) collective-permute-start(bf16[1024,256]{0,1:T(8,128)(2,1)S(1)} %convolution_convert_fusion.2), channel_id=1, source_target_pairs={{0,125},{1,126},{2,127},{3,0},{4,1},{5,2},{6,3},{7,4},{8,5},{9,6},... | collective-permute-start | bytes 1572872 | tf_op jit(solution)/shard_map/ppermute | solution.py:11
  58.8 0.0 collective-permute-done.4
  58.8 3.7 %select_convert_fusion.2 = bf16[1024,1024]{1,0:T(8,128)(2,1)S(1)} fusion(bf16[1024,256]{0,1:T(8,128)(2,1)} %multiply_convert_fusion.1, bf16[1024,256]{0,1:T(8,128)(2,1)} %collective-permute-done.4, s32[1024]{0:T(1024)S(1)} %collective-permute-done.3, s32[1024]{0:T(1024)S(1)} %iota_add_fusion.2, s32[1024]{0:T(1024)S(1)} %copy-done.4, s32[1024]{0:T(1024)S(1)} %iota_add_fusion.4), kind=kOutput, calls=%fused_computation.2 | convolution fusion | flops 553648128 | bytes 3162112 | tf_op jit(solution)/shard_map/dot_general | solution.py:15
  62.5 1.8 %convolution_convert_fusion.3 = bf16[1024,256]{0,1:T(8,128)(2,1)S(1)} fusion(bf16[1024,256]{0,1:T(8,128)(2,1)} %multiply_convert_fusion.1, bf16[1024,1024]{1,0:T(8,128)(2,1)S(1)} %select_convert_fusion.2), kind=kOutput, calls=%fused_computation.17 | convolution fusion | flops 537133056 | bytes 3145728 | tf_op jit(solution)/shard_map/dot_general | solution.py:41
  64.3 11.6 %collective-permute-start.5 = (bf16[1024,256]{0,1:T(8,128)(2,1)S(1)}, bf16[1024,256]{0,1:T(8,128)(2,1)S(1)}, u32[]{:S(2)}, u32[]{:S(2)}) collective-permute-start(bf16[1024,256]{0,1:T(8,128)(2,1)S(1)} %convolution_convert_fusion.3), channel_id=1, source_target_pairs={{0,126},{1,127},{2,0},{3,1},{4,2},{5,3},{6,4},{7,5},{8,6},{9,7},{1... | collective-permute-start | bytes 1572872 | tf_op jit(solution)/shard_map/ppermute | solution.py:11
  75.9 0.0 collective-permute-done
  75.9 0.0 collective-permute-done.1
  75.9 3.6 %select_convert_fusion.3 = bf16[1024,1024]{1,0:T(8,128)(2,1)S(1)} fusion(bf16[1024,256]{0,1:T(8,128)(2,1)} %multiply_convert_fusion.1, bf16[1024,256]{0,1:T(8,128)(2,1)S(1)} %collective-permute-done.1, s32[1024]{0:T(1024)S(1)} %collective-permute-done, s32[1024]{0:T(1024)S(1)} %iota_add_fusion.3, s32[1024]{0:T(1024)S(1)} %copy-done.4, ...), kind=kOutput, calls=%fused_computation.3 | convolution fusion | flops 553648128 | bytes 3162112 | tf_op jit(solution)/shard_map/dot_general | solution.py:15
  79.5 1.8 %convolution_convert_fusion.4 = bf16[1024,256]{0,1:T(8,128)(2,1)S(1)} fusion(bf16[1024,256]{0,1:T(8,128)(2,1)} %multiply_convert_fusion.1, bf16[1024,1024]{1,0:T(8,128)(2,1)S(1)} %select_convert_fusion.3), kind=kOutput, calls=%fused_computation.18 | convolution fusion | flops 537133056 | bytes 3145728 | tf_op jit(solution)/shard_map/dot_general | solution.py:41
  81.3 0.3 collective-permute-start.2
  81.6 1.8 %fusion.17 = f32[1024,256]{0,1:T(8,128)S(1)} fusion(bf16[1024,1024]{1,0:T(8,128)(2,1)S(1)} %select_convert_fusion, bf16[1024,256]{0,1:T(8,128)(2,1)} %collective-permute-done.10), kind=kOutput, calls=%fused_computation.40 | convolution fusion | flops 536870912 | bytes 3670016 | tf_op jit(solution)/shard_map/dot_general | solution.py:40
  83.4 1.8 %fusion.16 = f32[1024,256]{0,1:T(8,128)S(1)} fusion(bf16[1024,1024]{1,0:T(8,128)(2,1)S(1)} %select_convert_fusion.1, bf16[1024,256]{0,1:T(8,128)(2,1)} %collective-permute-done.7), kind=kOutput, calls=%fused_computation.39 | convolution fusion | flops 536870912 | bytes 3670016 | tf_op jit(solution)/shard_map/dot_general | solution.py:40
  85.2 0.0 copy-start.3
  85.2 1.9 %fusion.15 = f32[1024,256]{0,1:T(8,128)S(1)} fusion(bf16[1024,1024]{1,0:T(8,128)(2,1)S(1)} %select_convert_fusion.2, bf16[1024,256]{0,1:T(8,128)(2,1)} %collective-permute-done.4), kind=kOutput, calls=%fused_computation.38 | convolution fusion | flops 536870912 | bytes 3670016 | tf_op jit(solution)/shard_map/dot_general | solution.py:40
  87.1 0.0 collective-permute-done.11
  87.2 0.0 collective-permute-done.8
  87.2 3.6 %collective-permute-done.5 = bf16[1024,256]{0,1:T(8,128)(2,1)S(1)} collective-permute-done((bf16[1024,256]{0,1:T(8,128)(2,1)S(1)}, bf16[1024,256]{0,1:T(8,128)(2,1)S(1)}, u32[]{:S(2)}, u32[]{:S(2)}) %collective-permute-start.5) | collective-permute-done | bytes 524320 | tf_op jit(solution)/shard_map/ppermute | solution.py:11
  90.8 0.0 collective-permute-done.2
  90.8 0.0 copy-done.3
  90.8 1.3 %multiply_reduce_fusion = (f32[1024]{0:T(1024)S(1)}, f32[1024,256]{0,1:T(8,128)S(1)}) fusion(f32[1024,256]{0,1:T(8,128)S(1)} %get-tuple-element.3, f32[1024]{0:T(1024)S(1)} %add_rsqrt_fusion, bf16[1024,256]{0,1:T(8,128)(2,1)S(1)} %collective-permute-done.11, f32[1024,256]{0,1:T(8,128)S(1)} %fusion.17, bf16[1024,256]{0,1:T(8,128)(2,1)S(1)} %collective-permute-done.8, ...), kind=kOutput, calls=%fused_computation.23 | convolution fusion | flops 540802048 | bytes 11018240 | tf_op jit(solution)/shard_map/dot_general | solution.py:40
  92.1 0.2 multiply_convert_fusion
  92.3 0.0 copy-start.1
  92.3 0.8 copy-done.1
  93.1 0.7 fusion.8
  93.8 0.0 copy-start.2
  93.9 1.0 copy.13
  94.9 11.1 %all-to-all-start = ((bf16[128,8,256]{2,1,0:T(8,128)(2,1)}), bf16[128,8,256]{2,1,0:T(8,128)(2,1)S(1)}, u32[]{:S(2)}, u32[]{:S(2)}) async-start(bf16[128,8,256]{2,1,0:T(8,128)(2,1)} %bitcast.36), calls=%async_computation | async-start | bytes 1048576 | tf_op jit(solution)/shard_map/all_to_all | solution.py:53
  106.0 0.0 copy-done.2
  106.0 3.1 %convolution_convert_fusion = bf16[1024,1024]{1,0:T(8,128)(2,1)} fusion(bf16[1024,256]{0,1:T(8,128)(2,1)S(1)} %copy-done.2, bf16[1024,256]{1,0:T(8,128)(2,1)} %param.4), kind=kOutput, calls=%fused_computation.5 | convolution fusion | flops 537919488 | bytes 3145728 | tf_op jit(solution)/shard_map/dot_general | solution.py:47
  109.1 10.4 %all-to-all-done = bf16[128,8,256]{2,1,0:T(8,128)(2,1)S(1)} async-done(((bf16[128,8,256]{2,1,0:T(8,128)(2,1)}), bf16[128,8,256]{2,1,0:T(8,128)(2,1)S(1)}, u32[]{:S(2)}, u32[]{:S(2)}) %all-to-all-start) | async-done | bytes 524320 | tf_op jit(solution)/shard_map/all_to_all | solution.py:53
  119.5 0.7 convert_reduce_fusion
  (6 shorter events, 0.0 us)
Async XLA Ops:
  0.6 1.6 %copy-start = (bf16[1024,1024]{1,0:T(8,128)(2,1)S(1)}, bf16[1024,1024]{1,0:T(8,128)(2,1)}, u32[]{:S(2)}) copy-start(bf16[1024,1024]{1,0:T(8,128)(2,1)} %param.3) | copy-start | bytes 6291460
  2.2 8.3 %copy-start.4 = (s32[1024]{0:T(1024)S(1)}, s32[1024]{0:T(1024)}, u32[]{:S(2)}) copy-start(s32[1024]{0:T(1024)} %param.5) | copy-start | bytes 12292
  5.0 32.9 %collective-permute-start.10 = (bf16[1024,256]{0,1:T(8,128)(2,1)}, bf16[1024,256]{0,1:T(8,128)(2,1)}, u32[]{:S(2)}, u32[]{:S(2)}) collective-permute-start(bf16[1024,256]{0,1:T(8,128)(2,1)} %multiply_convert_fusion.1), channel_id=1, source_target_pairs={{0,4},{1,5},{2,6},{3,7},{4,8},{5,9},{6,10},{7,11},{8,12},{9,13},{1... | collective-permute-start | bytes 1572872 | tf_op jit(solution)/shard_map/ppermute | solution.py:11
  9.4 36.3 %collective-permute-start.7 = (bf16[1024,256]{0,1:T(8,128)(2,1)}, bf16[1024,256]{0,1:T(8,128)(2,1)}, u32[]{:S(2)}, u32[]{:S(2)}) collective-permute-start(bf16[1024,256]{0,1:T(8,128)(2,1)} %multiply_convert_fusion.1), channel_id=1, source_target_pairs={{0,3},{1,4},{2,5},{3,6},{4,7},{5,8},{6,9},{7,10},{8,11},{9,12},{10... | collective-permute-start | bytes 1572872 | tf_op jit(solution)/shard_map/ppermute | solution.py:11
  10.5 24.6 %collective-permute-start.9 = (s32[1024]{0:T(1024)S(1)}, s32[1024]{0:T(1024)S(1)}, u32[]{:S(2)}, u32[]{:S(2)}) collective-permute-start(s32[1024]{0:T(1024)S(1)} %copy-done.4), channel_id=1, source_target_pairs={{0,4},{1,5},{2,6},{3,7},{4,8},{5,9},{6,10},{7,11},{8,12},{9,13},{1... | collective-permute-start | bytes 12296 | tf_op jit(solution)/shard_map/ppermute | solution.py:11
  14.1 31.4 %collective-permute-start.6 = (s32[1024]{0:T(1024)S(1)}, s32[1024]{0:T(1024)S(1)}, u32[]{:S(2)}, u32[]{:S(2)}) collective-permute-start(s32[1024]{0:T(1024)S(1)} %copy-done.4), channel_id=1, source_target_pairs={{0,3},{1,4},{2,5},{3,6},{4,7},{5,8},{6,9},{7,10},{8,11},{9,12},{10... | collective-permute-start | bytes 12296 | tf_op jit(solution)/shard_map/ppermute | solution.py:11
  14.6 44.2 %collective-permute-start.4 = (bf16[1024,256]{0,1:T(8,128)(2,1)}, bf16[1024,256]{0,1:T(8,128)(2,1)}, u32[]{:S(2)}, u32[]{:S(2)}) collective-permute-start(bf16[1024,256]{0,1:T(8,128)(2,1)} %multiply_convert_fusion.1), channel_id=1, source_target_pairs={{0,2},{1,3},{2,4},{3,5},{4,6},{5,7},{6,8},{7,9},{8,10},{9,11},{10,... | collective-permute-start | bytes 1572872 | tf_op jit(solution)/shard_map/ppermute | solution.py:11
  35.1 19.5 %collective-permute-start.3 = (s32[1024]{0:T(1024)S(1)}, s32[1024]{0:T(1024)S(1)}, u32[]{:S(2)}, u32[]{:S(2)}) collective-permute-start(s32[1024]{0:T(1024)S(1)} %copy-done.4), channel_id=1, source_target_pairs={{0,2},{1,3},{2,4},{3,5},{4,6},{5,7},{6,8},{7,9},{8,10},{9,11},{10,... | collective-permute-start | bytes 12296 | tf_op jit(solution)/shard_map/ppermute | solution.py:11
  37.8 38.0 %collective-permute-start.1 = (bf16[1024,256]{0,1:T(8,128)(2,1)}, bf16[1024,256]{0,1:T(8,128)(2,1)S(1)}, u32[]{:S(2)}, u32[]{:S(2)}) collective-permute-start(bf16[1024,256]{0,1:T(8,128)(2,1)} %multiply_convert_fusion.1), channel_id=1, source_target_pairs={{0,1},{1,2},{2,3},{3,4},{4,5},{5,6},{6,7},{7,8},{8,9},{9,10},{10,1... | collective-permute-start | bytes 1572872 | tf_op jit(solution)/shard_map/ppermute | solution.py:11
  45.6 30.3 %collective-permute-start = (s32[1024]{0:T(1024)S(1)}, s32[1024]{0:T(1024)S(1)}, u32[]{:S(2)}, u32[]{:S(2)}) collective-permute-start(s32[1024]{0:T(1024)S(1)} %copy-done.4), channel_id=1, source_target_pairs={{0,1},{1,2},{2,3},{3,4},{4,5},{5,6},{6,7},{7,8},{8,9},{9,10},{10,1... | collective-permute-start | bytes 12296 | tf_op jit(solution)/shard_map/ppermute | solution.py:11
  45.7 41.5 %collective-permute-start.11 = (bf16[1024,256]{0,1:T(8,128)(2,1)S(1)}, bf16[1024,256]{0,1:T(8,128)(2,1)S(1)}, u32[]{:S(2)}, u32[]{:S(2)}) collective-permute-start(bf16[1024,256]{0,1:T(8,128)(2,1)S(1)} %convolution_convert_fusion.1), channel_id=1, source_target_pairs={{0,124},{1,125},{2,126},{3,127},{4,0},{5,1},{6,2},{7,3},{8,4},{9,5... | collective-permute-start | bytes 1572872 | tf_op jit(solution)/shard_map/ppermute | solution.py:11
  54.7 32.5 %collective-permute-start.8 = (bf16[1024,256]{0,1:T(8,128)(2,1)S(1)}, bf16[1024,256]{0,1:T(8,128)(2,1)S(1)}, u32[]{:S(2)}, u32[]{:S(2)}) collective-permute-start(bf16[1024,256]{0,1:T(8,128)(2,1)S(1)} %convolution_convert_fusion.2), channel_id=1, source_target_pairs={{0,125},{1,126},{2,127},{3,0},{4,1},{5,2},{6,3},{7,4},{8,5},{9,6},... | collective-permute-start | bytes 1572872 | tf_op jit(solution)/shard_map/ppermute | solution.py:11
  64.3 26.5 %collective-permute-start.5 = (bf16[1024,256]{0,1:T(8,128)(2,1)S(1)}, bf16[1024,256]{0,1:T(8,128)(2,1)S(1)}, u32[]{:S(2)}, u32[]{:S(2)}) collective-permute-start(bf16[1024,256]{0,1:T(8,128)(2,1)S(1)} %convolution_convert_fusion.3), channel_id=1, source_target_pairs={{0,126},{1,127},{2,0},{3,1},{4,2},{5,3},{6,4},{7,5},{8,6},{9,7},{1... | collective-permute-start | bytes 1572872 | tf_op jit(solution)/shard_map/ppermute | solution.py:11
  81.3 9.5 %collective-permute-start.2 = (bf16[1024,256]{0,1:T(8,128)(2,1)S(1)}, bf16[1024,256]{0,1:T(8,128)(2,1)S(1)}, u32[]{:S(2)}, u32[]{:S(2)}) collective-permute-start(bf16[1024,256]{0,1:T(8,128)(2,1)S(1)} %convolution_convert_fusion.4), channel_id=1, source_target_pairs={{0,127},{1,0},{2,1},{3,2},{4,3},{5,4},{6,5},{7,6},{8,7},{9,8},{10,... | collective-permute-start | bytes 1572872 | tf_op jit(solution)/shard_map/ppermute | solution.py:11
  85.2 5.6 %copy-start.3 = (f32[1024,256]{0,1:T(8,128)S(1)}, f32[1024,256]{0,1:T(8,128)}, u32[]{:S(2)}) copy-start(f32[1024,256]{0,1:T(8,128)} %fusion.3) | copy-start | bytes 3145732
  92.3 0.8 copy-start.1
  93.8 12.1 %copy-start.2 = (bf16[1024,256]{0,1:T(8,128)(2,1)S(1)}, bf16[1024,256]{0,1:T(8,128)(2,1)}, u32[]{:S(2)}) copy-start(bf16[1024,256]{0,1:T(8,128)(2,1)} %copy-done.1) | copy-start | bytes 1572868
  94.9 24.7 %all-to-all-start = ((bf16[128,8,256]{2,1,0:T(8,128)(2,1)}), bf16[128,8,256]{2,1,0:T(8,128)(2,1)S(1)}, u32[]{:S(2)}, u32[]{:S(2)}) async-start(bf16[128,8,256]{2,1,0:T(8,128)(2,1)} %bitcast.36), calls=%async_computation | async-start | bytes 1048576 | tf_op jit(solution)/shard_map/all_to_all | solution.py:53

commit v2 on v1

v2 whole, which is shorter than its diff:
```python
import functools
import math

import jax
import jax.numpy as jnp
from jax import lax
from jax.experimental import pallas as pl
from jax.experimental.pallas import tpu as pltpu
from jax.sharding import PartitionSpec as P

BF16, F32 = jnp.bfloat16, jnp.float32
ROWS, E, CODE = 1024, 256, 16
TILE = 256
VMEM = pl.BlockSpec(memory_space=pltpu.VMEM)
SMEM = pl.BlockSpec(memory_space=pltpu.SMEM)
BOTH_LAST = (((1,), (1,)), ((), ()))
BOTH_FIRST = (((0,), (0,)), ((), ()))
LIMIT = 24 * 2**20


def call(body, outs, specs, flops, aliases=None):
    return pl.pallas_call(
        body,
        out_shape=outs,
        in_specs=specs,
        out_specs=jax.tree.map(lambda _: VMEM, outs),
        input_output_aliases=aliases or {},
        compiler_params=pltpu.CompilerParams(vmem_limit_bytes=LIMIT),
        cost_estimate=pl.CostEstimate(flops=flops, bytes_accessed=4 * 2**20, transcendentals=0),
    )


def partners(msg_ref):
    code = msg_ref[ROWS : ROWS + CODE, :].astype(F32)
    return code[0:4, :] * 512.0 + code[4:8, :]


def across(rows):
    return jnp.concatenate([rows[k : k + 1, :] for k in range(4)], axis=1)


def embed_kernel(features_ref, head_ref, partner_ref, msg_ref, raw_ref):
    step = pl.program_id(0)
    raw = jnp.dot(features_ref[...], head_ref[...], preferred_element_type=F32)
    scale = lax.rsqrt(jnp.sum(raw * raw, axis=1, keepdims=True) + 1e-06)
    raw_ref[...] = raw
    at = pl.multiple_of(step * TILE, TILE)
    msg_ref[pl.ds(at, TILE), :] = (raw * scale).astype(BF16)

    @pl.when(step == 0)
    def _():
        ids = partner_ref[...]
        high = (ids + 256) >> 9
        low = ids - (high << 9)
        code = jnp.concatenate([high, low, jnp.zeros((8, E), jnp.int32)], axis=0)
        msg_ref[ROWS : ROWS + CODE, :] = code.astype(F32).astype(BF16)


def embed(features, head, partner):
    return pl.pallas_call(
        embed_kernel,
        grid=(ROWS // TILE,),
        out_shape=(
            jax.ShapeDtypeStruct((ROWS + CODE, E), BF16),
            jax.ShapeDtypeStruct((ROWS, E), F32),
        ),
        in_specs=[
            pl.BlockSpec((TILE, features.shape[1]), lambda i: (i, 0)),
            pl.BlockSpec(head.shape, lambda i: (0, 0)),
            pl.BlockSpec((4, E), lambda i: (0, 0)),
        ],
        out_specs=(
            pl.BlockSpec((ROWS + CODE, E), lambda i: (0, 0)),
            pl.BlockSpec((TILE, E), lambda i: (i, 0)),
        ),
        compiler_params=pltpu.CompilerParams(vmem_limit_bytes=LIMIT),
        cost_estimate=pl.CostEstimate(
            flops=2 * ROWS * 1024 * E, bytes_accessed=4 * 2**20, transcendentals=0
        ),
    )(features, head, partner.reshape(4, E))


def term(rows_ref, cols_ref, total, found, same=False):
    weight = 20.0 / total
    slope = 10.0 * math.log2(math.e)
    shift = slope - math.log2(weight)
    cols = cols_ref[0:ROWS, :]
    for at in range(0, ROWS, TILE):
        tile = slice(at, at + TILE)
        scores = lax.dot_general(rows_ref[tile, :], cols, BOTH_LAST, preferred_element_type=F32)
        coef = 1.0 / (jnp.exp2(shift - scores * slope) + 1.0 / weight)
        if same:
            i = lax.broadcasted_iota(jnp.int32, (TILE, ROWS), 0) + at
            j = lax.broadcasted_iota(jnp.int32, (TILE, ROWS), 1)
            coef = jnp.where(i != j, coef, 0.0)
        else:
            coef = jnp.where(found(at), coef - weight, coef)
        yield tile, jnp.dot(coef.astype(BF16), cols, preferred_element_type=F32)


def matcher(row_partner_ref, row_base, row_block, col_partner, col_block):
    j = lax.broadcasted_iota(jnp.int32, (1, ROWS), 1) + col_block * ROWS
    col_ids = j.astype(F32)

    def found(at):
        i = lax.broadcasted_iota(jnp.int32, (TILE, 1), 0) + (row_block * ROWS + at)
        row_ids = i.astype(F32)
        theirs = row_partner_ref[row_base + at : row_base + at + TILE, :]
        return (jnp.tile(theirs, (1, ROWS // 128)) == col_ids) | (col_partner == row_ids)

    return found


def diagonal_kernel(total, mine_ref, grad_ref):
    for tile, value in term(mine_ref, mine_ref, total, None, same=True):
        grad_ref[tile, :] = value


def chip_kernel(total, block_ref, mine_ref, other_ref, grad_ref, new_ref, spread_ref):
    for base, ref in ((0, mine_ref), (ROWS, other_ref)):
        ids = partners(ref)
        for k in range(8):
            piece = ids[k // 2 : k // 2 + 1, (k % 2) * 128 : (k % 2) * 128 + 128]
            spread_ref[base + k * 128 : base + k * 128 + 128, :] = jnp.broadcast_to(
                piece, (128, 128)
            ).T
    found = matcher(spread_ref, 0, block_ref[0], across(partners(other_ref)), block_ref[1])
    for tile, value in term(mine_ref, other_ref, total, found):
        new_ref[tile, :] = grad_ref[tile, :] + value


def mine_kernel(total, which, block_ref, cols_ref, mine_ref, spread_ref, grad_ref, new_ref):
    found = matcher(
        spread_ref, 0, block_ref[0], across(partners(cols_ref)), block_ref[which]
    )
    for tile, value in term(mine_ref, cols_ref, total, found):
        new_ref[tile, :] = grad_ref[tile, :] + value


def other_kernel(total, which, start, block_ref, cols_ref, other_ref, spread_ref, *rest):
    new_ref = rest[-1]
    found = matcher(
        spread_ref, ROWS, block_ref[1], across(partners(cols_ref)), block_ref[which]
    )
    for tile, value in term(other_ref, cols_ref, total, found):
        if not start:
            value = rest[0][tile, :] + value
        new_ref[tile, :] = value.astype(new_ref.dtype)


def final_kernel(features_ref, raw_ref, grad_ref, extra_ref, raw_grad_ref, partial_ref):
    raw = raw_ref[...]
    grad = grad_ref[...] + extra_ref[...].astype(F32)
    scale = lax.rsqrt(jnp.sum(raw * raw, axis=1, keepdims=True) + 1e-06)
    unit = raw * scale
    along = jnp.sum(unit * grad, axis=1, keepdims=True)
    raw_grad_ref[...] = ((grad - unit * along) * scale).astype(BF16)
    partial_ref[...] = lax.dot_general(
        features_ref[...], raw_grad_ref[...], BOTH_FIRST, preferred_element_type=F32
    ).astype(BF16)


def feature_kernel(raw_grad_ref, head_ref, out_ref):
    out_ref[...] = lax.dot_general(
        raw_grad_ref[...], head_ref[...], BOTH_LAST, preferred_element_type=F32
    ).astype(BF16)


def per_device(features, head, partner):
    count = lax.axis_size("batch")
    owner = lax.axis_index("batch")
    total = float(ROWS * count)
    pair = 4 * ROWS * ROWS * E
    shape = jax.ShapeDtypeStruct
    full = shape((ROWS, E), F32)

    def across_chip(x):
        return lax.ppermute(x, "batch", [(i, i ^ 1) for i in range(count)])

    def onward(x):
        hops = [(i, (i + (2 if i % 2 == 0 else -2)) % count) for i in range(count)]
        return lax.ppermute(x, "batch", hops)

    core = owner % 2
    chip = owner // 2
    back = jnp.where(core == 0, -1, 1)
    near = (chip + back) % (count // 2)
    far = (chip + 2 * back) % (count // 2)
    blocks = jnp.stack(
        [
            owner,
            owner ^ 1,
            2 * near + core,
            2 * near + 1 - core,
            2 * far + core,
            2 * far + 1 - core,
        ]
    ).astype(jnp.int32)

    mine, raw = embed(features, head, partner)
    near_same = onward(mine)
    other = across_chip(mine)
    near_cross = onward(other)
    far_same = onward(near_same)
    far_cross = onward(near_cross)

    grad = call(functools.partial(diagonal_kernel, total), full, [VMEM], pair)(mine)
    grad, spread = call(
        functools.partial(chip_kernel, total),
        (full, shape((2 * ROWS, 128), F32)),
        [SMEM, VMEM, VMEM, VMEM],
        pair,
    )(blocks, mine, other, grad)

    def on_mine(grad, which, cols):
        return call(
            functools.partial(mine_kernel, total, which), full, [SMEM] + [VMEM] * 4, pair
        )(blocks, cols, mine, spread, grad)

    def on_other(grad, which, cols, out=full):
        given = () if grad is None else (grad,)
        return call(
            functools.partial(other_kernel, total, which, grad is None),
            out,
            [SMEM] + [VMEM] * (3 + len(given)),
            pair,
        )(blocks, cols, other, spread, *given)

    theirs = on_other(None, 2, near_same)
    grad = on_mine(grad, 2, near_same)
    theirs = on_other(theirs, 3, near_cross)
    grad = on_mine(grad, 3, near_cross)
    grad = on_mine(grad, 4, far_same)
    theirs = on_other(theirs, 5, far_cross, shape((ROWS, E), BF16))
    extra = across_chip(theirs)
    grad = on_mine(grad, 5, far_cross)

    raw_grad, partial = call(
        final_kernel,
        (shape((ROWS, E), BF16), shape((features.shape[1], E), BF16)),
        [VMEM] * 4,
        pair // 2,
    )(features, raw, grad, extra)
    parts = lax.all_to_all(partial.reshape(count, -1, E), "batch", 0, 0)
    feature_grad = call(
        feature_kernel, shape((ROWS, features.shape[1]), BF16), [VMEM] * 2, pair // 2
    )(raw_grad, head)
    head_grad = jnp.sum(parts.astype(F32), axis=0)
    return (feature_grad, head_grad)


def solution(mesh):
    in_specs = (P("batch", None), P(), P("batch"))
    out_specs = (P("batch", None), P("batch", None))
    return jax.shard_map(
        per_device, mesh=mesh, in_specs=in_specs, out_specs=out_specs, check_vma=False
    )
```

time: 121 us -> 76.1 us (0.63)
  matrix products: 39.5 us -> 0 us
  Pallas kernels: 0 us -> 25.8 us
  starting transfers between devices: 45.9 us -> 25.8 us
  waiting for transfers between devices: 28.8 us -> 18.5 us
    dot_general x16 -> x0, matrix products: 39.5 us -> none  [the longest x4 14.7 us: tile_coef(): scores = jnp.dot(z_a, z_b.T, preferred_element_type=jnp.float32)]
    pallas_call x0 -> x12, Pallas kernels: none -> 25.8 us  [the longest x4 9.38 us: on_mine(): call(functools.partial(mine_kernel, total, which), full, [SMEM] + [VMEM]...]
    ppermute x12 -> x6, starting transfers between devices: 34.8 us -> 21.9 us  [the longest x4 20.1 us: onward(): return lax.ppermute(x, 'batch', hops)]
    ppermute x12 -> x6, waiting for transfers between devices: 18.3 us -> 6.85 us  [the longest x4 5.3 us: onward(): return lax.ppermute(x, 'batch', hops)]
    all_to_all x1, starting transfers between devices: 11.1 us -> 3.9 us  [per_device(): parts = lax.all_to_all(partial.reshape(count, -1, E), 'batch', 0, 0)]
    unnamed x10 -> x12, local copies, waits for them, and re-layouts: 2.39 us -> 3.44 us
  transfers between devices with their start and end apart: 13 -> 7, of which waited for: 3 -> 3; matrix products, arithmetic and copies ran while one was open for 30% -> 0% of each run, Pallas kernels for 0% -> 29%
where the time goes in v2:
time: 76.1 us; the launch traced here: 75.9 us
  Pallas kernels  25.8 us (34%)
  starting transfers between devices  25.8 us (34%)
  waiting for transfers between devices  18.5 us (24%)
  local copies, waits for them, and re-layouts  4.22 us (6%)
  between operations  0.79 us (1%)
    ppermute x4, starting transfers between devices, onward(): return lax.ppermute(x, 'batch', hops)  20.1 us
    all_to_all x1, waiting for transfers between devices, per_device(): parts = lax.all_to_all(partial.reshape(count, -1, E), 'batch', 0, 0)  11.6 us
    pallas_call x4, Pallas kernels, on_mine(): call(functools.partial(mine_kernel, total, which), full, [SMEM] + [VMEM]...  9.38 us
    pallas_call x3, Pallas kernels, on_other(): call(functools.partial(other_kernel, total, which, grad is None), out, [S...  7.04 us
    ppermute x4, waiting for transfers between devices, onward(): return lax.ppermute(x, 'batch', hops)  5.3 us
    all_to_all x1, starting transfers between devices, per_device(): parts = lax.all_to_all(partial.reshape(count, -1, E), 'batch', 0, 0)  3.9 us
    unnamed x12, local copies, waits for them, and re-layouts  3.44 us
    pallas_call x1, Pallas kernels, per_device(): call(functools.partial(chip_kernel, total), (full, shape((2 * ROWS, 128),...  2.34 us
  transfers between devices with their start and end apart: 7, of which 3 were waited for; matrix products, arithmetic and copies ran while one was open for 0% of the time, Pallas kernels for 29%

profile of v2, /device:TPU:1, one launch (start us, length us, event | category | flops | bytes accessed | tf_op | source)
XLA Modules:
  0.0 75.9 jit_solution(9168892449373332828)
XLA Ops:
  0.6 0.7 reshape.10.partner_ref
  1.3 0.0 copy-start
  1.3 1.6 %copy-done = bf16[1024,1024]{1,0:T(8,128)(2,1)S(1)} copy-done((bf16[1024,1024]{1,0:T(8,128)(2,1)S(1)}, bf16[1024,1024]{1,0:T(8,128)(2,1)}, u32[]{:S(2)}) %copy-start) | copy-done | bytes 2097176
  2.9 0.0 copy-start.2
  2.9 1.0 %copy-done.2 = bf16[1024,256]{1,0:T(8,128)(2,1)S(1)} copy-done((bf16[1024,256]{1,0:T(8,128)(2,1)S(1)}, bf16[1024,256]{1,0:T(8,128)(2,1)}, u32[]{:S(2)}) %copy-start.2) | copy-done | bytes 524312
  4.0 1.6 %shard_map.50 = (bf16[1040,256]{1,0:T(8,128)(2,1)S(1)}, f32[1024,256]{1,0:T(8,128)S(1)}) custom-call(bf16[1024,1024]{1,0:T(8,128)(2,1)S(1)} %copy-done, bf16[1024,256]{1,0:T(8,128)(2,1)S(1)} %copy-done.2, s32[4,256]{1,0:T(4,128)S(1)} %reshape.10.partner_ref), custom_call_target="tpu_custom_call" | custom-call | flops 536870912 | bytes 4194304 | tf_op jit(solution)/shard_map/pallas_call | solution.py:60
  5.5 1.5 %collective-permute-start = (bf16[1040,256]{1,0:T(8,128)(2,1)S(1)}, bf16[1040,256]{1,0:T(8,128)(2,1)S(1)}, u32[]{:S(2)}, u32[]{:S(2)}) collective-permute-start(bf16[1040,256]{1,0:T(8,128)(2,1)S(1)} %get-tuple-element.9.mine_ref), channel_id=1, source_target_pairs={{0,1},{1,0},{2,3},{3,2},{4,5},{5,4},{6,7},{7,6},{8,9},{9,8},{10,11... | collective-permute-start | bytes 1597448 | tf_op jit(solution)/shard_map/ppermute | solution.py:178
  7.0 1.5 %collective-permute-done.other_ref = bf16[1040,256]{1,0:T(8,128)(2,1)S(1)} collective-permute-done((bf16[1040,256]{1,0:T(8,128)(2,1)S(1)}, bf16[1040,256]{1,0:T(8,128)(2,1)S(1)}, u32[]{:S(2)}, u32[]{:S(2)}) %collective-permute-start) | collective-permute-done | bytes 532512 | tf_op jit(solution)/shard_map/ppermute | solution.py:178
  8.6 8.5 %collective-permute-start.1 = (bf16[1040,256]{1,0:T(8,128)(2,1)S(1)}, bf16[1040,256]{1,0:T(8,128)(2,1)S(1)}, u32[]{:S(2)}, u32[]{:S(2)}) collective-permute-start(bf16[1040,256]{1,0:T(8,128)(2,1)S(1)} %collective-permute-done.other_ref), channel_id=1, source_target_pairs={{0,2},{1,127},{2,4},{3,1},{4,6},{5,3},{6,8},{7,5},{8,10},{9,7},{10... | collective-permute-start | bytes 1597448 | tf_op jit(solution)/shard_map/ppermute | solution.py:182
  17.1 0.0 copy-start.4
  17.1 0.8 %copy-done.4 = bf16[1040,256]{1,0:T(8,128)(2,1)} copy-done((bf16[1040,256]{1,0:T(8,128)(2,1)}, bf16[1040,256]{1,0:T(8,128)(2,1)S(1)}, u32[]{:S(2)}) %copy-start.4) | copy-done | bytes 532504
  17.9 0.1 collective-permute-start.3
  18.0 5.3 %collective-permute-done.1.cols_ref = bf16[1040,256]{1,0:T(8,128)(2,1)S(1)} collective-permute-done((bf16[1040,256]{1,0:T(8,128)(2,1)S(1)}, bf16[1040,256]{1,0:T(8,128)(2,1)S(1)}, u32[]{:S(2)}, u32[]{:S(2)}) %collective-permute-start.1) | collective-permute-done | bytes 532512 | tf_op jit(solution)/shard_map/ppermute | solution.py:182
  23.3 7.3 %collective-permute-start.2 = (bf16[1040,256]{1,0:T(8,128)(2,1)S(1)}, bf16[1040,256]{1,0:T(8,128)(2,1)S(1)}, u32[]{:S(2)}, u32[]{:S(2)}) collective-permute-start(bf16[1040,256]{1,0:T(8,128)(2,1)S(1)} %collective-permute-done.1.cols_ref), channel_id=1, source_target_pairs={{0,2},{1,127},{2,4},{3,1},{4,6},{5,3},{6,8},{7,5},{8,10},{9,7},{10... | collective-permute-start | bytes 1597448 | tf_op jit(solution)/shard_map/ppermute | solution.py:182
  30.6 0.1 stack.27.block_ref
  30.7 0.0 copy-start.5
  30.7 1.4 %shard_map.51.grad_ref = f32[1024,256]{1,0:T(8,128)S(1)} custom-call(bf16[1040,256]{1,0:T(8,128)(2,1)S(1)} %get-tuple-element.9.mine_ref), custom_call_target="tpu_custom_call" | custom-call | flops 1073741824 | bytes 4194304 | tf_op jit(solution)/shard_map/pallas_call | solution.py:207
  32.1 0.0 collective-permute-done.3.cols_ref
  32.2 4.2 %collective-permute-start.4 = (bf16[1040,256]{1,0:T(8,128)(2,1)S(1)}, bf16[1040,256]{1,0:T(8,128)(2,1)S(1)}, u32[]{:S(2)}, u32[]{:S(2)}) collective-permute-start(bf16[1040,256]{1,0:T(8,128)(2,1)S(1)} %collective-permute-done.3.cols_ref), channel_id=1, source_target_pairs={{0,2},{1,127},{2,4},{3,1},{4,6},{5,3},{6,8},{7,5},{8,10},{9,7},{10... | collective-permute-start | bytes 1597448 | tf_op jit(solution)/shard_map/ppermute | solution.py:182
  36.3 0.0 copy-done.5
  36.3 2.3 %shard_map.52 = (f32[1024,256]{1,0:T(8,128)S(1)}, f32[2048,128]{1,0:T(8,128)S(1)}) custom-call(s32[6]{0:T(128)S(1)} %stack.27.block_ref, bf16[1040,256]{1,0:T(8,128)(2,1)S(1)} %get-tuple-element.9.mine_ref, bf16[1040,256]{1,0:T(8,128)(2,1)S(1)} %copy-done.5, f32[1024,256]{1,0:T(8,128)S(1)} %shard_map.51.grad_ref), custom_call_target="tpu_custom_call" | custom-call | flops 1073741824 | bytes 4194304 | tf_op jit(solution)/shard_map/pallas_call | solution.py:208
  38.7 2.3 %shard_map.57.rest_0_ = f32[1024,256]{1,0:T(8,128)S(1)} custom-call(s32[6]{0:T(128)S(1)} %stack.27.block_ref, bf16[1040,256]{1,0:T(8,128)(2,1)S(1)} %collective-permute-done.3.cols_ref, bf16[1040,256]{1,0:T(8,128)(2,1)S(1)} %copy-done.5, f32[2048,128]{1,0:T(8,128)S(1)} %get-tuple-element.10.spread_ref), custom_call_target="tpu_custom_call" | custom-call | flops 1073741824 | bytes 4194304 | tf_op jit(solution)/shard_map/pallas_call | solution.py:222
  41.0 2.4 %shard_map.58.rest_0_ = f32[1024,256]{1,0:T(8,128)S(1)} custom-call(s32[6]{0:T(128)S(1)} %stack.27.block_ref, bf16[1040,256]{1,0:T(8,128)(2,1)S(1)} %collective-permute-done.1.cols_ref, bf16[1040,256]{1,0:T(8,128)(2,1)S(1)} %copy-done.5, f32[2048,128]{1,0:T(8,128)S(1)} %get-tuple-element.10.spread_ref, f32[1024,256]{1,0:T(8,128)S(1)} %shard_map.57.rest_0_), custom_call_target="tpu_custom_call" | custom-call | flops 1073741824 | bytes 4194304 | tf_op jit(solution)/shard_map/pallas_call | solution.py:222
  43.4 0.0 collective-permute-done.2.cols_ref
  43.4 2.3 %shard_map.59 = bf16[1024,256]{1,0:T(8,128)(2,1)S(1)} custom-call(s32[6]{0:T(128)S(1)} %stack.27.block_ref, bf16[1040,256]{1,0:T(8,128)(2,1)S(1)} %collective-permute-done.2.cols_ref, bf16[1040,256]{1,0:T(8,128)(2,1)S(1)} %copy-done.5, f32[2048,128]{1,0:T(8,128)S(1)} %get-tuple-element.10.spread_ref, f32[1024,256]{1,0:T(8,128)S(1)} %shard_map.58.rest_0_), custom_call_target="tpu_custom_call" | custom-call | flops 1073741824 | bytes 4194304 | tf_op jit(solution)/shard_map/pallas_call | solution.py:222
  45.8 0.3 collective-permute-start.5
  46.0 2.4 %shard_map.53.grad_ref = f32[1024,256]{1,0:T(8,128)S(1)} custom-call(s32[6]{0:T(128)S(1)} %stack.27.block_ref, bf16[1040,256]{1,0:T(8,128)(2,1)S(1)} %collective-permute-done.3.cols_ref, bf16[1040,256]{1,0:T(8,128)(2,1)S(1)} %get-tuple-element.9.mine_ref, f32[2048,128]{1,0:T(8,128)S(1)} %get-tuple-element.10.spread_ref, ...), custom_call_target="tpu_custom_call" | custom-call | flops 1073741824 | bytes 4194304 | tf_op jit(solution)/shard_map/pallas_call | solution.py:216
  48.4 2.4 %shard_map.54.grad_ref = f32[1024,256]{1,0:T(8,128)S(1)} custom-call(s32[6]{0:T(128)S(1)} %stack.27.block_ref, bf16[1040,256]{1,0:T(8,128)(2,1)S(1)} %collective-permute-done.1.cols_ref, bf16[1040,256]{1,0:T(8,128)(2,1)S(1)} %get-tuple-element.9.mine_ref, f32[2048,128]{1,0:T(8,128)S(1)} %get-tuple-element.10.spread_ref, f32[1024,256]{1,0:T(8,128)S(1)} %shard_map.53.grad_ref), custom_call_target="tpu_custom_call" | custom-call | flops 1073741824 | bytes 4194304 | tf_op jit(solution)/shard_map/pallas_call | solution.py:216
  50.8 0.0 collective-permute-done.4.cols_ref
  50.8 2.3 %shard_map.55.grad_ref = f32[1024,256]{1,0:T(8,128)S(1)} custom-call(s32[6]{0:T(128)S(1)} %stack.27.block_ref, bf16[1040,256]{1,0:T(8,128)(2,1)S(1)} %collective-permute-done.4.cols_ref, bf16[1040,256]{1,0:T(8,128)(2,1)S(1)} %get-tuple-element.9.mine_ref, f32[2048,128]{1,0:T(8,128)S(1)} %get-tuple-element.10.spread_ref, f32[1024,256]{1,0:T(8,128)S(1)} %shard_map.54.grad_ref), custom_call_target="tpu_custom_call" | custom-call | flops 1073741824 | bytes 4194304 | tf_op jit(solution)/shard_map/pallas_call | solution.py:216
  53.1 0.0 copy-start.1
  53.1 2.3 %shard_map.56.grad_ref = f32[1024,256]{1,0:T(8,128)S(1)} custom-call(s32[6]{0:T(128)S(1)} %stack.27.block_ref, bf16[1040,256]{1,0:T(8,128)(2,1)S(1)} %collective-permute-done.2.cols_ref, bf16[1040,256]{1,0:T(8,128)(2,1)S(1)} %get-tuple-element.9.mine_ref, f32[2048,128]{1,0:T(8,128)S(1)} %get-tuple-element.10.spread_ref, f32[1024,256]{1,0:T(8,128)S(1)} %shard_map.55.grad_ref), custom_call_target="tpu_custom_call" | custom-call | flops 1073741824 | bytes 4194304 | tf_op jit(solution)/shard_map/pallas_call | solution.py:216
  55.5 0.0 collective-permute-done.5.extra_ref
  55.5 0.0 copy-done.1
  55.5 0.0 copy-start.3
  55.5 2.0 %shard_map.60 = (bf16[1024,256]{1,0:T(8,128)(2,1)S(1)}, bf16[1024,256]{1,0:T(8,128)(2,1)}) custom-call(bf16[1024,1024]{1,0:T(8,128)(2,1)S(1)} %copy-done.1, f32[1024,256]{1,0:T(8,128)S(1)} %get-tuple-element.8.raw_ref, f32[1024,256]{1,0:T(8,128)S(1)} %shard_map.56.grad_ref, bf16[1024,256]{1,0:T(8,128)(2,1)S(1)} %collective-permute-done.5.extra_ref), custom_call_target="tpu_custom_call" | custom-call | flops 536870912 | bytes 4194304 | tf_op jit(solution)/shard_map/pallas_call | solution.py:238
  57.5 3.9 %all-to-all-start = ((bf16[128,8,256]{2,1,0:T(8,128)(2,1)}), bf16[128,8,256]{2,1,0:T(8,128)(2,1)S(1)}, u32[]{:S(2)}, u32[]{:S(2)}) async-start(bf16[128,8,256]{2,1,0:T(8,128)(2,1)} %bitcast.6), calls=%async_computation | async-start | bytes 1048576 | tf_op jit(solution)/shard_map/all_to_all | solution.py:244
  61.4 0.0 copy-done.3
  61.4 2.1 %shard_map.61 = bf16[1024,1024]{1,0:T(8,128)(2,1)} custom-call(bf16[1024,256]{1,0:T(8,128)(2,1)S(1)} %get-tuple-element.12.raw_grad_ref, bf16[1024,256]{1,0:T(8,128)(2,1)S(1)} %copy-done.3), custom_call_target="tpu_custom_call" | custom-call | flops 536870912 | bytes 4194304 | tf_op jit(solution)/shard_map/pallas_call | solution.py:245
  63.5 11.6 %all-to-all-done = bf16[128,8,256]{2,1,0:T(8,128)(2,1)S(1)} async-done(((bf16[128,8,256]{2,1,0:T(8,128)(2,1)}), bf16[128,8,256]{2,1,0:T(8,128)(2,1)S(1)}, u32[]{:S(2)}, u32[]{:S(2)}) %all-to-all-start) | async-done | bytes 524320 | tf_op jit(solution)/shard_map/all_to_all | solution.py:244
  75.1 0.7 convert_reduce_fusion
Async XLA Ops:
  1.3 1.6 %copy-start = (bf16[1024,1024]{1,0:T(8,128)(2,1)S(1)}, bf16[1024,1024]{1,0:T(8,128)(2,1)}, u32[]{:S(2)}) copy-start(bf16[1024,1024]{1,0:T(8,128)(2,1)} %features_ref.3) | copy-start | bytes 6291460
  2.9 1.0 %copy-start.2 = (bf16[1024,256]{1,0:T(8,128)(2,1)S(1)}, bf16[1024,256]{1,0:T(8,128)(2,1)}, u32[]{:S(2)}) copy-start(bf16[1024,256]{1,0:T(8,128)(2,1)} %head_ref.3) | copy-start | bytes 1572868
  5.5 3.0 %collective-permute-start = (bf16[1040,256]{1,0:T(8,128)(2,1)S(1)}, bf16[1040,256]{1,0:T(8,128)(2,1)S(1)}, u32[]{:S(2)}, u32[]{:S(2)}) collective-permute-start(bf16[1040,256]{1,0:T(8,128)(2,1)S(1)} %get-tuple-element.9.mine_ref), channel_id=1, source_target_pairs={{0,1},{1,0},{2,3},{3,2},{4,5},{5,4},{6,7},{7,6},{8,9},{9,8},{10,11... | collective-permute-start | bytes 1597448 | tf_op jit(solution)/shard_map/ppermute | solution.py:178
  8.6 14.7 %collective-permute-start.1 = (bf16[1040,256]{1,0:T(8,128)(2,1)S(1)}, bf16[1040,256]{1,0:T(8,128)(2,1)S(1)}, u32[]{:S(2)}, u32[]{:S(2)}) collective-permute-start(bf16[1040,256]{1,0:T(8,128)(2,1)S(1)} %collective-permute-done.other_ref), channel_id=1, source_target_pairs={{0,2},{1,127},{2,4},{3,1},{4,6},{5,3},{6,8},{7,5},{8,10},{9,7},{10... | collective-permute-start | bytes 1597448 | tf_op jit(solution)/shard_map/ppermute | solution.py:182
  17.1 0.8 %copy-start.4 = (bf16[1040,256]{1,0:T(8,128)(2,1)}, bf16[1040,256]{1,0:T(8,128)(2,1)S(1)}, u32[]{:S(2)}) copy-start(bf16[1040,256]{1,0:T(8,128)(2,1)S(1)} %collective-permute-done.other_ref) | copy-start | bytes 1597444
  17.9 14.3 %collective-permute-start.3 = (bf16[1040,256]{1,0:T(8,128)(2,1)S(1)}, bf16[1040,256]{1,0:T(8,128)(2,1)S(1)}, u32[]{:S(2)}, u32[]{:S(2)}) collective-permute-start(bf16[1040,256]{1,0:T(8,128)(2,1)S(1)} %get-tuple-element.9.mine_ref), channel_id=1, source_target_pairs={{0,2},{1,127},{2,4},{3,1},{4,6},{5,3},{6,8},{7,5},{8,10},{9,7},{10... | collective-permute-start | bytes 1597448 | tf_op jit(solution)/shard_map/ppermute | solution.py:182
  23.3 20.1 %collective-permute-start.2 = (bf16[1040,256]{1,0:T(8,128)(2,1)S(1)}, bf16[1040,256]{1,0:T(8,128)(2,1)S(1)}, u32[]{:S(2)}, u32[]{:S(2)}) collective-permute-start(bf16[1040,256]{1,0:T(8,128)(2,1)S(1)} %collective-permute-done.1.cols_ref), channel_id=1, source_target_pairs={{0,2},{1,127},{2,4},{3,1},{4,6},{5,3},{6,8},{7,5},{8,10},{9,7},{10... | collective-permute-start | bytes 1597448 | tf_op jit(solution)/shard_map/ppermute | solution.py:182
  30.7 5.6 %copy-start.5 = (bf16[1040,256]{1,0:T(8,128)(2,1)S(1)}, bf16[1040,256]{1,0:T(8,128)(2,1)}, u32[]{:S(2)}) copy-start(bf16[1040,256]{1,0:T(8,128)(2,1)} %copy-done.4) | copy-start | bytes 1597444
  32.2 18.6 %collective-permute-start.4 = (bf16[1040,256]{1,0:T(8,128)(2,1)S(1)}, bf16[1040,256]{1,0:T(8,128)(2,1)S(1)}, u32[]{:S(2)}, u32[]{:S(2)}) collective-permute-start(bf16[1040,256]{1,0:T(8,128)(2,1)S(1)} %collective-permute-done.3.cols_ref), channel_id=1, source_target_pairs={{0,2},{1,127},{2,4},{3,1},{4,6},{5,3},{6,8},{7,5},{8,10},{9,7},{10... | collective-permute-start | bytes 1597448 | tf_op jit(solution)/shard_map/ppermute | solution.py:182
  45.8 9.7 %collective-permute-start.5 = (bf16[1024,256]{1,0:T(8,128)(2,1)S(1)}, bf16[1024,256]{1,0:T(8,128)(2,1)S(1)}, u32[]{:S(2)}, u32[]{:S(2)}) collective-permute-start(bf16[1024,256]{1,0:T(8,128)(2,1)S(1)} %shard_map.59), channel_id=1, source_target_pairs={{0,1},{1,0},{2,3},{3,2},{4,5},{5,4},{6,7},{7,6},{8,9},{9,8},{10,11... | collective-permute-start | bytes 1572872 | tf_op jit(solution)/shard_map/ppermute | solution.py:178
  53.1 2.3 %copy-start.1 = (bf16[1024,1024]{1,0:T(8,128)(2,1)S(1)}, bf16[1024,1024]{1,0:T(8,128)(2,1)}, u32[]{:S(2)}) copy-start(bf16[1024,1024]{1,0:T(8,128)(2,1)} %features_ref.3) | copy-start | bytes 6291460
  55.5 5.9 %copy-start.3 = (bf16[1024,256]{1,0:T(8,128)(2,1)S(1)}, bf16[1024,256]{1,0:T(8,128)(2,1)}, u32[]{:S(2)}) copy-start(bf16[1024,256]{1,0:T(8,128)(2,1)} %head_ref.3) | copy-start | bytes 1572868
  57.5 17.6 %all-to-all-start = ((bf16[128,8,256]{2,1,0:T(8,128)(2,1)}), bf16[128,8,256]{2,1,0:T(8,128)(2,1)S(1)}, u32[]{:S(2)}, u32[]{:S(2)}) async-start(bf16[128,8,256]{2,1,0:T(8,128)(2,1)} %bitcast.6), calls=%async_computation | async-start | bytes 1048576 | tf_op jit(solution)/shard_map/all_to_all | solution.py:244

commit v3 on v2

--- a/solution.py
+++ b/solution.py
@@ -12,10 +12,13 @@
 ROWS, E, CODE = 1024, 256, 16
 TILE = 256
 VMEM = pl.BlockSpec(memory_space=pltpu.VMEM)
+ANY = pl.BlockSpec(memory_space=pl.ANY)
 SMEM = pl.BlockSpec(memory_space=pltpu.SMEM)
 BOTH_LAST = (((1,), (1,)), ((), ()))
 BOTH_FIRST = (((0,), (0,)), ((), ()))
 LIMIT = 24 * 2**20
+EMBED_LIMIT = 60 * 2**20
+COST = 3
 
 
 def call(body, outs, specs, flops, aliases=None):
@@ -23,61 +26,67 @@
         body,
         out_shape=outs,
         in_specs=specs,
-        out_specs=jax.tree.map(lambda _: VMEM, outs),
+        out_specs=jax.tree.map(lambda _: VMEM, outs) if not aliases else (VMEM, ANY),
         input_output_aliases=aliases or {},
         compiler_params=pltpu.CompilerParams(vmem_limit_bytes=LIMIT),
-        cost_estimate=pl.CostEstimate(flops=flops, bytes_accessed=4 * 2**20, transcendentals=0),
+        cost_estimate=pl.CostEstimate(flops=int(COST * flops), bytes_accessed=4 * 2**20, transcendentals=0),
     )
 
 
 def partners(msg_ref):
     code = msg_ref[ROWS : ROWS + CODE, :].astype(F32)
-    return code[0:4, :] * 512.0 + code[4:8, :]
+    return code[0:8, 0:128] * 512.0 + code[0:8, 128:256]
 
 
 def across(rows):
-    return jnp.concatenate([rows[k : k + 1, :] for k in range(4)], axis=1)
-
-
-def embed_kernel(features_ref, head_ref, partner_ref, msg_ref, raw_ref):
-    step = pl.program_id(0)
-    raw = jnp.dot(features_ref[...], head_ref[...], preferred_element_type=F32)
-    scale = lax.rsqrt(jnp.sum(raw * raw, axis=1, keepdims=True) + 1e-06)
-    raw_ref[...] = raw
-    at = pl.multiple_of(step * TILE, TILE)
-    msg_ref[pl.ds(at, TILE), :] = (raw * scale).astype(BF16)
-
-    @pl.when(step == 0)
-    def _():
-        ids = partner_ref[...]
-        high = (ids + 256) >> 9
-        low = ids - (high << 9)
-        code = jnp.concatenate([high, low, jnp.zeros((8, E), jnp.int32)], axis=0)
-        msg_ref[ROWS : ROWS + CODE, :] = code.astype(F32).astype(BF16)
+    return jnp.concatenate([rows[k : k + 1, :] for k in range(8)], axis=1)
+
+
+def embed_kernel(features_ref, head_ref, partner_ref, msg_ref, raw_ref, held, weights, arrived):
+    tiles = [slice(at, at + TILE) for at in range(0, ROWS, TILE)]
+    copies = [pltpu.make_async_copy(head_ref, weights, arrived.at[len(tiles)])]
+    for k, tile in enumerate(tiles):
+        copies.append(pltpu.make_async_copy(features_ref.at[tile, :], held.at[tile, :], arrived.at[k]))
+    for copy in copies:
+        copy.start()
+    ids = partner_ref[...]
+    high = (ids + 256) >> 9
+    low = ids - (high << 9)
+    code = jnp.concatenate([high, low], axis=1)
+    code = jnp.concatenate([code, jnp.zeros((8, E), jnp.int32)], axis=0)
+    msg_ref[ROWS : ROWS + CODE, :] = code.astype(F32).astype(BF16)
+    copies[0].wait()
+    for copy, tile in zip(copies[1:], tiles):
+        copy.wait()
+        raw = jnp.dot(held[tile, :], weights[...], preferred_element_type=F32)
+        scale = lax.rsqrt(jnp.sum(raw * raw, axis=1, keepdims=True) + 1e-06)
+        raw_ref[tile, :] = raw
+        msg_ref[tile, :] = (raw * scale).astype(BF16)
 
 
 def embed(features, head, partner):
     return pl.pallas_call(
         embed_kernel,
-        grid=(ROWS // TILE,),
         out_shape=(
             jax.ShapeDtypeStruct((ROWS + CODE, E), BF16),
             jax.ShapeDtypeStruct((ROWS, E), F32),
         ),
         in_specs=[
-            pl.BlockSpec((TILE, features.shape[1]), lambda i: (i, 0)),
-            pl.BlockSpec(head.shape, lambda i: (0, 0)),
-            pl.BlockSpec((4, E), lambda i: (0, 0)),
+            pl.BlockSpec(memory_space=pltpu.HBM),
+            pl.BlockSpec(memory_space=pltpu.HBM),
+            VMEM,
         ],
-        out_specs=(
-            pl.BlockSpec((ROWS + CODE, E), lambda i: (0, 0)),
-            pl.BlockSpec((TILE, E), lambda i: (i, 0)),
-        ),
-        compiler_params=pltpu.CompilerParams(vmem_limit_bytes=LIMIT),
+        out_specs=(VMEM, VMEM),
+        scratch_shapes=[
+            pltpu.VMEM(features.shape, BF16),
+            pltpu.VMEM(head.shape, BF16),
+            pltpu.SemaphoreType.DMA((ROWS // TILE + 1,)),
+        ],
+        compiler_params=pltpu.CompilerParams(vmem_limit_bytes=EMBED_LIMIT),
         cost_estimate=pl.CostEstimate(
             flops=2 * ROWS * 1024 * E, bytes_accessed=4 * 2**20, transcendentals=0
         ),
-    )(features, head, partner.reshape(4, E))
+    )(features, head, partner.reshape(8, 128))
 
 
 def term(rows_ref, cols_ref, total, found, same=False):
@@ -120,32 +129,25 @@
     for base, ref in ((0, mine_ref), (ROWS, other_ref)):
         ids = partners(ref)
         for k in range(8):
-            piece = ids[k // 2 : k // 2 + 1, (k % 2) * 128 : (k % 2) * 128 + 128]
             spread_ref[base + k * 128 : base + k * 128 + 128, :] = jnp.broadcast_to(
-                piece, (128, 128)
+                ids[k : k + 1, :], (128, 128)
             ).T
     found = matcher(spread_ref, 0, block_ref[0], across(partners(other_ref)), block_ref[1])
     for tile, value in term(mine_ref, other_ref, total, found):
         new_ref[tile, :] = grad_ref[tile, :] + value
 
 
-def mine_kernel(total, which, block_ref, cols_ref, mine_ref, spread_ref, grad_ref, new_ref):
-    found = matcher(
-        spread_ref, 0, block_ref[0], across(partners(cols_ref)), block_ref[which]
-    )
-    for tile, value in term(mine_ref, cols_ref, total, found):
-        new_ref[tile, :] = grad_ref[tile, :] + value
-
-
-def other_kernel(total, which, start, block_ref, cols_ref, other_ref, spread_ref, *rest):
-    new_ref = rest[-1]
-    found = matcher(
-        spread_ref, ROWS, block_ref[1], across(partners(cols_ref)), block_ref[which]
-    )
-    for tile, value in term(other_ref, cols_ref, total, found):
-        if not start:
-            value = rest[0][tile, :] + value
-        new_ref[tile, :] = value.astype(new_ref.dtype)
+def rows_kernel(total, which, jobs, outs, block_ref, cols_ref, spread_ref, *refs):
+    refs = list(refs)
+    given = [(refs.pop(0), refs.pop(0) if summed else None) for _, summed in jobs]
+    columns = across(partners(cols_ref))
+    refs = refs[len(refs) - outs :]
+    for (place, _), (rows_ref, old_ref), new_ref in zip(jobs, given, refs):
+        found = matcher(spread_ref, place * ROWS, block_ref[place], columns, block_ref[which])
+        for tile, value in term(rows_ref, cols_ref, total, found):
+            if old_ref is not None:
+                value = old_ref[tile, :].astype(F32) + value
+            new_ref[tile, :] = value.astype(new_ref.dtype)
 
 
 def final_kernel(features_ref, raw_ref, grad_ref, extra_ref, raw_grad_ref, partial_ref):
@@ -212,28 +214,23 @@
         pair,
     )(blocks, mine, other, grad)
 
-    def on_mine(grad, which, cols):
+    def on_rows(which, cols, jobs, outs, passed=None):
+        given = [x for rows, old in jobs for x in ((rows,) if old is None else (rows, old))]
+        plan = tuple((0 if rows is mine else 1, old is not None) for rows, old in jobs)
         return call(
-            functools.partial(mine_kernel, total, which), full, [SMEM] + [VMEM] * 4, pair
-        )(blocks, cols, mine, spread, grad)
-
-    def on_other(grad, which, cols, out=full):
-        given = () if grad is None else (grad,)
-        return call(
-            functools.partial(other_kernel, total, which, grad is None),
-            out,
-            [SMEM] + [VMEM] * (3 + len(given)),
-            pair,
-        )(blocks, cols, other, spread, *given)
-
-    theirs = on_other(None, 2, near_same)
-    grad = on_mine(grad, 2, near_same)
-    theirs = on_other(theirs, 3, near_cross)
-    grad = on_mine(grad, 3, near_cross)
-    grad = on_mine(grad, 4, far_same)
-    theirs = on_other(theirs, 5, far_cross, shape((ROWS, E), BF16))
+            functools.partial(rows_kernel, total, which, plan, len(outs) + (passed is not None)),
+            tuple(outs) + (() if passed is None else (shape(passed.shape, passed.dtype),)),
+            [SMEM] + [VMEM] * (2 + len(given)) + ([] if passed is None else [ANY]),
+            len(jobs) * pair,
+            {} if passed is None else {3 + len(given): len(outs)},
+        )(blocks, cols, spread, *given, *(() if passed is None else (passed,)))
+
+    theirs, grad = on_rows(2, near_same, [(other, None), (mine, grad)], [full, full])
+    theirs, grad = on_rows(3, near_cross, [(other, theirs), (mine, grad)], [full, full])
+    grad, theirs = on_rows(4, far_same, [(mine, grad)], [full], theirs)
+    (theirs,) = on_rows(5, far_cross, [(other, theirs)], [shape((ROWS, E), BF16)])
     extra = across_chip(theirs)
-    grad = on_mine(grad, 5, far_cross)
+    (grad,) = on_rows(5, far_cross, [(mine, grad)], [full])
 
     raw_grad, partial = call(
         final_kernel,

time: 76.1 us -> 72.5 us (0.953)
  local copies, waits for them, and re-layouts: 4.22 us -> 1.15 us
  Pallas kernels: 25.8 us -> 27.6 us
  starting transfers between devices: 25.8 us -> 24.6 us
  waiting for transfers between devices: 18.5 us -> 17.3 us
    ppermute x4, starting transfers between devices: 20.1 us -> 16.2 us  [onward(): return lax.ppermute(x, 'batch', hops)]
    all_to_all x1, starting transfers between devices: 3.9 us -> 6.45 us  [per_device(): parts = lax.all_to_all(partial.reshape(count, -1, E), 'batch', 0, 0)]
    unnamed x12 -> x10, local copies, waits for them, and re-layouts: 3.44 us -> 1.06 us
    pallas_call x8 -> x6, Pallas kernels: 18 us -> 19.8 us  [the longest x5 14.8 us: on_rows(): call(functools.partial(rows_kernel, total, which, plan, len(outs) + (pass...]
    ppermute x2, waiting for transfers between devices: 1.55 us -> 0.01 us  [across_chip(): return lax.ppermute(x, 'batch', [(i, i ^ 1) for i in range(count)])]
  transfers between devices with their start and end apart: 7 -> 7, of which waited for: 3 -> 3; matrix products, arithmetic and copies ran while one was open for 0% -> 0% of each run, Pallas kernels for 29% -> 25%
where the time goes in v3:
time: 72.5 us; the launch traced here: 72.2 us
  Pallas kernels  27.6 us (38%)
  starting transfers between devices  24.6 us (34%)
  waiting for transfers between devices  17.3 us (24%)
  local copies, waits for them, and re-layouts  1.15 us (2%)
  between operations  0.78 us (1%)
  other arithmetic  0.73 us (1%)
    ppermute x4, starting transfers between devices, onward(): return lax.ppermute(x, 'batch', hops)  16.2 us
    pallas_call x5, Pallas kernels, on_rows(): call(functools.partial(rows_kernel, total, which, plan, len(outs) + (pass...  14.8 us
    all_to_all x1, waiting for transfers between devices, per_device(): parts = lax.all_to_all(partial.reshape(count, -1, E), 'batch', 0, 0)  11.5 us
    all_to_all x1, starting transfers between devices, per_device(): parts = lax.all_to_all(partial.reshape(count, -1, E), 'batch', 0, 0)  6.45 us
    ppermute x4, waiting for transfers between devices, onward(): return lax.ppermute(x, 'batch', hops)  5.83 us
    pallas_call x1, Pallas kernels, embed(): pl.pallas_call(embed_kernel, out_shape=(jax.ShapeDtypeStruct((ROWS + CODE...  5.01 us
    pallas_call x1, Pallas kernels, per_device(): call(functools.partial(chip_kernel, total), (full, shape((2 * ROWS, 128),...  2.35 us
    pallas_call x1, Pallas kernels, per_device(): call(feature_kernel, shape((ROWS, features.shape[1]), BF16), [VMEM] * 2,...  2.07 us
  transfers between devices with their start and end apart: 7, of which 3 were waited for; matrix products, arithmetic and copies ran while one was open for 0% of the time, Pallas kernels for 25%

profile of v3, /device:TPU:1, one launch (start us, length us, event | category | flops | bytes accessed | tf_op | source)
XLA Modules:
  0.0 72.2 jit_solution(5888875675161842987)
XLA Ops:
  0.6 5.0 %shard_map.50 = (bf16[1040,256]{1,0:T(8,128)(2,1)}, f32[1024,256]{1,0:T(8,128)}) custom-call(bf16[1024,1024]{1,0:T(8,128)(2,1)} %features_ref.3, bf16[1024,256]{1,0:T(8,128)(2,1)} %head_ref.3, s32[8,128]{1,0:T(8,128)} %bitcast.8), custom_call_target="tpu_custom_call" | custom-call | flops 536870912 | bytes 4194304 | tf_op jit(solution)/shard_map/pallas_call | solution.py:68
  5.6 1.5 %collective-permute-start = (bf16[1040,256]{1,0:T(8,128)(2,1)}, bf16[1040,256]{1,0:T(8,128)(2,1)S(1)}, u32[]{:S(2)}, u32[]{:S(2)}) collective-permute-start(bf16[1040,256]{1,0:T(8,128)(2,1)} %get-tuple-element.15.mine_ref.refs_1_.refs_2_.refs_0_), channel_id=1, source_target_pairs={{0,1},{1,0},{2,3},{3,2},{4,5},{5,4},{6,7},{7,6},{8,9},{9,8},{10,11... | collective-permute-start | bytes 1597448 | tf_op jit(solution)/shard_map/ppermute | solution.py:180
  7.1 8.5 %collective-permute-start.3 = (bf16[1040,256]{1,0:T(8,128)(2,1)}, bf16[1040,256]{1,0:T(8,128)(2,1)S(1)}, u32[]{:S(2)}, u32[]{:S(2)}) collective-permute-start(bf16[1040,256]{1,0:T(8,128)(2,1)} %get-tuple-element.15.mine_ref.refs_1_.refs_2_.refs_0_), channel_id=1, source_target_pairs={{0,2},{1,127},{2,4},{3,1},{4,6},{5,3},{6,8},{7,5},{8,10},{9,7},{10... | collective-permute-start | bytes 1597448 | tf_op jit(solution)/shard_map/ppermute | solution.py:184
  15.6 0.1 stack.27.block_ref
  15.7 0.0 copy-start.3
  15.7 1.0 %copy-done.3 = bf16[1040,256]{1,0:T(8,128)(2,1)S(1)} copy-done((bf16[1040,256]{1,0:T(8,128)(2,1)S(1)}, bf16[1040,256]{1,0:T(8,128)(2,1)}, u32[]{:S(2)}) %copy-start.3) | copy-done | bytes 532504
  16.8 1.4 %shard_map.51.grad_ref = f32[1024,256]{1,0:T(8,128)S(1)} custom-call(bf16[1040,256]{1,0:T(8,128)(2,1)S(1)} %copy-done.3), custom_call_target="tpu_custom_call" | custom-call | flops 3221225472 | bytes 4194304 | tf_op jit(solution)/shard_map/pallas_call | solution.py:209
  18.2 0.0 collective-permute-done.other_ref.refs_0_
  18.2 0.2 collective-permute-start.1
  18.4 3.8 %collective-permute-done.3.cols_ref = bf16[1040,256]{1,0:T(8,128)(2,1)S(1)} collective-permute-done((bf16[1040,256]{1,0:T(8,128)(2,1)}, bf16[1040,256]{1,0:T(8,128)(2,1)S(1)}, u32[]{:S(2)}, u32[]{:S(2)}) %collective-permute-start.3) | collective-permute-done | bytes 532512 | tf_op jit(solution)/shard_map/ppermute | solution.py:184
  22.2 7.2 %collective-permute-start.4 = (bf16[1040,256]{1,0:T(8,128)(2,1)S(1)}, bf16[1040,256]{1,0:T(8,128)(2,1)S(1)}, u32[]{:S(2)}, u32[]{:S(2)}) collective-permute-start(bf16[1040,256]{1,0:T(8,128)(2,1)S(1)} %collective-permute-done.3.cols_ref), channel_id=1, source_target_pairs={{0,2},{1,127},{2,4},{3,1},{4,6},{5,3},{6,8},{7,5},{8,10},{9,7},{10... | collective-permute-start | bytes 1597448 | tf_op jit(solution)/shard_map/ppermute | solution.py:184
  29.4 2.4 %shard_map.52 = (f32[1024,256]{1,0:T(8,128)S(1)}, f32[2048,128]{1,0:T(8,128)S(1)}) custom-call(s32[6]{0:T(128)S(1)} %stack.27.block_ref, bf16[1040,256]{1,0:T(8,128)(2,1)S(1)} %copy-done.3, bf16[1040,256]{1,0:T(8,128)(2,1)S(1)} %collective-permute-done.other_ref.refs_0_, f32[1024,256]{1,0:T(8,128)S(1)} %shard_map.51.grad_ref), custom_call_target="tpu_custom_call" | custom-call | flops 3221225472 | bytes 4194304 | tf_op jit(solution)/shard_map/pallas_call | solution.py:210
  31.7 3.8 %shard_map.53 = (f32[1024,256]{1,0:T(8,128)S(1)}, f32[1024,256]{1,0:T(8,128)S(1)}) custom-call(s32[6]{0:T(128)S(1)} %stack.27.block_ref, bf16[1040,256]{1,0:T(8,128)(2,1)S(1)} %collective-permute-done.3.cols_ref, f32[2048,128]{1,0:T(8,128)S(1)} %get-tuple-element.16.spread_ref, bf16[1040,256]{1,0:T(8,128)(2,1)S(1)} %collective-permute-done.other_ref.refs_0_, ...), custom_call_target="tpu_custom_call" | custom-call | flops 6442450944 | bytes 4194304 | tf_op jit(solution)/shard_map/pallas_call | solution.py:220
  35.6 0.0 collective-permute-done.1.cols_ref
  35.6 0.3 collective-permute-start.2
  35.9 3.9 %shard_map.54 = (f32[1024,256]{1,0:T(8,128)S(1)}, f32[1024,256]{1,0:T(8,128)S(1)}) custom-call(s32[6]{0:T(128)S(1)} %stack.27.block_ref, bf16[1040,256]{1,0:T(8,128)(2,1)S(1)} %collective-permute-done.1.cols_ref, f32[2048,128]{1,0:T(8,128)S(1)} %get-tuple-element.16.spread_ref, bf16[1040,256]{1,0:T(8,128)(2,1)S(1)} %collective-permute-done.other_ref.refs_0_, ...), custom_call_target="tpu_custom_call" | custom-call | flops 6442450944 | bytes 4194304 | tf_op jit(solution)/shard_map/pallas_call | solution.py:220
  39.8 0.0 collective-permute-done.4.cols_ref
  39.8 2.4 %shard_map.55 = (f32[1024,256]{1,0:T(8,128)S(1)}, f32[1024,256]{1,0:T(8,128)S(1)}) custom-call(s32[6]{0:T(128)S(1)} %stack.27.block_ref, bf16[1040,256]{1,0:T(8,128)(2,1)S(1)} %collective-permute-done.4.cols_ref, f32[2048,128]{1,0:T(8,128)S(1)} %get-tuple-element.16.spread_ref, bf16[1040,256]{1,0:T(8,128)(2,1)S(1)} %copy-done.3, ...), custom_call_target="tpu_custom_call", output_to_operand_aliasing={{1}: (5, {})} | custom-call | flops 3221225472 | bytes 4194304 | tf_op jit(solution)/shard_map/pallas_call | solution.py:220
  42.2 2.1 %collective-permute-done.2.cols_ref = bf16[1040,256]{1,0:T(8,128)(2,1)S(1)} collective-permute-done((bf16[1040,256]{1,0:T(8,128)(2,1)S(1)}, bf16[1040,256]{1,0:T(8,128)(2,1)S(1)}, u32[]{:S(2)}, u32[]{:S(2)}) %collective-permute-start.2) | collective-permute-done | bytes 532512 | tf_op jit(solution)/shard_map/ppermute | solution.py:184
  44.2 0.0 copy-start.4
  44.2 2.3 %shard_map.57 = bf16[1024,256]{1,0:T(8,128)(2,1)S(1)} custom-call(s32[6]{0:T(128)S(1)} %stack.27.block_ref, bf16[1040,256]{1,0:T(8,128)(2,1)S(1)} %collective-permute-done.2.cols_ref, f32[2048,128]{1,0:T(8,128)S(1)} %get-tuple-element.16.spread_ref, bf16[1040,256]{1,0:T(8,128)(2,1)S(1)} %collective-permute-done.other_ref.refs_0_, ...), custom_call_target="tpu_custom_call" | custom-call | flops 3221225472 | bytes 4194304 | tf_op jit(solution)/shard_map/pallas_call | solution.py:220
  46.6 0.5 collective-permute-start.5
  47.1 0.0 copy-done.4
  47.1 0.0 copy-start
  47.1 0.0 copy-start.2
  47.1 2.3 %shard_map.56.grad_ref = f32[1024,256]{1,0:T(8,128)S(1)} custom-call(s32[6]{0:T(128)S(1)} %stack.27.block_ref, bf16[1040,256]{1,0:T(8,128)(2,1)S(1)} %collective-permute-done.2.cols_ref, f32[2048,128]{1,0:T(8,128)S(1)} %get-tuple-element.16.spread_ref, bf16[1040,256]{1,0:T(8,128)(2,1)S(1)} %copy-done.4, f32[1024,256]{1,0:T(8,128)S(1)} %get-tuple-element.22.refs_1_), custom_call_target="tpu_custom_call" | custom-call | flops 3221225472 | bytes 4194304 | tf_op jit(solution)/shard_map/pallas_call | solution.py:220
  49.4 0.0 collective-permute-done.5.extra_ref
  49.4 0.0 copy-done
  49.4 0.0 copy-done.2
  49.4 0.0 copy-start.1
  49.5 2.0 %shard_map.58 = (bf16[1024,256]{1,0:T(8,128)(2,1)S(1)}, bf16[1024,256]{1,0:T(8,128)(2,1)}) custom-call(bf16[1024,1024]{1,0:T(8,128)(2,1)S(1)} %copy-done, f32[1024,256]{1,0:T(8,128)S(1)} %copy-done.2, f32[1024,256]{1,0:T(8,128)S(1)} %shard_map.56.grad_ref, bf16[1024,256]{1,0:T(8,128)(2,1)S(1)} %collective-permute-done.5.extra_ref), custom_call_target="tpu_custom_call" | custom-call | flops 1610612736 | bytes 4194304 | tf_op jit(solution)/shard_map/pallas_call | solution.py:235
  51.5 6.4 %all-to-all-start = ((bf16[128,8,256]{2,1,0:T(8,128)(2,1)}), bf16[128,8,256]{2,1,0:T(8,128)(2,1)S(1)}, u32[]{:S(2)}, u32[]{:S(2)}) async-start(bf16[128,8,256]{2,1,0:T(8,128)(2,1)} %bitcast.7), calls=%async_computation | async-start | bytes 1048576 | tf_op jit(solution)/shard_map/all_to_all | solution.py:241
  57.9 0.0 copy-done.1
  57.9 2.1 %shard_map.59 = bf16[1024,1024]{1,0:T(8,128)(2,1)} custom-call(bf16[1024,256]{1,0:T(8,128)(2,1)S(1)} %get-tuple-element.24.raw_grad_ref, bf16[1024,256]{1,0:T(8,128)(2,1)S(1)} %copy-done.1), custom_call_target="tpu_custom_call" | custom-call | flops 1610612736 | bytes 4194304 | tf_op jit(solution)/shard_map/pallas_call | solution.py:242
  60.0 11.5 %all-to-all-done = bf16[128,8,256]{2,1,0:T(8,128)(2,1)S(1)} async-done(((bf16[128,8,256]{2,1,0:T(8,128)(2,1)}), bf16[128,8,256]{2,1,0:T(8,128)(2,1)S(1)}, u32[]{:S(2)}, u32[]{:S(2)}) %all-to-all-start) | async-done | bytes 524320 | tf_op jit(solution)/shard_map/all_to_all | solution.py:241
  71.5 0.7 %convert_reduce_fusion = f32[8,256]{1,0:T(8,128)} fusion(bf16[128,8,256]{2,1,0:T(8,128)(2,1)S(1)} %all-to-all-done), kind=kLoop, calls=%fused_computation | loop fusion | flops 522240 | bytes 532480 | tf_op jit(solution)/shard_map/reduce_sum | solution.py:245
Async XLA Ops:
  5.6 12.5 %collective-permute-start = (bf16[1040,256]{1,0:T(8,128)(2,1)}, bf16[1040,256]{1,0:T(8,128)(2,1)S(1)}, u32[]{:S(2)}, u32[]{:S(2)}) collective-permute-start(bf16[1040,256]{1,0:T(8,128)(2,1)} %get-tuple-element.15.mine_ref.refs_1_.refs_2_.refs_0_), channel_id=1, source_target_pairs={{0,1},{1,0},{2,3},{3,2},{4,5},{5,4},{6,7},{7,6},{8,9},{9,8},{10,11... | collective-permute-start | bytes 1597448 | tf_op jit(solution)/shard_map/ppermute | solution.py:180
  7.1 15.0 %collective-permute-start.3 = (bf16[1040,256]{1,0:T(8,128)(2,1)}, bf16[1040,256]{1,0:T(8,128)(2,1)S(1)}, u32[]{:S(2)}, u32[]{:S(2)}) collective-permute-start(bf16[1040,256]{1,0:T(8,128)(2,1)} %get-tuple-element.15.mine_ref.refs_1_.refs_2_.refs_0_), channel_id=1, source_target_pairs={{0,2},{1,127},{2,4},{3,1},{4,6},{5,3},{6,8},{7,5},{8,10},{9,7},{10... | collective-permute-start | bytes 1597448 | tf_op jit(solution)/shard_map/ppermute | solution.py:184
  15.7 1.0 %copy-start.3 = (bf16[1040,256]{1,0:T(8,128)(2,1)S(1)}, bf16[1040,256]{1,0:T(8,128)(2,1)}, u32[]{:S(2)}) copy-start(bf16[1040,256]{1,0:T(8,128)(2,1)} %get-tuple-element.15.mine_ref.refs_1_.refs_2_.refs_0_) | copy-start | bytes 1597444
  18.2 17.4 %collective-permute-start.1 = (bf16[1040,256]{1,0:T(8,128)(2,1)S(1)}, bf16[1040,256]{1,0:T(8,128)(2,1)S(1)}, u32[]{:S(2)}, u32[]{:S(2)}) collective-permute-start(bf16[1040,256]{1,0:T(8,128)(2,1)S(1)} %collective-permute-done.other_ref.refs_0_), channel_id=1, source_target_pairs={{0,2},{1,127},{2,4},{3,1},{4,6},{5,3},{6,8},{7,5},{8,10},{9,7},{10... | collective-permute-start | bytes 1597448 | tf_op jit(solution)/shard_map/ppermute | solution.py:184
  22.2 17.6 %collective-permute-start.4 = (bf16[1040,256]{1,0:T(8,128)(2,1)S(1)}, bf16[1040,256]{1,0:T(8,128)(2,1)S(1)}, u32[]{:S(2)}, u32[]{:S(2)}) collective-permute-start(bf16[1040,256]{1,0:T(8,128)(2,1)S(1)} %collective-permute-done.3.cols_ref), channel_id=1, source_target_pairs={{0,2},{1,127},{2,4},{3,1},{4,6},{5,3},{6,8},{7,5},{8,10},{9,7},{10... | collective-permute-start | bytes 1597448 | tf_op jit(solution)/shard_map/ppermute | solution.py:184
  35.6 8.6 %collective-permute-start.2 = (bf16[1040,256]{1,0:T(8,128)(2,1)S(1)}, bf16[1040,256]{1,0:T(8,128)(2,1)S(1)}, u32[]{:S(2)}, u32[]{:S(2)}) collective-permute-start(bf16[1040,256]{1,0:T(8,128)(2,1)S(1)} %collective-permute-done.1.cols_ref), channel_id=1, source_target_pairs={{0,2},{1,127},{2,4},{3,1},{4,6},{5,3},{6,8},{7,5},{8,10},{9,7},{10... | collective-permute-start | bytes 1597448 | tf_op jit(solution)/shard_map/ppermute | solution.py:184
  44.2 2.8 %copy-start.4 = (bf16[1040,256]{1,0:T(8,128)(2,1)S(1)}, bf16[1040,256]{1,0:T(8,128)(2,1)}, u32[]{:S(2)}) copy-start(bf16[1040,256]{1,0:T(8,128)(2,1)} %get-tuple-element.15.mine_ref.refs_1_.refs_2_.refs_0_) | copy-start | bytes 1597444
  46.6 2.8 %collective-permute-start.5 = (bf16[1024,256]{1,0:T(8,128)(2,1)S(1)}, bf16[1024,256]{1,0:T(8,128)(2,1)S(1)}, u32[]{:S(2)}, u32[]{:S(2)}) collective-permute-start(bf16[1024,256]{1,0:T(8,128)(2,1)S(1)} %shard_map.57), channel_id=1, source_target_pairs={{0,1},{1,0},{2,3},{3,2},{4,5},{5,4},{6,7},{7,6},{8,9},{9,8},{10,11... | collective-permute-start | bytes 1572872 | tf_op jit(solution)/shard_map/ppermute | solution.py:180
  47.1 2.4 %copy-start = (bf16[1024,1024]{1,0:T(8,128)(2,1)S(1)}, bf16[1024,1024]{1,0:T(8,128)(2,1)}, u32[]{:S(2)}) copy-start(bf16[1024,1024]{1,0:T(8,128)(2,1)} %features_ref.3) | copy-start | bytes 6291460
  47.1 2.4 %copy-start.2 = (f32[1024,256]{1,0:T(8,128)S(1)}, f32[1024,256]{1,0:T(8,128)}, u32[]{:S(2)}) copy-start(f32[1024,256]{1,0:T(8,128)} %get-tuple-element.14.raw_ref) | copy-start | bytes 3145732
  49.4 8.5 %copy-start.1 = (bf16[1024,256]{1,0:T(8,128)(2,1)S(1)}, bf16[1024,256]{1,0:T(8,128)(2,1)}, u32[]{:S(2)}) copy-start(bf16[1024,256]{1,0:T(8,128)(2,1)} %head_ref.3) | copy-start | bytes 1572868
  51.5 20.0 %all-to-all-start = ((bf16[128,8,256]{2,1,0:T(8,128)(2,1)}), bf16[128,8,256]{2,1,0:T(8,128)(2,1)S(1)}, u32[]{:S(2)}, u32[]{:S(2)}) async-start(bf16[128,8,256]{2,1,0:T(8,128)(2,1)} %bitcast.7), calls=%async_computation | async-start | bytes 1048576 | tf_op jit(solution)/shard_map/all_to_all | solution.py:241

commit v4 on v3

v4 whole, which is shorter than its diff:
```python
import functools
import math

import jax
import jax.numpy as jnp
from jax import lax
from jax.experimental import pallas as pl
from jax.experimental.pallas import tpu as pltpu
from jax.sharding import PartitionSpec as P

BF16, F32 = jnp.bfloat16, jnp.float32
ROWS, E, CODE = 1024, 256, 16
TILE = 256
VMEM = pl.BlockSpec(memory_space=pltpu.VMEM)
ANY = pl.BlockSpec(memory_space=pl.ANY)
SMEM = pl.BlockSpec(memory_space=pltpu.SMEM)
BOTH_LAST = (((1,), (1,)), ((), ()))
BOTH_FIRST = (((0,), (0,)), ((), ()))
LIMIT = 24 * 2**20
EMBED_LIMIT = 60 * 2**20
COST = 6
EMBED_TILE = 1024
SAME_PARTS, CROSS_PARTS = 1, 2


def call(body, outs, specs, flops, aliases=None):
    return pl.pallas_call(
        body,
        out_shape=outs,
        in_specs=specs,
        out_specs=jax.tree.map(lambda _: VMEM, outs) if not aliases else (VMEM, ANY),
        input_output_aliases=aliases or {},
        compiler_params=pltpu.CompilerParams(vmem_limit_bytes=LIMIT),
        cost_estimate=pl.CostEstimate(flops=int(COST * flops), bytes_accessed=4 * 2**20, transcendentals=0),
    )


def partners(part_ref):
    size = part_ref.shape[0] - CODE
    code = part_ref[size : size + CODE, :].astype(F32)
    lines = size // 128
    return code[0:lines, 0:128] * 512.0 + code[0:lines, 128:256]


def embed_kernel(cuts, features_ref, head_ref, partner_ref, *refs):
    raw_ref, parts = refs[0], refs[1 : 1 + len(cuts)]
    held, weights, ids_held, raw_held, unit_held, code_held, arrived, left = refs[1 + len(cuts) :]
    tiles = [slice(at, at + EMBED_TILE) for at in range(0, ROWS, EMBED_TILE)]
    arrivals = [
        pltpu.make_async_copy(partner_ref, ids_held, arrived.at[len(tiles) + 1]),
        pltpu.make_async_copy(head_ref, weights, arrived.at[len(tiles)]),
    ]
    for k, tile in enumerate(tiles):
        arrivals.append(
            pltpu.make_async_copy(features_ref.at[tile, :], held.at[tile, :], arrived.at[k])
        )
    for copy in arrivals:
        copy.start()
    leavings = []

    def leave(source, target):
        copy = pltpu.make_async_copy(source, target, left.at[len(leavings)])
        copy.start()
        leavings.append(copy)

    arrivals[0].wait()
    ids = ids_held[...]
    high = (ids + 256) >> 9
    low = ids - (high << 9)
    code = jnp.concatenate([high, low], axis=1).astype(F32)
    for k, ((at, size), ref) in enumerate(zip(cuts, parts)):
        lines = code[at // 128 : (at + size) // 128, :]
        blank = jnp.zeros((CODE - size // 128, E), F32)
        code_held[k] = jnp.concatenate([lines, blank], axis=0).astype(BF16)
        leave(code_held.at[k], ref.at[size : size + CODE, :])
    arrivals[1].wait()
    for copy, tile in zip(arrivals[2:], tiles):
        copy.wait()
        raw = jnp.dot(held[tile, :], weights[...], preferred_element_type=F32)
        scale = lax.rsqrt(jnp.sum(raw * raw, axis=1, keepdims=True) + 1e-06)
        unit_held[tile, :] = (raw * scale).astype(BF16)
        for (at, size), ref in zip(cuts, parts):
            low_at, high_at = max(at, tile.start), min(at + size, tile.stop)
            if low_at < high_at:
                leave(unit_held.at[low_at:high_at, :], ref.at[low_at - at : high_at - at, :])
        raw_held[tile, :] = raw
        leave(raw_held.at[tile, :], raw_ref.at[tile, :])
    for copy in leavings:
        copy.wait()


def embed(features, head, partner, cuts):
    outs = [jax.ShapeDtypeStruct((ROWS, E), F32)]
    outs += [jax.ShapeDtypeStruct((size + CODE, E), BF16) for _, size in cuts]
    hbm = pl.BlockSpec(memory_space=pltpu.HBM)
    tiles = ROWS // EMBED_TILE
    held = sum(max(size // EMBED_TILE, 1) for _, size in cuts)
    return pl.pallas_call(
        functools.partial(embed_kernel, cuts),
        out_shape=outs,
        in_specs=[hbm, hbm, hbm],
        out_specs=[hbm] * len(outs),
        scratch_shapes=[
            pltpu.VMEM(features.shape, BF16),
            pltpu.VMEM(head.shape, BF16),
            pltpu.VMEM((8, 128), jnp.int32),
            pltpu.VMEM((ROWS, E), F32),
            pltpu.VMEM((ROWS, E), BF16),
            pltpu.VMEM((len(cuts), CODE, E), BF16),
            pltpu.SemaphoreType.DMA((tiles + 2,)),
            pltpu.SemaphoreType.DMA((len(cuts) + held + tiles,)),
        ],
        compiler_params=pltpu.CompilerParams(vmem_limit_bytes=EMBED_LIMIT),
        cost_estimate=pl.CostEstimate(
            flops=2 * ROWS * 1024 * E, bytes_accessed=4 * 2**20, transcendentals=0
        ),
    )(features, head, partner.reshape(8, 128))


def tile_of(parts, at):
    size = parts[0].shape[0] - CODE
    return parts[at // size][at % size : at % size + TILE, :]


def term(rows, cols_ref, total, found, same_at=None):
    weight = 20.0 / total
    slope = 10.0 * math.log2(math.e)
    shift = slope - math.log2(weight)
    size = cols_ref.shape[0] - CODE
    cols = cols_ref[0:size, :]
    for at in range(0, ROWS, TILE):
        scores = lax.dot_general(tile_of(rows, at), cols, BOTH_LAST, preferred_element_type=F32)
        coef = 1.0 / (jnp.exp2(shift - scores * slope) + 1.0 / weight)
        if same_at is not None:
            i = lax.broadcasted_iota(jnp.int32, (TILE, size), 0) + at
            j = lax.broadcasted_iota(jnp.int32, (TILE, size), 1) + same_at
            coef = jnp.where(i != j, coef, 0.0)
        else:
            coef = jnp.where(found(at), coef - weight, coef)
        yield slice(at, at + TILE), jnp.dot(coef.astype(BF16), cols, preferred_element_type=F32)


def matcher(spread_ref, place, row_block, cols_ref, col_block, col_at):
    ids = partners(cols_ref)
    col_partner = jnp.concatenate([ids[k : k + 1, :] for k in range(ids.shape[0])], axis=1)
    size = col_partner.shape[1]
    j = lax.broadcasted_iota(jnp.int32, (1, size), 1) + (col_block * ROWS + col_at)
    col_ids = j.astype(F32)

    def found(at):
        i = lax.broadcasted_iota(jnp.int32, (TILE, 1), 0) + (row_block * ROWS + at)
        row_ids = i.astype(F32)
        theirs = spread_ref[place * ROWS + at : place * ROWS + at + TILE, :]
        return (jnp.tile(theirs, (1, size // 128)) == col_ids) | (col_partner == row_ids)

    return found


def diagonal_kernel(total, *refs):
    mine, grad_ref = refs[:-1], refs[-1]
    size = mine[0].shape[0] - CODE
    for k, part in enumerate(mine):
        for tile, value in term(mine, part, total, None, same_at=k * size):
            grad_ref[tile, :] = value if k == 0 else grad_ref[tile, :] + value


def chip_kernel(total, n_mine, block_ref, *refs):
    mine, other = refs[:n_mine], refs[n_mine:-3]
    grad_ref, new_ref, spread_ref = refs[-3:]
    for base, parts in ((0, mine), (ROWS, other)):
        at = base
        for part in parts:
            ids = partners(part)
            for k in range(ids.shape[0]):
                spread_ref[at : at + 128, :] = jnp.broadcast_to(ids[k : k + 1, :], (128, 128)).T
                at += 128
    size = other[0].shape[0] - CODE
    for k, part in enumerate(other):
        found = matcher(spread_ref, 0, block_ref[0], part, block_ref[1], k * size)
        old_ref = grad_ref if k == 0 else new_ref
        for tile, value in term(mine, part, total, found):
            new_ref[tile, :] = old_ref[tile, :] + value


def rows_kernel(total, which, col_at, jobs, outs, block_ref, cols_ref, spread_ref, *refs):
    refs = list(refs)
    news = refs[len(refs) - outs :]
    for (place, count, summed), new_ref in zip(jobs, news):
        rows, refs = refs[:count], refs[count:]
        old_ref = refs.pop(0) if summed else None
        found = matcher(spread_ref, place, block_ref[place], cols_ref, block_ref[which], col_at)
        for tile, value in term(rows, cols_ref, total, found):
            if old_ref is not None:
                value = old_ref[tile, :].astype(F32) + value
            new_ref[tile, :] = value.astype(new_ref.dtype)


def final_kernel(features_ref, raw_ref, grad_ref, extra_ref, raw_grad_ref, partial_ref):
    raw = raw_ref[...]
    grad = grad_ref[...] + extra_ref[...].astype(F32)
    scale = lax.rsqrt(jnp.sum(raw * raw, axis=1, keepdims=True) + 1e-06)
    unit = raw * scale
    along = jnp.sum(unit * grad, axis=1, keepdims=True)
    raw_grad_ref[...] = ((grad - unit * along) * scale).astype(BF16)
    partial_ref[...] = lax.dot_general(
        features_ref[...], raw_grad_ref[...], BOTH_FIRST, preferred_element_type=F32
    ).astype(BF16)


def feature_kernel(raw_grad_ref, head_ref, out_ref):
    out_ref[...] = lax.dot_general(
        raw_grad_ref[...], head_ref[...], BOTH_LAST, preferred_element_type=F32
    ).astype(BF16)


def per_device(features, head, partner):
    count = lax.axis_size("batch")
    owner = lax.axis_index("batch")
    total = float(ROWS * count)
    pair = 4 * ROWS * ROWS * E
    shape = jax.ShapeDtypeStruct
    full = shape((ROWS, E), F32)

    def across_chip(x):
        return lax.ppermute(x, "batch", [(i, i ^ 1) for i in range(count)])

    def onward(x):
        hops = [(i, (i + (2 if i % 2 == 0 else -2)) % count) for i in range(count)]
        return lax.ppermute(x, "batch", hops)

    core = owner % 2
    chip = owner // 2
    back = jnp.where(core == 0, -1, 1)
    near = (chip + back) % (count // 2)
    far = (chip + 2 * back) % (count // 2)
    blocks = jnp.stack(
        [
            owner,
            owner ^ 1,
            2 * near + core,
            2 * near + 1 - core,
            2 * far + core,
            2 * far + 1 - core,
        ]
    ).astype(jnp.int32)

    def cut(n):
        return [(k * ROWS // n, ROWS // n) for k in range(n)]

    if SAME_PARTS == CROSS_PARTS:
        raw, *mine = embed(features, head, partner, cut(SAME_PARTS))
        given_over = mine
    else:
        raw, *parts = embed(features, head, partner, cut(SAME_PARTS) + cut(CROSS_PARTS))
        mine, given_over = parts[:SAME_PARTS], parts[SAME_PARTS:]
    near_same = [onward(x) for x in mine]
    other = [across_chip(x) for x in given_over]

    grad = call(functools.partial(diagonal_kernel, total), full, [VMEM] * len(mine), pair)(*mine)
    grad, spread = call(
        functools.partial(chip_kernel, total, len(mine)),
        (full, shape((2 * ROWS, 128), F32)),
        [SMEM] + [VMEM] * (len(mine) + len(other) + 1),
        pair,
    )(blocks, *mine, *other, grad)
    near_cross = [onward(x) for x in other]
    far_same = [onward(x) for x in near_same]
    far_cross = [onward(x) for x in near_cross]

    def on_rows(which, at, cols, jobs, outs, passed=None):
        given, plan = [], []
        for rows, old in jobs:
            plan.append((0 if rows is mine else 1, len(rows), old is not None))
            given += list(rows) + ([] if old is None else [old])
        tied = [] if passed is None else [passed]
        return call(
            functools.partial(rows_kernel, total, which, at, tuple(plan), len(outs) + len(tied)),
            tuple(outs) + tuple(shape(x.shape, x.dtype) for x in tied),
            [SMEM] + [VMEM] * (2 + len(given)) + [ANY] * len(tied),
            len(jobs) * pair * (cols.shape[0] - CODE) // ROWS,
            {3 + len(given): len(outs)} if tied else {},
        )(blocks, cols, spread, *given, *tied)

    theirs = None
    for which, group in ((2, near_same), (3, near_cross)):
        for k, cols in enumerate(group):
            theirs, grad = on_rows(
                which, k * ROWS // len(group), cols, [(other, theirs), (mine, grad)], [full, full]
            )
    for k, cols in enumerate(far_same):
        grad, theirs = on_rows(4, k * ROWS // len(far_same), cols, [(mine, grad)], [full], theirs)
    for k, cols in enumerate(far_cross[:-1]):
        theirs, grad = on_rows(
            5, k * ROWS // len(far_cross), cols, [(other, theirs), (mine, grad)], [full, full]
        )
    last_at = ROWS - ROWS // len(far_cross)
    cols = far_cross[-1]
    (theirs,) = on_rows(5, last_at, cols, [(other, theirs)], [shape((ROWS, E), BF16)])
    extra = across_chip(theirs)
    (grad,) = on_rows(5, last_at, cols, [(mine, grad)], [full])

    raw_grad, partial = call(
        final_kernel,
        (shape((ROWS, E), BF16), shape((features.shape[1], E), BF16)),
        [VMEM] * 4,
        pair // 2,
    )(features, raw, grad, extra)
    parts = lax.all_to_all(partial.reshape(count, -1, E), "batch", 0, 0)
    feature_grad = call(
        feature_kernel, shape((ROWS, features.shape[1]), BF16), [VMEM] * 2, pair // 2
    )(raw_grad, head)
    head_grad = jnp.sum(parts.astype(F32), axis=0)
    return (feature_grad, head_grad)


def solution(mesh):
    in_specs = (P("batch", None), P(), P("batch"))
    out_specs = (P("batch", None), P("batch", None))
    return jax.shard_map(
        per_device, mesh=mesh, in_specs=in_specs, out_specs=out_specs, check_vma=False
    )
```

time: 72.5 us -> 69.6 us (0.960)
  waiting for transfers between devices: 17.3 us -> 13 us
  Pallas kernels: 27.6 us -> 28.7 us
    ppermute x4 -> x6, waiting for transfers between devices: 5.83 us -> 1.28 us  [onward(): return lax.ppermute(x, 'batch', hops)]
    ppermute x4 -> x6, starting transfers between devices: 16.2 us -> 17.9 us  [onward(): return lax.ppermute(x, 'batch', hops)]
    all_to_all x1, starting transfers between devices: 6.45 us -> 5.27 us  [per_device(): parts = lax.all_to_all(partial.reshape(count, -1, E), 'batch', 0, 0)]
    pallas_call x8 -> x10, Pallas kernels: 23.6 us -> 24.6 us  [the longest x7 16.9 us: on_rows(): call(functools.partial(rows_kernel, total, which, at, tuple(plan), len(ou...]
    ppermute x2 -> x3, starting transfers between devices: 1.97 us -> 1.68 us  [across_chip(): return lax.ppermute(x, 'batch', [(i, i ^ 1) for i in range(count)])]
  transfers between devices with their start and end apart: 7 -> 10, of which waited for: 3 -> 3; matrix products, arithmetic and copies ran while one was open for 0% -> 0% of each run, Pallas kernels for 25% -> 30%
where the time goes in v4:
time: 69.6 us; the launch traced here: 69.4 us
  Pallas kernels  28.7 us (41%)
  starting transfers between devices  24.8 us (36%)
  waiting for transfers between devices  13 us (19%)
  local copies, waits for them, and re-layouts  1.18 us (2%)
  between operations  0.86 us (1%)
  other arithmetic  0.73 us (1%)
    ppermute x6, starting transfers between devices, onward(): return lax.ppermute(x, 'batch', hops)  17.9 us
    pallas_call x7, Pallas kernels, on_rows(): call(functools.partial(rows_kernel, total, which, at, tuple(plan), len(ou...  16.9 us
    all_to_all x1, waiting for transfers between devices, per_device(): parts = lax.all_to_all(partial.reshape(count, -1, E), 'batch', 0, 0)  11.5 us
    all_to_all x1, starting transfers between devices, per_device(): parts = lax.all_to_all(partial.reshape(count, -1, E), 'batch', 0, 0)  5.27 us
    pallas_call x1, Pallas kernels, embed(): pl.pallas_call(functools.partial(embed_kernel, cuts), out_shape=outs, in_...  3.99 us
    pallas_call x1, Pallas kernels, per_device(): call(functools.partial(chip_kernel, total, len(mine)), (full, shape((2 *...  2.36 us
    pallas_call x1, Pallas kernels, per_device(): call(feature_kernel, shape((ROWS, features.shape[1]), BF16), [VMEM] * 2,...  2.07 us
    pallas_call x1, Pallas kernels, per_device(): call(final_kernel, (shape((ROWS, E), BF16), shape((features.shape[1], E),...  2.01 us
  transfers between devices with their start and end apart: 10, of which 3 were waited for; matrix products, arithmetic and copies ran while one was open for 0% of the time, Pallas kernels for 30%

profile of v4, /device:TPU:1, one launch (start us, length us, event | category | flops | bytes accessed | tf_op | source)
XLA Modules:
  0.0 69.4 jit_solution(6940878142637210374)
XLA Ops:
  0.6 4.0 %shard_map.50 = (f32[1024,256]{1,0:T(8,128)}, bf16[1040,256]{1,0:T(8,128)(2,1)}, bf16[528,256]{1,0:T(8,128)(2,1)}, bf16[528,256]{1,0:T(8,128)(2,1)}) custom-call(bf16[1024,1024]{1,0:T(8,128)(2,1)} %features_ref.3, bf16[1024,256]{1,0:T(8,128)(2,1)} %head_ref.3, s32[8,128]{1,0:T(8,128)} %bitcast.8), custom_call_target="tpu_custom_call" | custom-call | flops 536870912 | bytes 4194304 | tf_op jit(solution)/shard_map/pallas_call | solution.py:98
  4.6 1.5 %collective-permute-start = (bf16[528,256]{1,0:T(8,128)(2,1)}, bf16[528,256]{1,0:T(8,128)(2,1)S(1)}, u32[]{:S(2)}, u32[]{:S(2)}) collective-permute-start(bf16[528,256]{1,0:T(8,128)(2,1)} %get-tuple-element.21), channel_id=1, source_target_pairs={{0,1},{1,0},{2,3},{3,2},{4,5},{5,4},{6,7},{7,6},{8,9},{9,8},{10,11... | collective-permute-start | bytes 811016 | tf_op jit(solution)/shard_map/ppermute | solution.py:225
  6.1 0.1 collective-permute-start.3
  6.2 8.5 %collective-permute-start.6 = (bf16[1040,256]{1,0:T(8,128)(2,1)}, bf16[1040,256]{1,0:T(8,128)(2,1)S(1)}, u32[]{:S(2)}, u32[]{:S(2)}) collective-permute-start(bf16[1040,256]{1,0:T(8,128)(2,1)} %get-tuple-element.22.refs_0_.refs_2_.refs_3_), channel_id=1, source_target_pairs={{0,2},{1,127},{2,4},{3,1},{4,6},{5,3},{6,8},{7,5},{8,10},{9,7},{10... | collective-permute-start | bytes 1597448 | tf_op jit(solution)/shard_map/ppermute | solution.py:229
  14.7 0.0 copy-start.3
  14.7 1.1 %copy-done.3 = bf16[1040,256]{1,0:T(8,128)(2,1)S(1)} copy-done((bf16[1040,256]{1,0:T(8,128)(2,1)S(1)}, bf16[1040,256]{1,0:T(8,128)(2,1)}, u32[]{:S(2)}) %copy-start.3) | copy-done | bytes 532504
  15.8 0.0 copy-start.4
  15.8 1.4 %shard_map.51.refs_3_ = f32[1024,256]{1,0:T(8,128)S(1)} custom-call(bf16[1040,256]{1,0:T(8,128)(2,1)S(1)} %copy-done.3), custom_call_target="tpu_custom_call" | custom-call | flops 6442450944 | bytes 4194304 | tf_op jit(solution)/shard_map/pallas_call | solution.py:259
  17.3 0.1 stack.27.block_ref
  17.3 0.0 collective-permute-done.3.refs_1_.refs_0_
  17.4 0.2 collective-permute-start.4
  17.5 0.0 collective-permute-done.refs_2_.refs_1_
  17.5 0.1 collective-permute-start.1
  17.6 0.0 copy-done.4
  17.6 2.4 %shard_map.52 = (f32[1024,256]{1,0:T(8,128)S(1)}, f32[2048,128]{1,0:T(8,128)S(1)}) custom-call(s32[6]{0:T(128)S(1)} %stack.27.block_ref, bf16[1040,256]{1,0:T(8,128)(2,1)S(1)} %copy-done.4, bf16[528,256]{1,0:T(8,128)(2,1)S(1)} %collective-permute-done.3.refs_1_.refs_0_, bf16[528,256]{1,0:T(8,128)(2,1)S(1)} %collective-permute-done.refs_2_.refs_1_, ...), custom_call_target="tpu_custom_call" | custom-call | flops 6442450944 | bytes 4194304 | tf_op jit(solution)/shard_map/pallas_call | solution.py:260
  20.0 1.3 %collective-permute-done.6.cols_ref = bf16[1040,256]{1,0:T(8,128)(2,1)S(1)} collective-permute-done((bf16[1040,256]{1,0:T(8,128)(2,1)}, bf16[1040,256]{1,0:T(8,128)(2,1)S(1)}, u32[]{:S(2)}, u32[]{:S(2)}) %collective-permute-start.6) | collective-permute-done | bytes 532512 | tf_op jit(solution)/shard_map/ppermute | solution.py:229
  21.2 7.2 %collective-permute-start.7 = (bf16[1040,256]{1,0:T(8,128)(2,1)S(1)}, bf16[1040,256]{1,0:T(8,128)(2,1)S(1)}, u32[]{:S(2)}, u32[]{:S(2)}) collective-permute-start(bf16[1040,256]{1,0:T(8,128)(2,1)S(1)} %collective-permute-done.6.cols_ref), channel_id=1, source_target_pairs={{0,2},{1,127},{2,4},{3,1},{4,6},{5,3},{6,8},{7,5},{8,10},{9,7},{10... | collective-permute-start | bytes 1597448 | tf_op jit(solution)/shard_map/ppermute | solution.py:229
  28.5 3.8 %shard_map.53 = (f32[1024,256]{1,0:T(8,128)S(1)}, f32[1024,256]{1,0:T(8,128)S(1)}) custom-call(s32[6]{0:T(128)S(1)} %stack.27.block_ref, bf16[1040,256]{1,0:T(8,128)(2,1)S(1)} %collective-permute-done.6.cols_ref, f32[2048,128]{1,0:T(8,128)S(1)} %get-tuple-element.24.spread_ref, bf16[528,256]{1,0:T(8,128)(2,1)S(1)} %collective-permute-done.3.refs_1_.refs_0_, ...), custom_call_target="tpu_custom_call" | custom-call | flops 12884901888 | bytes 4194304 | tf_op jit(solution)/shard_map/pallas_call | solution.py:276
  32.3 0.0 collective-permute-done.4.cols_ref
  32.3 0.1 collective-permute-start.5
  32.4 0.0 collective-permute-done.1.cols_ref
  32.4 1.8 %collective-permute-start.2 = (bf16[528,256]{1,0:T(8,128)(2,1)S(1)}, bf16[528,256]{1,0:T(8,128)(2,1)S(1)}, u32[]{:S(2)}, u32[]{:S(2)}) collective-permute-start(bf16[528,256]{1,0:T(8,128)(2,1)S(1)} %collective-permute-done.1.cols_ref), channel_id=1, source_target_pairs={{0,2},{1,127},{2,4},{3,1},{4,6},{5,3},{6,8},{7,5},{8,10},{9,7},{10... | collective-permute-start | bytes 811016 | tf_op jit(solution)/shard_map/ppermute | solution.py:229
  34.3 2.5 %shard_map.54 = (f32[1024,256]{1,0:T(8,128)S(1)}, f32[1024,256]{1,0:T(8,128)S(1)}) custom-call(s32[6]{0:T(128)S(1)} %stack.27.block_ref, bf16[528,256]{1,0:T(8,128)(2,1)S(1)} %collective-permute-done.4.cols_ref, f32[2048,128]{1,0:T(8,128)S(1)} %get-tuple-element.24.spread_ref, bf16[528,256]{1,0:T(8,128)(2,1)S(1)} %collective-permute-done.3.refs_1_.refs_0_, ...), custom_call_target="tpu_custom_call" | custom-call | flops 6442450944 | bytes 4194304 | tf_op jit(solution)/shard_map/pallas_call | solution.py:276
  36.7 2.5 %shard_map.55 = (f32[1024,256]{1,0:T(8,128)S(1)}, f32[1024,256]{1,0:T(8,128)S(1)}) custom-call(s32[6]{0:T(128)S(1)} %stack.27.block_ref, bf16[528,256]{1,0:T(8,128)(2,1)S(1)} %collective-permute-done.1.cols_ref, f32[2048,128]{1,0:T(8,128)S(1)} %get-tuple-element.24.spread_ref, bf16[528,256]{1,0:T(8,128)(2,1)S(1)} %collective-permute-done.3.refs_1_.refs_0_, ...), custom_call_target="tpu_custom_call" | custom-call | flops 6442450944 | bytes 4194304 | tf_op jit(solution)/shard_map/pallas_call | solution.py:276
  39.3 0.0 collective-permute-done.7.cols_ref
  39.3 2.3 %shard_map.56 = (f32[1024,256]{1,0:T(8,128)S(1)}, f32[1024,256]{1,0:T(8,128)S(1)}) custom-call(s32[6]{0:T(128)S(1)} %stack.27.block_ref, bf16[1040,256]{1,0:T(8,128)(2,1)S(1)} %collective-permute-done.7.cols_ref, f32[2048,128]{1,0:T(8,128)S(1)} %get-tuple-element.24.spread_ref, bf16[1040,256]{1,0:T(8,128)(2,1)S(1)} %copy-done.4, ...), custom_call_target="tpu_custom_call", output_to_operand_aliasing={{1}: (5, {})} | custom-call | flops 6442450944 | bytes 4194304 | tf_op jit(solution)/shard_map/pallas_call | solution.py:276
  41.6 0.0 collective-permute-done.5.cols_ref
  41.6 2.5 %shard_map.57 = (f32[1024,256]{1,0:T(8,128)S(1)}, f32[1024,256]{1,0:T(8,128)S(1)}) custom-call(s32[6]{0:T(128)S(1)} %stack.27.block_ref, bf16[528,256]{1,0:T(8,128)(2,1)S(1)} %collective-permute-done.5.cols_ref, f32[2048,128]{1,0:T(8,128)S(1)} %get-tuple-element.24.spread_ref, bf16[528,256]{1,0:T(8,128)(2,1)S(1)} %collective-permute-done.3.refs_1_.refs_0_, ...), custom_call_target="tpu_custom_call" | custom-call | flops 6442450944 | bytes 4194304 | tf_op jit(solution)/shard_map/pallas_call | solution.py:276
  44.1 0.0 collective-permute-done.2.cols_ref
  44.1 1.6 %shard_map.59 = bf16[1024,256]{1,0:T(8,128)(2,1)S(1)} custom-call(s32[6]{0:T(128)S(1)} %stack.27.block_ref, bf16[528,256]{1,0:T(8,128)(2,1)S(1)} %collective-permute-done.2.cols_ref, f32[2048,128]{1,0:T(8,128)S(1)} %get-tuple-element.24.spread_ref, bf16[528,256]{1,0:T(8,128)(2,1)S(1)} %collective-permute-done.3.refs_1_.refs_0_, ...), custom_call_target="tpu_custom_call" | custom-call | flops 3221225472 | bytes 4194304 | tf_op jit(solution)/shard_map/pallas_call | solution.py:276
  45.8 0.1 collective-permute-start.8
  45.9 0.0 copy-start
  45.9 0.0 copy-start.2
  45.9 1.6 %shard_map.58.grad_ref = f32[1024,256]{1,0:T(8,128)S(1)} custom-call(s32[6]{0:T(128)S(1)} %stack.27.block_ref, bf16[528,256]{1,0:T(8,128)(2,1)S(1)} %collective-permute-done.2.cols_ref, f32[2048,128]{1,0:T(8,128)S(1)} %get-tuple-element.24.spread_ref, bf16[1040,256]{1,0:T(8,128)(2,1)S(1)} %copy-done.4, f32[1024,256]{1,0:T(8,128)S(1)} %get-tuple-element.34.refs_1_), custom_call_target="tpu_custom_call" | custom-call | flops 3221225472 | bytes 4194304 | tf_op jit(solution)/shard_map/pallas_call | solution.py:276
  47.5 0.3 collective-permute-done.8.extra_ref
  47.8 0.0 copy-done
  47.8 0.0 copy-done.2
  47.8 0.0 copy-start.1
  47.8 2.0 %shard_map.60 = (bf16[1024,256]{1,0:T(8,128)(2,1)S(1)}, bf16[1024,256]{1,0:T(8,128)(2,1)}) custom-call(bf16[1024,1024]{1,0:T(8,128)(2,1)S(1)} %copy-done, f32[1024,256]{1,0:T(8,128)S(1)} %copy-done.2, f32[1024,256]{1,0:T(8,128)S(1)} %shard_map.58.grad_ref, bf16[1024,256]{1,0:T(8,128)(2,1)S(1)} %collective-permute-done.8.extra_ref), custom_call_target="tpu_custom_call" | custom-call | flops 3221225472 | bytes 4194304 | tf_op jit(solution)/shard_map/pallas_call | solution.py:302
  49.8 5.3 %all-to-all-start = ((bf16[128,8,256]{2,1,0:T(8,128)(2,1)}), bf16[128,8,256]{2,1,0:T(8,128)(2,1)S(1)}, u32[]{:S(2)}, u32[]{:S(2)}) async-start(bf16[128,8,256]{2,1,0:T(8,128)(2,1)} %bitcast.7), calls=%async_computation | async-start | bytes 1048576 | tf_op jit(solution)/shard_map/all_to_all | solution.py:308
  55.1 0.0 copy-done.1
  55.1 2.1 %shard_map.61 = bf16[1024,1024]{1,0:T(8,128)(2,1)} custom-call(bf16[1024,256]{1,0:T(8,128)(2,1)S(1)} %get-tuple-element.36.raw_grad_ref, bf16[1024,256]{1,0:T(8,128)(2,1)S(1)} %copy-done.1), custom_call_target="tpu_custom_call" | custom-call | flops 3221225472 | bytes 4194304 | tf_op jit(solution)/shard_map/pallas_call | solution.py:309
  57.1 11.5 %all-to-all-done = bf16[128,8,256]{2,1,0:T(8,128)(2,1)S(1)} async-done(((bf16[128,8,256]{2,1,0:T(8,128)(2,1)}), bf16[128,8,256]{2,1,0:T(8,128)(2,1)S(1)}, u32[]{:S(2)}, u32[]{:S(2)}) %all-to-all-start) | async-done | bytes 524320 | tf_op jit(solution)/shard_map/all_to_all | solution.py:308
  68.6 0.7 %convert_reduce_fusion = f32[8,256]{1,0:T(8,128)} fusion(bf16[128,8,256]{2,1,0:T(8,128)(2,1)S(1)} %all-to-all-done), kind=kLoop, calls=%fused_computation | loop fusion | flops 522240 | bytes 532480 | tf_op jit(solution)/shard_map/reduce_sum | solution.py:312
Async XLA Ops:
  4.6 12.9 %collective-permute-start = (bf16[528,256]{1,0:T(8,128)(2,1)}, bf16[528,256]{1,0:T(8,128)(2,1)S(1)}, u32[]{:S(2)}, u32[]{:S(2)}) collective-permute-start(bf16[528,256]{1,0:T(8,128)(2,1)} %get-tuple-element.21), channel_id=1, source_target_pairs={{0,1},{1,0},{2,3},{3,2},{4,5},{5,4},{6,7},{7,6},{8,9},{9,8},{10,11... | collective-permute-start | bytes 811016 | tf_op jit(solution)/shard_map/ppermute | solution.py:225
  6.1 11.2 %collective-permute-start.3 = (bf16[528,256]{1,0:T(8,128)(2,1)}, bf16[528,256]{1,0:T(8,128)(2,1)S(1)}, u32[]{:S(2)}, u32[]{:S(2)}) collective-permute-start(bf16[528,256]{1,0:T(8,128)(2,1)} %get-tuple-element.23), channel_id=1, source_target_pairs={{0,1},{1,0},{2,3},{3,2},{4,5},{5,4},{6,7},{7,6},{8,9},{9,8},{10,11... | collective-permute-start | bytes 811016 | tf_op jit(solution)/shard_map/ppermute | solution.py:225
  6.2 15.0 %collective-permute-start.6 = (bf16[1040,256]{1,0:T(8,128)(2,1)}, bf16[1040,256]{1,0:T(8,128)(2,1)S(1)}, u32[]{:S(2)}, u32[]{:S(2)}) collective-permute-start(bf16[1040,256]{1,0:T(8,128)(2,1)} %get-tuple-element.22.refs_0_.refs_2_.refs_3_), channel_id=1, source_target_pairs={{0,2},{1,127},{2,4},{3,1},{4,6},{5,3},{6,8},{7,5},{8,10},{9,7},{10... | collective-permute-start | bytes 1597448 | tf_op jit(solution)/shard_map/ppermute | solution.py:229
  14.7 1.1 %copy-start.3 = (bf16[1040,256]{1,0:T(8,128)(2,1)S(1)}, bf16[1040,256]{1,0:T(8,128)(2,1)}, u32[]{:S(2)}) copy-start(bf16[1040,256]{1,0:T(8,128)(2,1)} %get-tuple-element.22.refs_0_.refs_2_.refs_3_) | copy-start | bytes 1597444
  15.8 1.8 %copy-start.4 = (bf16[1040,256]{1,0:T(8,128)(2,1)S(1)}, bf16[1040,256]{1,0:T(8,128)(2,1)}, u32[]{:S(2)}) copy-start(bf16[1040,256]{1,0:T(8,128)(2,1)} %get-tuple-element.22.refs_0_.refs_2_.refs_3_) | copy-start | bytes 1597444
  17.4 15.0 %collective-permute-start.4 = (bf16[528,256]{1,0:T(8,128)(2,1)S(1)}, bf16[528,256]{1,0:T(8,128)(2,1)S(1)}, u32[]{:S(2)}, u32[]{:S(2)}) collective-permute-start(bf16[528,256]{1,0:T(8,128)(2,1)S(1)} %collective-permute-done.3.refs_1_.refs_0_), channel_id=1, source_target_pairs={{0,2},{1,127},{2,4},{3,1},{4,6},{5,3},{6,8},{7,5},{8,10},{9,7},{10... | collective-permute-start | bytes 811016 | tf_op jit(solution)/shard_map/ppermute | solution.py:229
  17.5 14.9 %collective-permute-start.1 = (bf16[528,256]{1,0:T(8,128)(2,1)S(1)}, bf16[528,256]{1,0:T(8,128)(2,1)S(1)}, u32[]{:S(2)}, u32[]{:S(2)}) collective-permute-start(bf16[528,256]{1,0:T(8,128)(2,1)S(1)} %collective-permute-done.refs_2_.refs_1_), channel_id=1, source_target_pairs={{0,2},{1,127},{2,4},{3,1},{4,6},{5,3},{6,8},{7,5},{8,10},{9,7},{10... | collective-permute-start | bytes 811016 | tf_op jit(solution)/shard_map/ppermute | solution.py:229
  21.2 18.0 %collective-permute-start.7 = (bf16[1040,256]{1,0:T(8,128)(2,1)S(1)}, bf16[1040,256]{1,0:T(8,128)(2,1)S(1)}, u32[]{:S(2)}, u32[]{:S(2)}) collective-permute-start(bf16[1040,256]{1,0:T(8,128)(2,1)S(1)} %collective-permute-done.6.cols_ref), channel_id=1, source_target_pairs={{0,2},{1,127},{2,4},{3,1},{4,6},{5,3},{6,8},{7,5},{8,10},{9,7},{10... | collective-permute-start | bytes 1597448 | tf_op jit(solution)/shard_map/ppermute | solution.py:229
  32.3 9.3 %collective-permute-start.5 = (bf16[528,256]{1,0:T(8,128)(2,1)S(1)}, bf16[528,256]{1,0:T(8,128)(2,1)S(1)}, u32[]{:S(2)}, u32[]{:S(2)}) collective-permute-start(bf16[528,256]{1,0:T(8,128)(2,1)S(1)} %collective-permute-done.4.cols_ref), channel_id=1, source_target_pairs={{0,2},{1,127},{2,4},{3,1},{4,6},{5,3},{6,8},{7,5},{8,10},{9,7},{10... | collective-permute-start | bytes 811016 | tf_op jit(solution)/shard_map/ppermute | solution.py:229
  32.4 11.7 %collective-permute-start.2 = (bf16[528,256]{1,0:T(8,128)(2,1)S(1)}, bf16[528,256]{1,0:T(8,128)(2,1)S(1)}, u32[]{:S(2)}, u32[]{:S(2)}) collective-permute-start(bf16[528,256]{1,0:T(8,128)(2,1)S(1)} %collective-permute-done.1.cols_ref), channel_id=1, source_target_pairs={{0,2},{1,127},{2,4},{3,1},{4,6},{5,3},{6,8},{7,5},{8,10},{9,7},{10... | collective-permute-start | bytes 811016 | tf_op jit(solution)/shard_map/ppermute | solution.py:229
  45.8 2.0 %collective-permute-start.8 = (bf16[1024,256]{1,0:T(8,128)(2,1)S(1)}, bf16[1024,256]{1,0:T(8,128)(2,1)S(1)}, u32[]{:S(2)}, u32[]{:S(2)}) collective-permute-start(bf16[1024,256]{1,0:T(8,128)(2,1)S(1)} %shard_map.59), channel_id=1, source_target_pairs={{0,1},{1,0},{2,3},{3,2},{4,5},{5,4},{6,7},{7,6},{8,9},{9,8},{10,11... | collective-permute-start | bytes 1572872 | tf_op jit(solution)/shard_map/ppermute | solution.py:225
  45.9 1.9 %copy-start = (bf16[1024,1024]{1,0:T(8,128)(2,1)S(1)}, bf16[1024,1024]{1,0:T(8,128)(2,1)}, u32[]{:S(2)}) copy-start(bf16[1024,1024]{1,0:T(8,128)(2,1)} %features_ref.3) | copy-start | bytes 6291460
  45.9 1.9 %copy-start.2 = (f32[1024,256]{1,0:T(8,128)S(1)}, f32[1024,256]{1,0:T(8,128)}, u32[]{:S(2)}) copy-start(f32[1024,256]{1,0:T(8,128)} %get-tuple-element.20.raw_ref) | copy-start | bytes 3145732
  47.8 7.3 %copy-start.1 = (bf16[1024,256]{1,0:T(8,128)(2,1)S(1)}, bf16[1024,256]{1,0:T(8,128)(2,1)}, u32[]{:S(2)}) copy-start(bf16[1024,256]{1,0:T(8,128)(2,1)} %head_ref.3) | copy-start | bytes 1572868
  49.8 18.9 %all-to-all-start = ((bf16[128,8,256]{2,1,0:T(8,128)(2,1)}), bf16[128,8,256]{2,1,0:T(8,128)(2,1)S(1)}, u32[]{:S(2)}, u32[]{:S(2)}) async-start(bf16[128,8,256]{2,1,0:T(8,128)(2,1)} %bitcast.7), calls=%async_computation | async-start | bytes 1048576 | tf_op jit(solution)/shard_map/all_to_all | solution.py:308

commit v5 on v4

--- a/solution.py
+++ b/solution.py
@@ -13,14 +13,15 @@
 TILE = 256
 VMEM = pl.BlockSpec(memory_space=pltpu.VMEM)
 ANY = pl.BlockSpec(memory_space=pl.ANY)
-SMEM = pl.BlockSpec(memory_space=pltpu.SMEM)
 BOTH_LAST = (((1,), (1,)), ((), ()))
 BOTH_FIRST = (((0,), (0,)), ((), ()))
 LIMIT = 24 * 2**20
 EMBED_LIMIT = 60 * 2**20
-COST = 6
+COST = 1
+OWN_COST = 0.3
 EMBED_TILE = 1024
-SAME_PARTS, CROSS_PARTS = 1, 2
+SAME_PARTS, CROSS_PARTS = 2, 2
+TIES = 1
 
 
 def call(body, outs, specs, flops, aliases=None):
@@ -136,22 +137,33 @@
             j = lax.broadcasted_iota(jnp.int32, (TILE, size), 1) + same_at
             coef = jnp.where(i != j, coef, 0.0)
         else:
-            coef = jnp.where(found(at), coef - weight, coef)
+            coef = coef.astype(BF16)
+            coef = jnp.where(found(at), coef - jnp.bfloat16(weight), coef)
         yield slice(at, at + TILE), jnp.dot(coef.astype(BF16), cols, preferred_element_type=F32)
 
 
-def matcher(spread_ref, place, row_block, cols_ref, col_block, col_at):
+def matcher(spread_ref, place, row_first, cols_ref, col_first, col_at):
     ids = partners(cols_ref)
     col_partner = jnp.concatenate([ids[k : k + 1, :] for k in range(ids.shape[0])], axis=1)
     size = col_partner.shape[1]
-    j = lax.broadcasted_iota(jnp.int32, (1, size), 1) + (col_block * ROWS + col_at)
-    col_ids = j.astype(F32)
+    wide = size // 128
+
+    def small(local, end):
+        return jnp.clip(local, -1.0, float(end)).astype(jnp.int32).astype(jnp.int16)
+
+    col_partner = col_partner - jnp.tile(row_first, (1, wide))
+    col_partner = small(jnp.broadcast_to(col_partner, (16, size)), ROWS)
+    col_partner = jnp.tile(col_partner, (TILE // 16, 1))
+    col_ids = lax.broadcasted_iota(jnp.int32, (16, size), 1).astype(jnp.int16)
+    col_ids = jnp.tile(col_ids, (TILE // 16, 1))
 
     def found(at):
-        i = lax.broadcasted_iota(jnp.int32, (TILE, 1), 0) + (row_block * ROWS + at)
-        row_ids = i.astype(F32)
+        row_ids = (lax.broadcasted_iota(jnp.int32, (TILE, 128), 0) + at).astype(jnp.int16)
         theirs = spread_ref[place * ROWS + at : place * ROWS + at + TILE, :]
-        return (jnp.tile(theirs, (1, size // 128)) == col_ids) | (col_partner == row_ids)
+        theirs = small(theirs - (col_first + float(col_at)), size)
+        return (jnp.tile(theirs, (1, wide)) == col_ids) | (
+            col_partner == jnp.tile(row_ids, (1, wide))
+        )
 
     return found
 
@@ -164,9 +176,10 @@
             grad_ref[tile, :] = value if k == 0 else grad_ref[tile, :] + value
 
 
-def chip_kernel(total, n_mine, block_ref, *refs):
-    mine, other = refs[:n_mine], refs[n_mine:-3]
-    grad_ref, new_ref, spread_ref = refs[-3:]
+def chip_kernel(total, n_mine, first_ref, *refs):
+    mine, other = refs[:n_mine], refs[n_mine:-4]
+    grad_ref, new_ref, spread_ref, again_ref = refs[-4:]
+    again_ref[...] = other[-1][...]
     for base, parts in ((0, mine), (ROWS, other)):
         at = base
         for part in parts:
@@ -176,19 +189,20 @@
                 at += 128
     size = other[0].shape[0] - CODE
     for k, part in enumerate(other):
-        found = matcher(spread_ref, 0, block_ref[0], part, block_ref[1], k * size)
+        found = matcher(spread_ref, 0, first_ref[0:1, :], part, first_ref[1:2, :], k * size)
         old_ref = grad_ref if k == 0 else new_ref
         for tile, value in term(mine, part, total, found):
             new_ref[tile, :] = old_ref[tile, :] + value
 
 
-def rows_kernel(total, which, col_at, jobs, outs, block_ref, cols_ref, spread_ref, *refs):
+def rows_kernel(total, which, col_at, jobs, outs, first_ref, cols_ref, spread_ref, *refs):
     refs = list(refs)
     news = refs[len(refs) - outs :]
     for (place, count, summed), new_ref in zip(jobs, news):
         rows, refs = refs[:count], refs[count:]
         old_ref = refs.pop(0) if summed else None
-        found = matcher(spread_ref, place, block_ref[place], cols_ref, block_ref[which], col_at)
+        row_first, col_first = first_ref[place : place + 1, :], first_ref[which : which + 1, :]
+        found = matcher(spread_ref, place, row_first, cols_ref, col_first, col_at)
         for tile, value in term(rows, cols_ref, total, found):
             if old_ref is not None:
                 value = old_ref[tile, :].astype(F32) + value
@@ -233,7 +247,7 @@
     back = jnp.where(core == 0, -1, 1)
     near = (chip + back) % (count // 2)
     far = (chip + 2 * back) % (count // 2)
-    blocks = jnp.stack(
+    first_ids = jnp.stack(
         [
             owner,
             owner ^ 1,
@@ -241,8 +255,11 @@
             2 * near + 1 - core,
             2 * far + core,
             2 * far + 1 - core,
+            owner,
+            owner,
         ]
-    ).astype(jnp.int32)
+    )
+    first_ids = jnp.broadcast_to((first_ids * ROWS).astype(F32)[:, None], (8, 128))
 
     def cut(n):
         return [(k * ROWS // n, ROWS // n) for k in range(n)]
@@ -256,18 +273,18 @@
     near_same = [onward(x) for x in mine]
     other = [across_chip(x) for x in given_over]
 
-    grad = call(functools.partial(diagonal_kernel, total), full, [VMEM] * len(mine), pair)(*mine)
-    grad, spread = call(
+    grad = call(functools.partial(diagonal_kernel, total), full, [VMEM] * len(mine), OWN_COST * pair)(*mine)
+    grad, spread, again = call(
         functools.partial(chip_kernel, total, len(mine)),
-        (full, shape((2 * ROWS, 128), F32)),
-        [SMEM] + [VMEM] * (len(mine) + len(other) + 1),
-        pair,
-    )(blocks, *mine, *other, grad)
-    near_cross = [onward(x) for x in other]
+        (full, shape((2 * ROWS, 128), F32), shape(other[-1].shape, BF16)),
+        [VMEM] + [VMEM] * (len(mine) + len(other) + 1),
+        OWN_COST * pair,
+    )(first_ids, *mine, *other, grad)
+    near_cross = [onward(x) for x in other[:-1] + [again]]
     far_same = [onward(x) for x in near_same]
     far_cross = [onward(x) for x in near_cross]
 
-    def on_rows(which, at, cols, jobs, outs, passed=None):
+    def on_rows(which, at, cols, jobs, outs, passed=None, after=()):
         given, plan = [], []
         for rows, old in jobs:
             plan.append((0 if rows is mine else 1, len(rows), old is not None))
@@ -276,17 +293,19 @@
         return call(
             functools.partial(rows_kernel, total, which, at, tuple(plan), len(outs) + len(tied)),
             tuple(outs) + tuple(shape(x.shape, x.dtype) for x in tied),
-            [SMEM] + [VMEM] * (2 + len(given)) + [ANY] * len(tied),
+            [VMEM] + [VMEM] * (2 + len(given)) + [ANY] * (len(tied) + len(after)),
             len(jobs) * pair * (cols.shape[0] - CODE) // ROWS,
             {3 + len(given): len(outs)} if tied else {},
-        )(blocks, cols, spread, *given, *tied)
+        )(first_ids, cols, spread, *given, *tied, *after)
 
     theirs = None
-    for which, group in ((2, near_same), (3, near_cross)):
-        for k, cols in enumerate(group):
-            theirs, grad = on_rows(
-                which, k * ROWS // len(group), cols, [(other, theirs), (mine, grad)], [full, full]
-            )
+    near = [(2, k * ROWS // len(near_same), x) for k, x in enumerate(near_same)]
+    near += [(3, k * ROWS // len(near_cross), x) for k, x in enumerate(near_cross)]
+    for k, (which, at, cols) in enumerate(near):
+        after = [x for _, _, x in near[k + 1 : k + 2]] if k >= TIES else []
+        theirs, grad = on_rows(
+            which, at, cols, [(other, theirs), (mine, grad)], [full, full], after=after
+        )
     for k, cols in enumerate(far_same):
         grad, theirs = on_rows(4, k * ROWS // len(far_same), cols, [(mine, grad)], [full], theirs)
     for k, cols in enumerate(far_cross[:-1]):

time: 69.6 us -> 66.7 us (0.958)
  Pallas kernels: 28.7 us -> 23.7 us
  starting transfers between devices: 24.8 us -> 26.7 us
  local copies, waits for them, and re-layouts: 1.18 us -> 2.08 us
    pallas_call x7 -> x9, Pallas kernels: 16.9 us -> 12.7 us  [on_rows(): call(functools.partial(rows_kernel, total, which, at, tuple(plan), len(ou...]
    ppermute x6 -> x8, starting transfers between devices: 17.9 us -> 21.3 us  [onward(): return lax.ppermute(x, 'batch', hops)]
    all_to_all x1, starting transfers between devices: 5.27 us -> 3.72 us  [per_device(): parts = lax.all_to_all(partial.reshape(count, -1, E), 'batch', 0, 0)]
    ppermute x6 -> x8, waiting for transfers between devices: 1.28 us -> 0.02 us  [onward(): return lax.ppermute(x, 'batch', hops)]
    unnamed x10 -> x14, local copies, waits for them, and re-layouts: 1.1 us -> 1.93 us
    pallas_call x1, Pallas kernels: 2.36 us -> 1.63 us  [per_device(): call(functools.partial(chip_kernel, total, len(mine)), (full, shape((2 *...]
  transfers between devices with their start and end apart: 10 -> 12, of which waited for: 3 -> 2; matrix products, arithmetic and copies ran while one was open for 0% -> 0% of each run, Pallas kernels for 30% -> 25%
where the time goes in v5:
time: 66.7 us; the launch traced here: 66.4 us
  starting transfers between devices  26.7 us (40%)
  Pallas kernels  23.7 us (36%)
  waiting for transfers between devices  12.4 us (19%)
  local copies, waits for them, and re-layouts  2.08 us (3%)
  between operations  0.85 us (1%)
  other arithmetic  0.74 us (1%)
    ppermute x8, starting transfers between devices, onward(): return lax.ppermute(x, 'batch', hops)  21.3 us
    pallas_call x9, Pallas kernels, on_rows(): call(functools.partial(rows_kernel, total, which, at, tuple(plan), len(ou...  12.7 us
    all_to_all x1, waiting for transfers between devices, per_device(): parts = lax.all_to_all(partial.reshape(count, -1, E), 'batch', 0, 0)  11.5 us
    pallas_call x1, Pallas kernels, embed(): pl.pallas_call(functools.partial(embed_kernel, cuts), out_shape=outs, in_...  3.79 us
    all_to_all x1, starting transfers between devices, per_device(): parts = lax.all_to_all(partial.reshape(count, -1, E), 'batch', 0, 0)  3.72 us
    pallas_call x1, Pallas kernels, per_device(): call(feature_kernel, shape((ROWS, features.shape[1]), BF16), [VMEM] * 2,...  2.07 us
    pallas_call x1, Pallas kernels, per_device(): call(final_kernel, (shape((ROWS, E), BF16), shape((features.shape[1], E),...  2.04 us
    unnamed x14, local copies, waits for them, and re-layouts  1.93 us
  transfers between devices with their start and end apart: 12, of which 2 were waited for; matrix products, arithmetic and copies ran while one was open for 0% of the time, Pallas kernels for 25%

profile of v5, /device:TPU:1, one launch (start us, length us, event | category | flops | bytes accessed | tf_op | source)
XLA Modules:
  0.0 66.4 jit_solution(15591456492605425756)
XLA Ops:
  0.6 3.8 %shard_map.50 = (f32[1024,256]{1,0:T(8,128)}, bf16[528,256]{1,0:T(8,128)(2,1)}, bf16[528,256]{1,0:T(8,128)(2,1)}) custom-call(bf16[1024,1024]{1,0:T(8,128)(2,1)} %features_ref.3, bf16[1024,256]{1,0:T(8,128)(2,1)} %head_ref.3, s32[8,128]{1,0:T(8,128)} %bitcast.8), custom_call_target="tpu_custom_call" | custom-call | flops 536870912 | bytes 4194304 | tf_op jit(solution)/shard_map/pallas_call | solution.py:99
  4.4 1.5 %collective-permute-start = (bf16[528,256]{1,0:T(8,128)(2,1)}, bf16[528,256]{1,0:T(8,128)(2,1)S(1)}, u32[]{:S(2)}, u32[]{:S(2)}) collective-permute-start(bf16[528,256]{1,0:T(8,128)(2,1)} %get-tuple-element.25.refs_0_.refs_2_.refs_3_), channel_id=1, source_target_pairs={{0,1},{1,0},{2,3},{3,2},{4,5},{5,4},{6,7},{7,6},{8,9},{9,8},{10,11... | collective-permute-start | bytes 811016 | tf_op jit(solution)/shard_map/ppermute | solution.py:239
  5.9 0.1 collective-permute-start.1
  6.0 8.5 %collective-permute-start.8 = (bf16[528,256]{1,0:T(8,128)(2,1)}, bf16[528,256]{1,0:T(8,128)(2,1)S(1)}, u32[]{:S(2)}, u32[]{:S(2)}) collective-permute-start(bf16[528,256]{1,0:T(8,128)(2,1)} %get-tuple-element.25.refs_0_.refs_2_.refs_3_), channel_id=1, source_target_pairs={{0,2},{1,127},{2,4},{3,1},{4,6},{5,3},{6,8},{7,5},{8,10},{9,7},{10... | collective-permute-start | bytes 811016 | tf_op jit(solution)/shard_map/ppermute | solution.py:243
  14.5 0.1 collective-permute-start.6
  14.6 0.1 stack.29
  14.7 0.0 copy-start
  14.7 1.0 %copy-done = bf16[528,256]{1,0:T(8,128)(2,1)S(1)} copy-done((bf16[528,256]{1,0:T(8,128)(2,1)S(1)}, bf16[528,256]{1,0:T(8,128)(2,1)}, u32[]{:S(2)}) %copy-start) | copy-done | bytes 270360
  15.7 0.0 copy-start.2
  15.7 1.0 %copy-done.2 = bf16[528,256]{1,0:T(8,128)(2,1)S(1)} copy-done((bf16[528,256]{1,0:T(8,128)(2,1)S(1)}, bf16[528,256]{1,0:T(8,128)(2,1)}, u32[]{:S(2)}) %copy-start.2) | copy-done | bytes 270360
  16.6 1.4 %shard_map.51.refs_4_ = f32[1024,256]{1,0:T(8,128)S(1)} custom-call(bf16[528,256]{1,0:T(8,128)(2,1)S(1)} %copy-done, bf16[528,256]{1,0:T(8,128)(2,1)S(1)} %copy-done.2), custom_call_target="tpu_custom_call" | custom-call | flops 322122560 | bytes 4194304 | tf_op jit(solution)/shard_map/pallas_call | solution.py:276
  18.1 0.0 collective-permute-done.refs_2_.refs_0_
  18.1 0.1 collective-permute-start.4
  18.2 0.0 collective-permute-done.1.refs_3_.refs_1_
  18.2 0.1 broadcast_in_dim.2.first_ref
  18.2 1.6 %shard_map.52 = (f32[1024,256]{1,0:T(8,128)S(1)}, f32[2048,128]{1,0:T(8,128)S(1)}, bf16[528,256]{1,0:T(8,128)(2,1)S(1)}) custom-call(f32[8,128]{1,0:T(8,128)S(1)} %broadcast_in_dim.2.first_ref, bf16[528,256]{1,0:T(8,128)(2,1)S(1)} %copy-done, bf16[528,256]{1,0:T(8,128)(2,1)S(1)} %copy-done.2, bf16[528,256]{1,0:T(8,128)(2,1)S(1)} %collective-permute-done.refs_2_.refs_0_, ...), custom_call_target="tpu_custom_call" | custom-call | flops 322122560 | bytes 4194304 | tf_op jit(solution)/shard_map/pallas_call | solution.py:277
  19.9 0.1 collective-permute-start.2
  20.0 0.0 collective-permute-done.8.cols_ref
  20.0 5.5 %collective-permute-start.9 = (bf16[528,256]{1,0:T(8,128)(2,1)S(1)}, bf16[528,256]{1,0:T(8,128)(2,1)S(1)}, u32[]{:S(2)}, u32[]{:S(2)}) collective-permute-start(bf16[528,256]{1,0:T(8,128)(2,1)S(1)} %collective-permute-done.8.cols_ref), channel_id=1, source_target_pairs={{0,2},{1,127},{2,4},{3,1},{4,6},{5,3},{6,8},{7,5},{8,10},{9,7},{10... | collective-permute-start | bytes 811016 | tf_op jit(solution)/shard_map/ppermute | solution.py:243
  25.5 0.0 collective-permute-done.6.cols_ref
  25.5 2.9 %collective-permute-start.7 = (bf16[528,256]{1,0:T(8,128)(2,1)S(1)}, bf16[528,256]{1,0:T(8,128)(2,1)S(1)}, u32[]{:S(2)}, u32[]{:S(2)}) collective-permute-start(bf16[528,256]{1,0:T(8,128)(2,1)S(1)} %collective-permute-done.6.cols_ref), channel_id=1, source_target_pairs={{0,2},{1,127},{2,4},{3,1},{4,6},{5,3},{6,8},{7,5},{8,10},{9,7},{10... | collective-permute-start | bytes 811016 | tf_op jit(solution)/shard_map/ppermute | solution.py:243
  28.4 1.7 %shard_map.53 = (f32[1024,256]{1,0:T(8,128)S(1)}, f32[1024,256]{1,0:T(8,128)S(1)}) custom-call(f32[8,128]{1,0:T(8,128)S(1)} %broadcast_in_dim.2.first_ref, bf16[528,256]{1,0:T(8,128)(2,1)S(1)} %collective-permute-done.8.cols_ref, f32[2048,128]{1,0:T(8,128)S(1)} %get-tuple-element.28.spread_ref, bf16[528,256]{1,0:T(8,128)(2,1)S(1)} %collective-permute-done.refs_2_.refs_0_, ...), custom_call_target="tpu_custom_call" | custom-call | flops 1073741824 | bytes 4194304 | tf_op jit(solution)/shard_map/pallas_call | solution.py:293
  30.0 0.0 collective-permute-done.4.refs_6_.cols_ref
  30.1 1.2 %collective-permute-start.5 = (bf16[528,256]{1,0:T(8,128)(2,1)S(1)}, bf16[528,256]{1,0:T(8,128)(2,1)S(1)}, u32[]{:S(2)}, u32[]{:S(2)}) collective-permute-start(bf16[528,256]{1,0:T(8,128)(2,1)S(1)} %collective-permute-done.4.refs_6_.cols_ref), channel_id=1, source_target_pairs={{0,2},{1,127},{2,4},{3,1},{4,6},{5,3},{6,8},{7,5},{8,10},{9,7},{10... | collective-permute-start | bytes 811016 | tf_op jit(solution)/shard_map/ppermute | solution.py:243
  31.3 0.0 collective-permute-done.2.refs_6_.cols_ref
  31.3 2.9 %collective-permute-start.3 = (bf16[528,256]{1,0:T(8,128)(2,1)S(1)}, bf16[528,256]{1,0:T(8,128)(2,1)S(1)}, u32[]{:S(2)}, u32[]{:S(2)}) collective-permute-start(bf16[528,256]{1,0:T(8,128)(2,1)S(1)} %collective-permute-done.2.refs_6_.cols_ref), channel_id=1, source_target_pairs={{0,2},{1,127},{2,4},{3,1},{4,6},{5,3},{6,8},{7,5},{8,10},{9,7},{10... | collective-permute-start | bytes 811016 | tf_op jit(solution)/shard_map/ppermute | solution.py:243
  34.2 1.7 %shard_map.54 = (f32[1024,256]{1,0:T(8,128)S(1)}, f32[1024,256]{1,0:T(8,128)S(1)}) custom-call(f32[8,128]{1,0:T(8,128)S(1)} %broadcast_in_dim.2.first_ref, bf16[528,256]{1,0:T(8,128)(2,1)S(1)} %collective-permute-done.6.cols_ref, f32[2048,128]{1,0:T(8,128)S(1)} %get-tuple-element.28.spread_ref, bf16[528,256]{1,0:T(8,128)(2,1)S(1)} %collective-permute-done.refs_2_.refs_0_, ...), custom_call_target="tpu_custom_call" | custom-call | flops 1073741824 | bytes 4194304 | tf_op jit(solution)/shard_map/pallas_call | solution.py:293
  35.9 1.8 %shard_map.55 = (f32[1024,256]{1,0:T(8,128)S(1)}, f32[1024,256]{1,0:T(8,128)S(1)}) custom-call(f32[8,128]{1,0:T(8,128)S(1)} %broadcast_in_dim.2.first_ref, bf16[528,256]{1,0:T(8,128)(2,1)S(1)} %collective-permute-done.4.refs_6_.cols_ref, f32[2048,128]{1,0:T(8,128)S(1)} %get-tuple-element.28.spread_ref, ...), custom_call_target="tpu_custom_call" | custom-call | flops 1073741824 | bytes 4194304 | tf_op jit(solution)/shard_map/pallas_call | solution.py:293
  37.7 1.8 %shard_map.56 = (f32[1024,256]{1,0:T(8,128)S(1)}, f32[1024,256]{1,0:T(8,128)S(1)}) custom-call(f32[8,128]{1,0:T(8,128)S(1)} %broadcast_in_dim.2.first_ref, bf16[528,256]{1,0:T(8,128)(2,1)S(1)} %collective-permute-done.2.refs_6_.cols_ref, f32[2048,128]{1,0:T(8,128)S(1)} %get-tuple-element.28.spread_ref, ...), custom_call_target="tpu_custom_call" | custom-call | flops 1073741824 | bytes 4194304 | tf_op jit(solution)/shard_map/pallas_call | solution.py:293
  39.5 0.0 collective-permute-done.9.cols_ref
  39.5 1.0 %shard_map.57 = (f32[1024,256]{1,0:T(8,128)S(1)}, f32[1024,256]{1,0:T(8,128)S(1)}) custom-call(f32[8,128]{1,0:T(8,128)S(1)} %broadcast_in_dim.2.first_ref, bf16[528,256]{1,0:T(8,128)(2,1)S(1)} %collective-permute-done.9.cols_ref, f32[2048,128]{1,0:T(8,128)S(1)} %get-tuple-element.28.spread_ref, ...), custom_call_target="tpu_custom_call", output_to_operand_aliasing={{1}: (6, {})} | custom-call | flops 536870912 | bytes 4194304 | tf_op jit(solution)/shard_map/pallas_call | solution.py:293
  40.5 0.0 collective-permute-done.7.cols_ref
  40.5 1.0 %shard_map.58 = (f32[1024,256]{1,0:T(8,128)S(1)}, f32[1024,256]{1,0:T(8,128)S(1)}) custom-call(f32[8,128]{1,0:T(8,128)S(1)} %broadcast_in_dim.2.first_ref, bf16[528,256]{1,0:T(8,128)(2,1)S(1)} %collective-permute-done.7.cols_ref, f32[2048,128]{1,0:T(8,128)S(1)} %get-tuple-element.28.spread_ref, ...), custom_call_target="tpu_custom_call", output_to_operand_aliasing={{1}: (6, {})} | custom-call | flops 536870912 | bytes 4194304 | tf_op jit(solution)/shard_map/pallas_call | solution.py:293
  41.5 0.0 collective-permute-done.5.cols_ref
  41.5 1.8 %shard_map.59 = (f32[1024,256]{1,0:T(8,128)S(1)}, f32[1024,256]{1,0:T(8,128)S(1)}) custom-call(f32[8,128]{1,0:T(8,128)S(1)} %broadcast_in_dim.2.first_ref, bf16[528,256]{1,0:T(8,128)(2,1)S(1)} %collective-permute-done.5.cols_ref, f32[2048,128]{1,0:T(8,128)S(1)} %get-tuple-element.28.spread_ref, bf16[528,256]{1,0:T(8,128)(2,1)S(1)} %collective-permute-done.refs_2_.refs_0_, ...), custom_call_target="tpu_custom_call" | custom-call | flops 1073741824 | bytes 4194304 | tf_op jit(solution)/shard_map/pallas_call | solution.py:293
  43.3 0.0 copy-start.1
  43.3 0.0 copy-start.3
  43.3 0.0 collective-permute-done.3.cols_ref
  43.3 1.0 %shard_map.61 = bf16[1024,256]{1,0:T(8,128)(2,1)S(1)} custom-call(f32[8,128]{1,0:T(8,128)S(1)} %broadcast_in_dim.2.first_ref, bf16[528,256]{1,0:T(8,128)(2,1)S(1)} %collective-permute-done.3.cols_ref, f32[2048,128]{1,0:T(8,128)S(1)} %get-tuple-element.28.spread_ref, bf16[528,256]{1,0:T(8,128)(2,1)S(1)} %collective-permute-done.refs_2_.refs_0_, ...), custom_call_target="tpu_custom_call" | custom-call | flops 536870912 | bytes 4194304 | tf_op jit(solution)/shard_map/pallas_call | solution.py:293
  44.3 0.0 copy-start.4
  44.3 0.0 copy-start.6
  44.3 0.1 collective-permute-start.10
  44.4 0.0 copy-done.1
  44.4 0.0 copy-done.3
  44.5 1.0 %shard_map.60.grad_ref = f32[1024,256]{1,0:T(8,128)S(1)} custom-call(f32[8,128]{1,0:T(8,128)S(1)} %broadcast_in_dim.2.first_ref, bf16[528,256]{1,0:T(8,128)(2,1)S(1)} %collective-permute-done.3.cols_ref, f32[2048,128]{1,0:T(8,128)S(1)} %get-tuple-element.28.spread_ref, bf16[528,256]{1,0:T(8,128)(2,1)S(1)} %copy-done.1, bf16[528,256]{1,0:T(8,128)(2,1)S(1)} %copy-done.3, ...), custom_call_target="tpu_custom_call" | custom-call | flops 536870912 | bytes 4194304 | tf_op jit(solution)/shard_map/pallas_call | solution.py:293
  45.4 0.9 %collective-permute-done.10.extra_ref = bf16[1024,256]{1,0:T(8,128)(2,1)S(1)} collective-permute-done((bf16[1024,256]{1,0:T(8,128)(2,1)S(1)}, bf16[1024,256]{1,0:T(8,128)(2,1)S(1)}, u32[]{:S(2)}, u32[]{:S(2)}) %collective-permute-start.10) | collective-permute-done | bytes 524320 | tf_op jit(solution)/shard_map/ppermute | solution.py:239
  46.3 0.0 copy-done.4
  46.3 0.0 copy-done.6
  46.3 0.0 copy-start.5
  46.3 2.0 %shard_map.62 = (bf16[1024,256]{1,0:T(8,128)(2,1)S(1)}, bf16[1024,256]{1,0:T(8,128)(2,1)}) custom-call(bf16[1024,1024]{1,0:T(8,128)(2,1)S(1)} %copy-done.4, f32[1024,256]{1,0:T(8,128)S(1)} %copy-done.6, f32[1024,256]{1,0:T(8,128)S(1)} %shard_map.60.grad_ref, bf16[1024,256]{1,0:T(8,128)(2,1)S(1)} %collective-permute-done.10.extra_ref), custom_call_target="tpu_custom_call" | custom-call | flops 536870912 | bytes 4194304 | tf_op jit(solution)/shard_map/pallas_call | solution.py:321
  48.4 3.7 %all-to-all-start = ((bf16[128,8,256]{2,1,0:T(8,128)(2,1)}), bf16[128,8,256]{2,1,0:T(8,128)(2,1)S(1)}, u32[]{:S(2)}, u32[]{:S(2)}) async-start(bf16[128,8,256]{2,1,0:T(8,128)(2,1)} %bitcast.7), calls=%async_computation | async-start | bytes 1048576 | tf_op jit(solution)/shard_map/all_to_all | solution.py:327
  52.1 0.0 copy-done.5
  52.1 2.1 %shard_map.63 = bf16[1024,1024]{1,0:T(8,128)(2,1)} custom-call(bf16[1024,256]{1,0:T(8,128)(2,1)S(1)} %get-tuple-element.44.raw_grad_ref, bf16[1024,256]{1,0:T(8,128)(2,1)S(1)} %copy-done.5), custom_call_target="tpu_custom_call" | custom-call | flops 536870912 | bytes 4194304 | tf_op jit(solution)/shard_map/pallas_call | solution.py:328
  54.2 11.5 %all-to-all-done = bf16[128,8,256]{2,1,0:T(8,128)(2,1)S(1)} async-done(((bf16[128,8,256]{2,1,0:T(8,128)(2,1)}), bf16[128,8,256]{2,1,0:T(8,128)(2,1)S(1)}, u32[]{:S(2)}, u32[]{:S(2)}) %all-to-all-start) | async-done | bytes 524320 | tf_op jit(solution)/shard_map/all_to_all | solution.py:327
  65.7 0.7 %convert_reduce_fusion = f32[8,256]{1,0:T(8,128)} fusion(bf16[128,8,256]{2,1,0:T(8,128)(2,1)S(1)} %all-to-all-done), kind=kLoop, calls=%fused_computation | loop fusion | flops 522240 | bytes 532480 | tf_op jit(solution)/shard_map/reduce_sum | solution.py:331
  (1 shorter events, 0.0 us)
Async XLA Ops:
  4.4 13.6 %collective-permute-start = (bf16[528,256]{1,0:T(8,128)(2,1)}, bf16[528,256]{1,0:T(8,128)(2,1)S(1)}, u32[]{:S(2)}, u32[]{:S(2)}) collective-permute-start(bf16[528,256]{1,0:T(8,128)(2,1)} %get-tuple-element.25.refs_0_.refs_2_.refs_3_), channel_id=1, source_target_pairs={{0,1},{1,0},{2,3},{3,2},{4,5},{5,4},{6,7},{7,6},{8,9},{9,8},{10,11... | collective-permute-start | bytes 811016 | tf_op jit(solution)/shard_map/ppermute | solution.py:239
  5.9 12.2 %collective-permute-start.1 = (bf16[528,256]{1,0:T(8,128)(2,1)}, bf16[528,256]{1,0:T(8,128)(2,1)S(1)}, u32[]{:S(2)}, u32[]{:S(2)}) collective-permute-start(bf16[528,256]{1,0:T(8,128)(2,1)} %get-tuple-element.26.refs_1_.refs_3_.refs_4_), channel_id=1, source_target_pairs={{0,1},{1,0},{2,3},{3,2},{4,5},{5,4},{6,7},{7,6},{8,9},{9,8},{10,11... | collective-permute-start | bytes 811016 | tf_op jit(solution)/shard_map/ppermute | solution.py:239
  6.0 13.9 %collective-permute-start.8 = (bf16[528,256]{1,0:T(8,128)(2,1)}, bf16[528,256]{1,0:T(8,128)(2,1)S(1)}, u32[]{:S(2)}, u32[]{:S(2)}) collective-permute-start(bf16[528,256]{1,0:T(8,128)(2,1)} %get-tuple-element.25.refs_0_.refs_2_.refs_3_), channel_id=1, source_target_pairs={{0,2},{1,127},{2,4},{3,1},{4,6},{5,3},{6,8},{7,5},{8,10},{9,7},{10... | collective-permute-start | bytes 811016 | tf_op jit(solution)/shard_map/ppermute | solution.py:243
  14.5 11.0 %collective-permute-start.6 = (bf16[528,256]{1,0:T(8,128)(2,1)}, bf16[528,256]{1,0:T(8,128)(2,1)S(1)}, u32[]{:S(2)}, u32[]{:S(2)}) collective-permute-start(bf16[528,256]{1,0:T(8,128)(2,1)} %get-tuple-element.26.refs_1_.refs_3_.refs_4_), channel_id=1, source_target_pairs={{0,2},{1,127},{2,4},{3,1},{4,6},{5,3},{6,8},{7,5},{8,10},{9,7},{10... | collective-permute-start | bytes 811016 | tf_op jit(solution)/shard_map/ppermute | solution.py:243
  14.7 1.0 %copy-start = (bf16[528,256]{1,0:T(8,128)(2,1)S(1)}, bf16[528,256]{1,0:T(8,128)(2,1)}, u32[]{:S(2)}) copy-start(bf16[528,256]{1,0:T(8,128)(2,1)} %get-tuple-element.25.refs_0_.refs_2_.refs_3_) | copy-start | bytes 811012
  15.7 1.0 %copy-start.2 = (bf16[528,256]{1,0:T(8,128)(2,1)S(1)}, bf16[528,256]{1,0:T(8,128)(2,1)}, u32[]{:S(2)}) copy-start(bf16[528,256]{1,0:T(8,128)(2,1)} %get-tuple-element.26.refs_1_.refs_3_.refs_4_) | copy-start | bytes 811012
  18.1 12.0 %collective-permute-start.4 = (bf16[528,256]{1,0:T(8,128)(2,1)S(1)}, bf16[528,256]{1,0:T(8,128)(2,1)S(1)}, u32[]{:S(2)}, u32[]{:S(2)}) collective-permute-start(bf16[528,256]{1,0:T(8,128)(2,1)S(1)} %collective-permute-done.refs_2_.refs_0_), channel_id=1, source_target_pairs={{0,2},{1,127},{2,4},{3,1},{4,6},{5,3},{6,8},{7,5},{8,10},{9,7},{10... | collective-permute-start | bytes 811016 | tf_op jit(solution)/shard_map/ppermute | solution.py:243
  19.9 11.4 %collective-permute-start.2 = (bf16[528,256]{1,0:T(8,128)(2,1)S(1)}, bf16[528,256]{1,0:T(8,128)(2,1)S(1)}, u32[]{:S(2)}, u32[]{:S(2)}) collective-permute-start(bf16[528,256]{1,0:T(8,128)(2,1)S(1)} %get-tuple-element.27), channel_id=1, source_target_pairs={{0,2},{1,127},{2,4},{3,1},{4,6},{5,3},{6,8},{7,5},{8,10},{9,7},{10... | collective-permute-start | bytes 811016 | tf_op jit(solution)/shard_map/ppermute | solution.py:243
  20.0 19.5 %collective-permute-start.9 = (bf16[528,256]{1,0:T(8,128)(2,1)S(1)}, bf16[528,256]{1,0:T(8,128)(2,1)S(1)}, u32[]{:S(2)}, u32[]{:S(2)}) collective-permute-start(bf16[528,256]{1,0:T(8,128)(2,1)S(1)} %collective-permute-done.8.cols_ref), channel_id=1, source_target_pairs={{0,2},{1,127},{2,4},{3,1},{4,6},{5,3},{6,8},{7,5},{8,10},{9,7},{10... | collective-permute-start | bytes 811016 | tf_op jit(solution)/shard_map/ppermute | solution.py:243
  25.5 15.0 %collective-permute-start.7 = (bf16[528,256]{1,0:T(8,128)(2,1)S(1)}, bf16[528,256]{1,0:T(8,128)(2,1)S(1)}, u32[]{:S(2)}, u32[]{:S(2)}) collective-permute-start(bf16[528,256]{1,0:T(8,128)(2,1)S(1)} %collective-permute-done.6.cols_ref), channel_id=1, source_target_pairs={{0,2},{1,127},{2,4},{3,1},{4,6},{5,3},{6,8},{7,5},{8,10},{9,7},{10... | collective-permute-start | bytes 811016 | tf_op jit(solution)/shard_map/ppermute | solution.py:243
  30.1 11.4 %collective-permute-start.5 = (bf16[528,256]{1,0:T(8,128)(2,1)S(1)}, bf16[528,256]{1,0:T(8,128)(2,1)S(1)}, u32[]{:S(2)}, u32[]{:S(2)}) collective-permute-start(bf16[528,256]{1,0:T(8,128)(2,1)S(1)} %collective-permute-done.4.refs_6_.cols_ref), channel_id=1, source_target_pairs={{0,2},{1,127},{2,4},{3,1},{4,6},{5,3},{6,8},{7,5},{8,10},{9,7},{10... | collective-permute-start | bytes 811016 | tf_op jit(solution)/shard_map/ppermute | solution.py:243
  31.3 12.0 %collective-permute-start.3 = (bf16[528,256]{1,0:T(8,128)(2,1)S(1)}, bf16[528,256]{1,0:T(8,128)(2,1)S(1)}, u32[]{:S(2)}, u32[]{:S(2)}) collective-permute-start(bf16[528,256]{1,0:T(8,128)(2,1)S(1)} %collective-permute-done.2.refs_6_.cols_ref), channel_id=1, source_target_pairs={{0,2},{1,127},{2,4},{3,1},{4,6},{5,3},{6,8},{7,5},{8,10},{9,7},{10... | collective-permute-start | bytes 811016 | tf_op jit(solution)/shard_map/ppermute | solution.py:243
  43.3 1.2 %copy-start.1 = (bf16[528,256]{1,0:T(8,128)(2,1)S(1)}, bf16[528,256]{1,0:T(8,128)(2,1)}, u32[]{:S(2)}) copy-start(bf16[528,256]{1,0:T(8,128)(2,1)} %get-tuple-element.25.refs_0_.refs_2_.refs_3_) | copy-start | bytes 811012
  43.3 1.2 %copy-start.3 = (bf16[528,256]{1,0:T(8,128)(2,1)S(1)}, bf16[528,256]{1,0:T(8,128)(2,1)}, u32[]{:S(2)}) copy-start(bf16[528,256]{1,0:T(8,128)(2,1)} %get-tuple-element.26.refs_1_.refs_3_.refs_4_) | copy-start | bytes 811012
  44.3 2.0 %copy-start.4 = (bf16[1024,1024]{1,0:T(8,128)(2,1)S(1)}, bf16[1024,1024]{1,0:T(8,128)(2,1)}, u32[]{:S(2)}) copy-start(bf16[1024,1024]{1,0:T(8,128)(2,1)} %features_ref.3) | copy-start | bytes 6291460
  44.3 2.0 %copy-start.6 = (f32[1024,256]{1,0:T(8,128)S(1)}, f32[1024,256]{1,0:T(8,128)}, u32[]{:S(2)}) copy-start(f32[1024,256]{1,0:T(8,128)} %get-tuple-element.24.raw_ref) | copy-start | bytes 3145732
  44.3 2.0 %collective-permute-start.10 = (bf16[1024,256]{1,0:T(8,128)(2,1)S(1)}, bf16[1024,256]{1,0:T(8,128)(2,1)S(1)}, u32[]{:S(2)}, u32[]{:S(2)}) collective-permute-start(bf16[1024,256]{1,0:T(8,128)(2,1)S(1)} %shard_map.61), channel_id=1, source_target_pairs={{0,1},{1,0},{2,3},{3,2},{4,5},{5,4},{6,7},{7,6},{8,9},{9,8},{10,11... | collective-permute-start | bytes 1572872 | tf_op jit(solution)/shard_map/ppermute | solution.py:239
  46.3 5.8 %copy-start.5 = (bf16[1024,256]{1,0:T(8,128)(2,1)S(1)}, bf16[1024,256]{1,0:T(8,128)(2,1)}, u32[]{:S(2)}) copy-start(bf16[1024,256]{1,0:T(8,128)(2,1)} %head_ref.3) | copy-start | bytes 1572868
  48.4 17.3 %all-to-all-start = ((bf16[128,8,256]{2,1,0:T(8,128)(2,1)}), bf16[128,8,256]{2,1,0:T(8,128)(2,1)S(1)}, u32[]{:S(2)}, u32[]{:S(2)}) async-start(bf16[128,8,256]{2,1,0:T(8,128)(2,1)} %bitcast.7), calls=%async_computation | async-start | bytes 1048576 | tf_op jit(solution)/shard_map/all_to_all | solution.py:327

commit v6 on v5

--- a/solution.py
+++ b/solution.py
@@ -11,13 +11,14 @@
 BF16, F32 = jnp.bfloat16, jnp.float32
 ROWS, E, CODE = 1024, 256, 16
 TILE = 256
+FINAL_TILE = 512
 VMEM = pl.BlockSpec(memory_space=pltpu.VMEM)
 ANY = pl.BlockSpec(memory_space=pl.ANY)
 BOTH_LAST = (((1,), (1,)), ((), ()))
 BOTH_FIRST = (((0,), (0,)), ((), ()))
 LIMIT = 24 * 2**20
 EMBED_LIMIT = 60 * 2**20
-COST = 1
+COST = 0.7
 OWN_COST = 0.3
 EMBED_TILE = 1024
 SAME_PARTS, CROSS_PARTS = 2, 2
@@ -195,30 +196,46 @@
             new_ref[tile, :] = old_ref[tile, :] + value
 
 
-def rows_kernel(total, which, col_at, jobs, outs, first_ref, cols_ref, spread_ref, *refs):
+def hold_kernel(cols_ref, after_ref, out_ref):
+    out_ref[...] = cols_ref[...]
+
+
+def rows_kernel(total, which, ats, jobs, outs, first_ref, spread_ref, *refs):
     refs = list(refs)
     news = refs[len(refs) - outs :]
+    columns, refs = refs[: len(ats)], refs[len(ats) :]
     for (place, count, summed), new_ref in zip(jobs, news):
         rows, refs = refs[:count], refs[count:]
         old_ref = refs.pop(0) if summed else None
         row_first, col_first = first_ref[place : place + 1, :], first_ref[which : which + 1, :]
-        found = matcher(spread_ref, place, row_first, cols_ref, col_first, col_at)
-        for tile, value in term(rows, cols_ref, total, found):
+        works = []
+        for cols_ref, at in zip(columns, ats):
+            found = matcher(spread_ref, place, row_first, cols_ref, col_first, at)
+            works.append(term(rows, cols_ref, total, found))
+        for values in zip(*works):
+            tile = values[0][0]
+            value = sum(x for _, x in values)
             if old_ref is not None:
                 value = old_ref[tile, :].astype(F32) + value
             new_ref[tile, :] = value.astype(new_ref.dtype)
 
 
 def final_kernel(features_ref, raw_ref, grad_ref, extra_ref, raw_grad_ref, partial_ref):
-    raw = raw_ref[...]
-    grad = grad_ref[...] + extra_ref[...].astype(F32)
-    scale = lax.rsqrt(jnp.sum(raw * raw, axis=1, keepdims=True) + 1e-06)
-    unit = raw * scale
-    along = jnp.sum(unit * grad, axis=1, keepdims=True)
-    raw_grad_ref[...] = ((grad - unit * along) * scale).astype(BF16)
-    partial_ref[...] = lax.dot_general(
-        features_ref[...], raw_grad_ref[...], BOTH_FIRST, preferred_element_type=F32
-    ).astype(BF16)
+    summed = None
+    for at in range(0, ROWS, FINAL_TILE):
+        tile = slice(at, at + FINAL_TILE)
+        raw = raw_ref[tile, :]
+        grad = grad_ref[tile, :] + extra_ref[tile, :].astype(F32)
+        scale = lax.rsqrt(jnp.sum(raw * raw, axis=1, keepdims=True) + 1e-06)
+        unit = raw * scale
+        along = jnp.sum(unit * grad, axis=1, keepdims=True)
+        raw_grad = ((grad - unit * along) * scale).astype(BF16)
+        raw_grad_ref[tile, :] = raw_grad
+        value = lax.dot_general(
+            features_ref[tile, :], raw_grad, BOTH_FIRST, preferred_element_type=F32
+        )
+        summed = value if summed is None else summed + value
+    partial_ref[...] = summed.astype(BF16)
 
 
 def feature_kernel(raw_grad_ref, head_ref, out_ref):
@@ -282,21 +299,20 @@
     )(first_ids, *mine, *other, grad)
     near_cross = [onward(x) for x in other[:-1] + [again]]
     far_same = [onward(x) for x in near_same]
-    far_cross = [onward(x) for x in near_cross]
-
-    def on_rows(which, at, cols, jobs, outs, passed=None, after=()):
+
+    def on_rows(which, ats, cols, jobs, outs, passed=None, after=()):
         given, plan = [], []
         for rows, old in jobs:
             plan.append((0 if rows is mine else 1, len(rows), old is not None))
             given += list(rows) + ([] if old is None else [old])
         tied = [] if passed is None else [passed]
         return call(
-            functools.partial(rows_kernel, total, which, at, tuple(plan), len(outs) + len(tied)),
+            functools.partial(rows_kernel, total, which, tuple(ats), tuple(plan), len(outs) + len(tied)),
             tuple(outs) + tuple(shape(x.shape, x.dtype) for x in tied),
-            [VMEM] + [VMEM] * (2 + len(given)) + [ANY] * (len(tied) + len(after)),
-            len(jobs) * pair * (cols.shape[0] - CODE) // ROWS,
-            {3 + len(given): len(outs)} if tied else {},
-        )(first_ids, cols, spread, *given, *tied, *after)
+            [VMEM] * (2 + len(cols) + len(given)) + [ANY] * (len(tied) + len(after)),
+            len(jobs) * pair * sum(x.shape[0] - CODE for x in cols) // ROWS,
+            {2 + len(cols) + len(given): len(outs)} if tied else {},
+        )(first_ids, spread, *cols, *given, *tied, *after)
 
     theirs = None
     near = [(2, k * ROWS // len(near_same), x) for k, x in enumerate(near_same)]
@@ -304,19 +320,24 @@
     for k, (which, at, cols) in enumerate(near):
         after = [x for _, _, x in near[k + 1 : k + 2]] if k >= TIES else []
         theirs, grad = on_rows(
-            which, at, cols, [(other, theirs), (mine, grad)], [full, full], after=after
-        )
-    for k, cols in enumerate(far_same):
-        grad, theirs = on_rows(4, k * ROWS // len(far_same), cols, [(mine, grad)], [full], theirs)
+            which, [at], [cols], [(other, theirs), (mine, grad)], [full, full], after=after
+        )
+        if k == len(near_same) - 1:
+            last = call(hold_kernel, shape(near_cross[-1].shape, BF16), [VMEM, ANY], 0)(
+                near_cross[-1], grad
+            )
+            far_cross = [onward(x) for x in near_cross[:-1] + [last]]
+    ats = [k * ROWS // len(far_same) for k in range(len(far_same))]
+    grad, theirs = on_rows(4, ats, far_same, [(mine, grad)], [full], theirs)
     for k, cols in enumerate(far_cross[:-1]):
         theirs, grad = on_rows(
-            5, k * ROWS // len(far_cross), cols, [(other, theirs), (mine, grad)], [full, full]
+            5, [k * ROWS // len(far_cross)], [cols], [(other, theirs), (mine, grad)], [full, full]
         )
     last_at = ROWS - ROWS // len(far_cross)
     cols = far_cross[-1]
-    (theirs,) = on_rows(5, last_at, cols, [(other, theirs)], [shape((ROWS, E), BF16)])
+    (theirs,) = on_rows(5, [last_at], [cols], [(other, theirs)], [shape((ROWS, E), BF16)])
     extra = across_chip(theirs)
-    (grad,) = on_rows(5, last_at, cols, [(mine, grad)], [full])
+    (grad,) = on_rows(5, [last_at], [cols], [(mine, grad)], [full])
 
     raw_grad, partial = call(
         final_kernel,

time: 66.7 us -> 66.7 us (level)
    all_to_all x1, starting transfers between devices: 3.72 us -> 5.44 us  [per_device(): parts = lax.all_to_all(partial.reshape(count, -1, E), 'batch', 0, 0)]
    ppermute x8, starting transfers between devices: 21.3 us -> 19.8 us  [onward(): return lax.ppermute(x, 'batch', hops)]
where the time goes in v6:
time: 66.7 us; the launch traced here: 66.4 us
  starting transfers between devices  26.9 us (40%)
  Pallas kernels  23.5 us (35%)
  waiting for transfers between devices  12.4 us (19%)
  local copies, waits for them, and re-layouts  2.08 us (3%)
  between operations  0.83 us (1%)
  other arithmetic  0.74 us (1%)
    ppermute x8, starting transfers between devices, onward(): return lax.ppermute(x, 'batch', hops)  19.8 us
    pallas_call x8, Pallas kernels, on_rows(): call(functools.partial(rows_kernel, total, which, tuple(ats), tuple(plan)...  12.5 us
    all_to_all x1, waiting for transfers between devices, per_device(): parts = lax.all_to_all(partial.reshape(count, -1, E), 'batch', 0, 0)  11.5 us
    all_to_all x1, starting transfers between devices, per_device(): parts = lax.all_to_all(partial.reshape(count, -1, E), 'batch', 0, 0)  5.44 us
    pallas_call x1, Pallas kernels, embed(): pl.pallas_call(functools.partial(embed_kernel, cuts), out_shape=outs, in_...  3.79 us
    pallas_call x1, Pallas kernels, per_device(): call(feature_kernel, shape((ROWS, features.shape[1]), BF16), [VMEM] * 2,...  2.06 us
    pallas_call x1, Pallas kernels, per_device(): call(final_kernel, (shape((ROWS, E), BF16), shape((features.shape[1], E),...  2.05 us
    unnamed x14, local copies, waits for them, and re-layouts  1.93 us
  transfers between devices with their start and end apart: 12, of which 2 were waited for; matrix products, arithmetic and copies ran while one was open for 0% of the time, Pallas kernels for 25%

profile of v6, /device:TPU:1, one launch (start us, length us, event | category | flops | bytes accessed | tf_op | source)
XLA Modules:
  0.0 66.4 jit_solution(17584696026416380919)
XLA Ops:
  0.6 3.8 %shard_map.50 = (f32[1024,256]{1,0:T(8,128)}, bf16[528,256]{1,0:T(8,128)(2,1)}, bf16[528,256]{1,0:T(8,128)(2,1)}) custom-call(bf16[1024,1024]{1,0:T(8,128)(2,1)} %features_ref.3, bf16[1024,256]{1,0:T(8,128)(2,1)} %head_ref.3, s32[8,128]{1,0:T(8,128)} %bitcast.8), custom_call_target="tpu_custom_call" | custom-call | flops 536870912 | bytes 4194304 | tf_op jit(solution)/shard_map/pallas_call | solution.py:100
  4.4 1.5 %collective-permute-start = (bf16[528,256]{1,0:T(8,128)(2,1)}, bf16[528,256]{1,0:T(8,128)(2,1)S(1)}, u32[]{:S(2)}, u32[]{:S(2)}) collective-permute-start(bf16[528,256]{1,0:T(8,128)(2,1)} %get-tuple-element.23.refs_0_.refs_3_.refs_4_.refs_2_.refs_1_), channel_id=1, source_target_pairs={{0,1},{1,0},{2,3},{3,2},{4,5},{5,4},{6,7},{7,6},{8,9},{9,8},{10,11... | collective-permute-start | bytes 811016 | tf_op jit(solution)/shard_map/ppermute | solution.py:256
  5.9 0.1 collective-permute-start.1
  6.0 8.5 %collective-permute-start.4 = (bf16[528,256]{1,0:T(8,128)(2,1)}, bf16[528,256]{1,0:T(8,128)(2,1)S(1)}, u32[]{:S(2)}, u32[]{:S(2)}) collective-permute-start(bf16[528,256]{1,0:T(8,128)(2,1)} %get-tuple-element.23.refs_0_.refs_3_.refs_4_.refs_2_.refs_1_), channel_id=1, source_target_pairs={{0,2},{1,127},{2,4},{3,1},{4,6},{5,3},{6,8},{7,5},{8,10},{9,7},{10... | collective-permute-start | bytes 811016 | tf_op jit(solution)/shard_map/ppermute | solution.py:260
  14.5 0.1 collective-permute-start.3
  14.6 0.1 stack.29
  14.7 0.0 collective-permute-done.refs_2_.refs_1_
  14.7 1.1 %collective-permute-start.5 = (bf16[528,256]{1,0:T(8,128)(2,1)S(1)}, bf16[528,256]{1,0:T(8,128)(2,1)S(1)}, u32[]{:S(2)}, u32[]{:S(2)}) collective-permute-start(bf16[528,256]{1,0:T(8,128)(2,1)S(1)} %collective-permute-done.refs_2_.refs_1_), channel_id=1, source_target_pairs={{0,2},{1,127},{2,4},{3,1},{4,6},{5,3},{6,8},{7,5},{8,10},{9,7},{10... | collective-permute-start | bytes 811016 | tf_op jit(solution)/shard_map/ppermute | solution.py:260
  15.8 0.0 copy-start
  15.8 1.0 %copy-done = bf16[528,256]{1,0:T(8,128)(2,1)S(1)} copy-done((bf16[528,256]{1,0:T(8,128)(2,1)S(1)}, bf16[528,256]{1,0:T(8,128)(2,1)}, u32[]{:S(2)}) %copy-start) | copy-done | bytes 270360
  16.8 0.0 copy-start.2
  16.8 1.0 %copy-done.2 = bf16[528,256]{1,0:T(8,128)(2,1)S(1)} copy-done((bf16[528,256]{1,0:T(8,128)(2,1)S(1)}, bf16[528,256]{1,0:T(8,128)(2,1)}, u32[]{:S(2)}) %copy-start.2) | copy-done | bytes 270360
  17.7 1.4 %shard_map.51.refs_4_ = f32[1024,256]{1,0:T(8,128)S(1)} custom-call(bf16[528,256]{1,0:T(8,128)(2,1)S(1)} %copy-done, bf16[528,256]{1,0:T(8,128)(2,1)S(1)} %copy-done.2), custom_call_target="tpu_custom_call" | custom-call | flops 225485776 | bytes 4194304 | tf_op jit(solution)/shard_map/pallas_call | solution.py:293
  19.1 0.0 collective-permute-done.1.refs_3_.refs_2_
  19.1 0.1 broadcast_in_dim.2.first_ref
  19.2 1.6 %shard_map.52 = (f32[1024,256]{1,0:T(8,128)S(1)}, f32[2048,128]{1,0:T(8,128)S(1)}, bf16[528,256]{1,0:T(8,128)(2,1)S(1)}) custom-call(f32[8,128]{1,0:T(8,128)S(1)} %broadcast_in_dim.2.first_ref, bf16[528,256]{1,0:T(8,128)(2,1)S(1)} %copy-done, bf16[528,256]{1,0:T(8,128)(2,1)S(1)} %copy-done.2, bf16[528,256]{1,0:T(8,128)(2,1)S(1)} %collective-permute-done.refs_2_.refs_1_, ...), custom_call_target="tpu_custom_call" | custom-call | flops 225485776 | bytes 4194304 | tf_op jit(solution)/shard_map/pallas_call | solution.py:294
  20.9 0.2 collective-permute-start.2
  21.0 0.0 collective-permute-done.4.refs_0_
  21.0 4.4 %collective-permute-start.8 = (bf16[528,256]{1,0:T(8,128)(2,1)S(1)}, bf16[528,256]{1,0:T(8,128)(2,1)S(1)}, u32[]{:S(2)}, u32[]{:S(2)}) collective-permute-start(bf16[528,256]{1,0:T(8,128)(2,1)S(1)} %collective-permute-done.4.refs_0_), channel_id=1, source_target_pairs={{0,2},{1,127},{2,4},{3,1},{4,6},{5,3},{6,8},{7,5},{8,10},{9,7},{10... | collective-permute-start | bytes 811016 | tf_op jit(solution)/shard_map/ppermute | solution.py:260
  25.5 0.0 collective-permute-done.3.refs_0_
  25.5 2.9 %collective-permute-start.9 = (bf16[528,256]{1,0:T(8,128)(2,1)S(1)}, bf16[528,256]{1,0:T(8,128)(2,1)S(1)}, u32[]{:S(2)}, u32[]{:S(2)}) collective-permute-start(bf16[528,256]{1,0:T(8,128)(2,1)S(1)} %collective-permute-done.3.refs_0_), channel_id=1, source_target_pairs={{0,2},{1,127},{2,4},{3,1},{4,6},{5,3},{6,8},{7,5},{8,10},{9,7},{10... | collective-permute-start | bytes 811016 | tf_op jit(solution)/shard_map/ppermute | solution.py:260
  28.4 1.6 %shard_map.53 = (f32[1024,256]{1,0:T(8,128)S(1)}, f32[1024,256]{1,0:T(8,128)S(1)}) custom-call(f32[8,128]{1,0:T(8,128)S(1)} %broadcast_in_dim.2.first_ref, f32[2048,128]{1,0:T(8,128)S(1)} %get-tuple-element.25.spread_ref, bf16[528,256]{1,0:T(8,128)(2,1)S(1)} %collective-permute-done.4.refs_0_, bf16[528,256]{1,0:T(8,128)(2,1)S(1)} %collective-permute-done.refs_2_.refs_1_, ...), custom_call_target="tpu_custom_call" | custom-call | flops 751619264 | bytes 4194304 | tf_op jit(solution)/shard_map/pallas_call | solution.py:309
  30.0 0.0 collective-permute-done.5.refs_7_.refs_0_
  30.0 1.2 %collective-permute-start.7 = (bf16[528,256]{1,0:T(8,128)(2,1)S(1)}, bf16[528,256]{1,0:T(8,128)(2,1)S(1)}, u32[]{:S(2)}, u32[]{:S(2)}) collective-permute-start(bf16[528,256]{1,0:T(8,128)(2,1)S(1)} %collective-permute-done.5.refs_7_.refs_0_), channel_id=1, source_target_pairs={{0,2},{1,127},{2,4},{3,1},{4,6},{5,3},{6,8},{7,5},{8,10},{9,7},{10... | collective-permute-start | bytes 811016 | tf_op jit(solution)/shard_map/ppermute | solution.py:260
  31.3 0.0 copy-start.1
  31.3 0.0 copy-start.3
  31.3 1.8 %shard_map.54 = (f32[1024,256]{1,0:T(8,128)S(1)}, f32[1024,256]{1,0:T(8,128)S(1)}) custom-call(f32[8,128]{1,0:T(8,128)S(1)} %broadcast_in_dim.2.first_ref, f32[2048,128]{1,0:T(8,128)S(1)} %get-tuple-element.25.spread_ref, bf16[528,256]{1,0:T(8,128)(2,1)S(1)} %collective-permute-done.3.refs_0_, bf16[528,256]{1,0:T(8,128)(2,1)S(1)} %collective-permute-done.refs_2_.refs_1_, ...), custom_call_target="tpu_custom_call" | custom-call | flops 751619264 | bytes 4194304 | tf_op jit(solution)/shard_map/pallas_call | solution.py:309
  33.0 0.0 collective-permute-done.2.cols_ref.refs_7_.refs_0_
  33.1 1.4 %collective-permute-start.6 = (bf16[528,256]{1,0:T(8,128)(2,1)S(1)}, bf16[528,256]{1,0:T(8,128)(2,1)S(1)}, u32[]{:S(2)}, u32[]{:S(2)}) collective-permute-start(bf16[528,256]{1,0:T(8,128)(2,1)S(1)} %shard_map.55), channel_id=1, source_target_pairs={{0,2},{1,127},{2,4},{3,1},{4,6},{5,3},{6,8},{7,5},{8,10},{9,7},{10... | collective-permute-start | bytes 811016 | tf_op jit(solution)/shard_map/ppermute | solution.py:260
  34.4 0.0 copy-done.1
  34.4 0.0 copy-done.3
  34.4 1.8 %shard_map.56 = (f32[1024,256]{1,0:T(8,128)S(1)}, f32[1024,256]{1,0:T(8,128)S(1)}) custom-call(f32[8,128]{1,0:T(8,128)S(1)} %broadcast_in_dim.2.first_ref, f32[2048,128]{1,0:T(8,128)S(1)} %get-tuple-element.25.spread_ref, bf16[528,256]{1,0:T(8,128)(2,1)S(1)} %collective-permute-done.5.refs_7_.refs_0_, ...), custom_call_target="tpu_custom_call" | custom-call | flops 751619264 | bytes 4194304 | tf_op jit(solution)/shard_map/pallas_call | solution.py:309
  36.2 1.8 %shard_map.57 = (f32[1024,256]{1,0:T(8,128)S(1)}, f32[1024,256]{1,0:T(8,128)S(1)}) custom-call(f32[8,128]{1,0:T(8,128)S(1)} %broadcast_in_dim.2.first_ref, f32[2048,128]{1,0:T(8,128)S(1)} %get-tuple-element.25.spread_ref, bf16[528,256]{1,0:T(8,128)(2,1)S(1)} %collective-permute-done.2.cols_ref.refs_7_.refs_0_, ...), custom_call_target="tpu_custom_call" | custom-call | flops 751619264 | bytes 4194304 | tf_op jit(solution)/shard_map/pallas_call | solution.py:309
  38.0 0.0 collective-permute-done.8.refs_0_
  38.0 0.0 collective-permute-done.9.refs_1_
  38.0 1.8 %shard_map.58 = (f32[1024,256]{1,0:T(8,128)S(1)}, f32[1024,256]{1,0:T(8,128)S(1)}) custom-call(f32[8,128]{1,0:T(8,128)S(1)} %broadcast_in_dim.2.first_ref, f32[2048,128]{1,0:T(8,128)S(1)} %get-tuple-element.25.spread_ref, bf16[528,256]{1,0:T(8,128)(2,1)S(1)} %collective-permute-done.8.refs_0_, ...), custom_call_target="tpu_custom_call", output_to_operand_aliasing={{1}: (7, {})} | custom-call | flops 751619264 | bytes 4194304 | tf_op jit(solution)/shard_map/pallas_call | solution.py:309
  39.8 0.0 collective-permute-done.7.refs_0_
  39.8 1.7 %shard_map.59 = (f32[1024,256]{1,0:T(8,128)S(1)}, f32[1024,256]{1,0:T(8,128)S(1)}) custom-call(f32[8,128]{1,0:T(8,128)S(1)} %broadcast_in_dim.2.first_ref, f32[2048,128]{1,0:T(8,128)S(1)} %get-tuple-element.25.spread_ref, bf16[528,256]{1,0:T(8,128)(2,1)S(1)} %collective-permute-done.7.refs_0_, bf16[528,256]{1,0:T(8,128)(2,1)S(1)} %collective-permute-done.refs_2_.refs_1_, ...), custom_call_target="tpu_custom_call" | custom-call | flops 751619264 | bytes 4194304 | tf_op jit(solution)/shard_map/pallas_call | solution.py:309
  41.6 0.0 collective-permute-done.6.refs_0_
  41.6 1.0 %shard_map.61 = bf16[1024,256]{1,0:T(8,128)(2,1)S(1)} custom-call(f32[8,128]{1,0:T(8,128)S(1)} %broadcast_in_dim.2.first_ref, f32[2048,128]{1,0:T(8,128)S(1)} %get-tuple-element.25.spread_ref, bf16[528,256]{1,0:T(8,128)(2,1)S(1)} %collective-permute-done.6.refs_0_, bf16[528,256]{1,0:T(8,128)(2,1)S(1)} %collective-permute-done.refs_2_.refs_1_, ...), custom_call_target="tpu_custom_call" | custom-call | flops 375809632 | bytes 4194304 | tf_op jit(solution)/shard_map/pallas_call | solution.py:309
  42.6 0.0 copy-start.4
  42.6 0.0 copy-start.6
  42.6 0.1 collective-permute-start.10
  42.7 1.0 %shard_map.60.grad_ref = f32[1024,256]{1,0:T(8,128)S(1)} custom-call(f32[8,128]{1,0:T(8,128)S(1)} %broadcast_in_dim.2.first_ref, f32[2048,128]{1,0:T(8,128)S(1)} %get-tuple-element.25.spread_ref, bf16[528,256]{1,0:T(8,128)(2,1)S(1)} %collective-permute-done.6.refs_0_, bf16[528,256]{1,0:T(8,128)(2,1)S(1)} %copy-done.1, bf16[528,256]{1,0:T(8,128)(2,1)S(1)} %copy-done.3, ...), custom_call_target="tpu_custom_call" | custom-call | flops 375809632 | bytes 4194304 | tf_op jit(solution)/shard_map/pallas_call | solution.py:309
  43.7 0.9 %collective-permute-done.10.extra_ref = bf16[1024,256]{1,0:T(8,128)(2,1)S(1)} collective-permute-done((bf16[1024,256]{1,0:T(8,128)(2,1)S(1)}, bf16[1024,256]{1,0:T(8,128)(2,1)S(1)}, u32[]{:S(2)}, u32[]{:S(2)}) %collective-permute-start.10) | collective-permute-done | bytes 524320 | tf_op jit(solution)/shard_map/ppermute | solution.py:256
  44.6 0.0 copy-done.4
  44.6 0.0 copy-done.6
  44.6 0.0 copy-start.5
  44.6 2.0 %shard_map.62 = (bf16[1024,256]{1,0:T(8,128)(2,1)S(1)}, bf16[1024,256]{1,0:T(8,128)(2,1)}) custom-call(bf16[1024,1024]{1,0:T(8,128)(2,1)S(1)} %copy-done.4, f32[1024,256]{1,0:T(8,128)S(1)} %copy-done.6, f32[1024,256]{1,0:T(8,128)S(1)} %shard_map.60.grad_ref, bf16[1024,256]{1,0:T(8,128)(2,1)S(1)} %collective-permute-done.10.extra_ref), custom_call_target="tpu_custom_call" | custom-call | flops 375809632 | bytes 4194304 | tf_op jit(solution)/shard_map/pallas_call | solution.py:342
  46.7 5.4 %all-to-all-start = ((bf16[128,8,256]{2,1,0:T(8,128)(2,1)}), bf16[128,8,256]{2,1,0:T(8,128)(2,1)S(1)}, u32[]{:S(2)}, u32[]{:S(2)}) async-start(bf16[128,8,256]{2,1,0:T(8,128)(2,1)} %bitcast.7), calls=%async_computation | async-start | bytes 1048576 | tf_op jit(solution)/shard_map/all_to_all | solution.py:348
  52.1 0.0 copy-done.5
  52.1 2.1 %shard_map.63 = bf16[1024,1024]{1,0:T(8,128)(2,1)} custom-call(bf16[1024,256]{1,0:T(8,128)(2,1)S(1)} %get-tuple-element.40.raw_grad_ref, bf16[1024,256]{1,0:T(8,128)(2,1)S(1)} %copy-done.5), custom_call_target="tpu_custom_call" | custom-call | flops 375809632 | bytes 4194304 | tf_op jit(solution)/shard_map/pallas_call | solution.py:349
  54.2 11.5 %all-to-all-done = bf16[128,8,256]{2,1,0:T(8,128)(2,1)S(1)} async-done(((bf16[128,8,256]{2,1,0:T(8,128)(2,1)}), bf16[128,8,256]{2,1,0:T(8,128)(2,1)S(1)}, u32[]{:S(2)}, u32[]{:S(2)}) %all-to-all-start) | async-done | bytes 524320 | tf_op jit(solution)/shard_map/all_to_all | solution.py:348
  65.7 0.7 %convert_reduce_fusion = f32[8,256]{1,0:T(8,128)} fusion(bf16[128,8,256]{2,1,0:T(8,128)(2,1)S(1)} %all-to-all-done), kind=kLoop, calls=%fused_computation | loop fusion | flops 522240 | bytes 532480 | tf_op jit(solution)/shard_map/reduce_sum | solution.py:352
  (2 shorter events, 0.0 us)
Async XLA Ops:
  4.4 10.3 %collective-permute-start = (bf16[528,256]{1,0:T(8,128)(2,1)}, bf16[528,256]{1,0:T(8,128)(2,1)S(1)}, u32[]{:S(2)}, u32[]{:S(2)}) collective-permute-start(bf16[528,256]{1,0:T(8,128)(2,1)} %get-tuple-element.23.refs_0_.refs_3_.refs_4_.refs_2_.refs_1_), channel_id=1, source_target_pairs={{0,1},{1,0},{2,3},{3,2},{4,5},{5,4},{6,7},{7,6},{8,9},{9,8},{10,11... | collective-permute-start | bytes 811016 | tf_op jit(solution)/shard_map/ppermute | solution.py:256
  5.9 13.2 %collective-permute-start.1 = (bf16[528,256]{1,0:T(8,128)(2,1)}, bf16[528,256]{1,0:T(8,128)(2,1)S(1)}, u32[]{:S(2)}, u32[]{:S(2)}) collective-permute-start(bf16[528,256]{1,0:T(8,128)(2,1)} %get-tuple-element.24.refs_1_.refs_4_.refs_5_.refs_3_.refs_2_), channel_id=1, source_target_pairs={{0,1},{1,0},{2,3},{3,2},{4,5},{5,4},{6,7},{7,6},{8,9},{9,8},{10,11... | collective-permute-start | bytes 811016 | tf_op jit(solution)/shard_map/ppermute | solution.py:256
  6.0 15.0 %collective-permute-start.4 = (bf16[528,256]{1,0:T(8,128)(2,1)}, bf16[528,256]{1,0:T(8,128)(2,1)S(1)}, u32[]{:S(2)}, u32[]{:S(2)}) collective-permute-start(bf16[528,256]{1,0:T(8,128)(2,1)} %get-tuple-element.23.refs_0_.refs_3_.refs_4_.refs_2_.refs_1_), channel_id=1, source_target_pairs={{0,2},{1,127},{2,4},{3,1},{4,6},{5,3},{6,8},{7,5},{8,10},{9,7},{10... | collective-permute-start | bytes 811016 | tf_op jit(solution)/shard_map/ppermute | solution.py:260
  14.5 11.0 %collective-permute-start.3 = (bf16[528,256]{1,0:T(8,128)(2,1)}, bf16[528,256]{1,0:T(8,128)(2,1)S(1)}, u32[]{:S(2)}, u32[]{:S(2)}) collective-permute-start(bf16[528,256]{1,0:T(8,128)(2,1)} %get-tuple-element.24.refs_1_.refs_4_.refs_5_.refs_3_.refs_2_), channel_id=1, source_target_pairs={{0,2},{1,127},{2,4},{3,1},{4,6},{5,3},{6,8},{7,5},{8,10},{9,7},{10... | collective-permute-start | bytes 811016 | tf_op jit(solution)/shard_map/ppermute | solution.py:260
  14.7 15.3 %collective-permute-start.5 = (bf16[528,256]{1,0:T(8,128)(2,1)S(1)}, bf16[528,256]{1,0:T(8,128)(2,1)S(1)}, u32[]{:S(2)}, u32[]{:S(2)}) collective-permute-start(bf16[528,256]{1,0:T(8,128)(2,1)S(1)} %collective-permute-done.refs_2_.refs_1_), channel_id=1, source_target_pairs={{0,2},{1,127},{2,4},{3,1},{4,6},{5,3},{6,8},{7,5},{8,10},{9,7},{10... | collective-permute-start | bytes 811016 | tf_op jit(solution)/shard_map/ppermute | solution.py:260
  15.8 1.0 %copy-start = (bf16[528,256]{1,0:T(8,128)(2,1)S(1)}, bf16[528,256]{1,0:T(8,128)(2,1)}, u32[]{:S(2)}) copy-start(bf16[528,256]{1,0:T(8,128)(2,1)} %get-tuple-element.23.refs_0_.refs_3_.refs_4_.refs_2_.refs_1_) | copy-start | bytes 811012
  16.8 1.0 %copy-start.2 = (bf16[528,256]{1,0:T(8,128)(2,1)S(1)}, bf16[528,256]{1,0:T(8,128)(2,1)}, u32[]{:S(2)}) copy-start(bf16[528,256]{1,0:T(8,128)(2,1)} %get-tuple-element.24.refs_1_.refs_4_.refs_5_.refs_3_.refs_2_) | copy-start | bytes 811012
  20.9 12.2 %collective-permute-start.2 = (bf16[528,256]{1,0:T(8,128)(2,1)S(1)}, bf16[528,256]{1,0:T(8,128)(2,1)S(1)}, u32[]{:S(2)}, u32[]{:S(2)}) collective-permute-start(bf16[528,256]{1,0:T(8,128)(2,1)S(1)} %get-tuple-element.26), channel_id=1, source_target_pairs={{0,2},{1,127},{2,4},{3,1},{4,6},{5,3},{6,8},{7,5},{8,10},{9,7},{10... | collective-permute-start | bytes 811016 | tf_op jit(solution)/shard_map/ppermute | solution.py:260
  21.0 16.9 %collective-permute-start.8 = (bf16[528,256]{1,0:T(8,128)(2,1)S(1)}, bf16[528,256]{1,0:T(8,128)(2,1)S(1)}, u32[]{:S(2)}, u32[]{:S(2)}) collective-permute-start(bf16[528,256]{1,0:T(8,128)(2,1)S(1)} %collective-permute-done.4.refs_0_), channel_id=1, source_target_pairs={{0,2},{1,127},{2,4},{3,1},{4,6},{5,3},{6,8},{7,5},{8,10},{9,7},{10... | collective-permute-start | bytes 811016 | tf_op jit(solution)/shard_map/ppermute | solution.py:260
  25.5 12.5 %collective-permute-start.9 = (bf16[528,256]{1,0:T(8,128)(2,1)S(1)}, bf16[528,256]{1,0:T(8,128)(2,1)S(1)}, u32[]{:S(2)}, u32[]{:S(2)}) collective-permute-start(bf16[528,256]{1,0:T(8,128)(2,1)S(1)} %collective-permute-done.3.refs_0_), channel_id=1, source_target_pairs={{0,2},{1,127},{2,4},{3,1},{4,6},{5,3},{6,8},{7,5},{8,10},{9,7},{10... | collective-permute-start | bytes 811016 | tf_op jit(solution)/shard_map/ppermute | solution.py:260
  30.0 9.8 %collective-permute-start.7 = (bf16[528,256]{1,0:T(8,128)(2,1)S(1)}, bf16[528,256]{1,0:T(8,128)(2,1)S(1)}, u32[]{:S(2)}, u32[]{:S(2)}) collective-permute-start(bf16[528,256]{1,0:T(8,128)(2,1)S(1)} %collective-permute-done.5.refs_7_.refs_0_), channel_id=1, source_target_pairs={{0,2},{1,127},{2,4},{3,1},{4,6},{5,3},{6,8},{7,5},{8,10},{9,7},{10... | collective-permute-start | bytes 811016 | tf_op jit(solution)/shard_map/ppermute | solution.py:260
  31.3 3.2 %copy-start.1 = (bf16[528,256]{1,0:T(8,128)(2,1)S(1)}, bf16[528,256]{1,0:T(8,128)(2,1)}, u32[]{:S(2)}) copy-start(bf16[528,256]{1,0:T(8,128)(2,1)} %get-tuple-element.23.refs_0_.refs_3_.refs_4_.refs_2_.refs_1_) | copy-start | bytes 811012
  31.3 3.2 %copy-start.3 = (bf16[528,256]{1,0:T(8,128)(2,1)S(1)}, bf16[528,256]{1,0:T(8,128)(2,1)}, u32[]{:S(2)}) copy-start(bf16[528,256]{1,0:T(8,128)(2,1)} %get-tuple-element.24.refs_1_.refs_4_.refs_5_.refs_3_.refs_2_) | copy-start | bytes 811012
  33.1 8.5 %collective-permute-start.6 = (bf16[528,256]{1,0:T(8,128)(2,1)S(1)}, bf16[528,256]{1,0:T(8,128)(2,1)S(1)}, u32[]{:S(2)}, u32[]{:S(2)}) collective-permute-start(bf16[528,256]{1,0:T(8,128)(2,1)S(1)} %shard_map.55), channel_id=1, source_target_pairs={{0,2},{1,127},{2,4},{3,1},{4,6},{5,3},{6,8},{7,5},{8,10},{9,7},{10... | collective-permute-start | bytes 811016 | tf_op jit(solution)/shard_map/ppermute | solution.py:260
  42.6 2.0 %copy-start.4 = (bf16[1024,1024]{1,0:T(8,128)(2,1)S(1)}, bf16[1024,1024]{1,0:T(8,128)(2,1)}, u32[]{:S(2)}) copy-start(bf16[1024,1024]{1,0:T(8,128)(2,1)} %features_ref.3) | copy-start | bytes 6291460
  42.6 2.0 %copy-start.6 = (f32[1024,256]{1,0:T(8,128)S(1)}, f32[1024,256]{1,0:T(8,128)}, u32[]{:S(2)}) copy-start(f32[1024,256]{1,0:T(8,128)} %get-tuple-element.22.raw_ref) | copy-start | bytes 3145732
  42.6 2.0 %collective-permute-start.10 = (bf16[1024,256]{1,0:T(8,128)(2,1)S(1)}, bf16[1024,256]{1,0:T(8,128)(2,1)S(1)}, u32[]{:S(2)}, u32[]{:S(2)}) collective-permute-start(bf16[1024,256]{1,0:T(8,128)(2,1)S(1)} %shard_map.61), channel_id=1, source_target_pairs={{0,1},{1,0},{2,3},{3,2},{4,5},{5,4},{6,7},{7,6},{8,9},{9,8},{10,11... | collective-permute-start | bytes 1572872 | tf_op jit(solution)/shard_map/ppermute | solution.py:256
  44.6 7.5 %copy-start.5 = (bf16[1024,256]{1,0:T(8,128)(2,1)S(1)}, bf16[1024,256]{1,0:T(8,128)(2,1)}, u32[]{:S(2)}) copy-start(bf16[1024,256]{1,0:T(8,128)(2,1)} %head_ref.3) | copy-start | bytes 1572868
  46.7 19.0 %all-to-all-start = ((bf16[128,8,256]{2,1,0:T(8,128)(2,1)}), bf16[128,8,256]{2,1,0:T(8,128)(2,1)S(1)}, u32[]{:S(2)}, u32[]{:S(2)}) async-start(bf16[128,8,256]{2,1,0:T(8,128)(2,1)} %bitcast.7), calls=%async_computation | async-start | bytes 1048576 | tf_op jit(solution)/shard_map/all_to_all | solution.py:348

commit v7 on v5

--- a/solution.py
+++ b/solution.py
@@ -10,7 +10,7 @@
 
 BF16, F32 = jnp.bfloat16, jnp.float32
 ROWS, E, CODE = 1024, 256, 16
-TILE = 256
+TILE = 512
 VMEM = pl.BlockSpec(memory_space=pltpu.VMEM)
 ANY = pl.BlockSpec(memory_space=pl.ANY)
 BOTH_LAST = (((1,), (1,)), ((), ()))

time: 66.7 us -> 66.7 us (level)
  no operation moved by 1% of the time
where the time goes in v7:
time: 66.7 us; the launch traced here: 66.4 us
  starting transfers between devices  27.1 us (41%)
  Pallas kernels  23.2 us (35%)
  waiting for transfers between devices  12.4 us (19%)
  local copies, waits for them, and re-layouts  2.08 us (3%)
  between operations  0.84 us (1%)
  other arithmetic  0.74 us (1%)
    ppermute x8, starting transfers between devices, onward(): return lax.ppermute(x, 'batch', hops)  21.3 us
    pallas_call x9, Pallas kernels, on_rows(): call(functools.partial(rows_kernel, total, which, at, tuple(plan), len(ou...  12.3 us
    all_to_all x1, waiting for transfers between devices, per_device(): parts = lax.all_to_all(partial.reshape(count, -1, E), 'batch', 0, 0)  11.5 us
    all_to_all x1, starting transfers between devices, per_device(): parts = lax.all_to_all(partial.reshape(count, -1, E), 'batch', 0, 0)  4.1 us
    pallas_call x1, Pallas kernels, embed(): pl.pallas_call(functools.partial(embed_kernel, cuts), out_shape=outs, in_...  3.79 us
    pallas_call x1, Pallas kernels, per_device(): call(feature_kernel, shape((ROWS, features.shape[1]), BF16), [VMEM] * 2,...  2.06 us
    pallas_call x1, Pallas kernels, per_device(): call(final_kernel, (shape((ROWS, E), BF16), shape((features.shape[1], E),...  2.04 us
    unnamed x14, local copies, waits for them, and re-layouts  1.93 us
  transfers between devices with their start and end apart: 12, of which 2 were waited for; matrix products, arithmetic and copies ran while one was open for 0% of the time, Pallas kernels for 25%

profile of v7, /device:TPU:1, one launch (start us, length us, event | category | flops | bytes accessed | tf_op | source)
XLA Modules:
  0.0 66.4 jit_solution(16330966859917381129)
XLA Ops:
  0.6 3.8 %shard_map.50 = (f32[1024,256]{1,0:T(8,128)}, bf16[528,256]{1,0:T(8,128)(2,1)}, bf16[528,256]{1,0:T(8,128)(2,1)}) custom-call(bf16[1024,1024]{1,0:T(8,128)(2,1)} %features_ref.3, bf16[1024,256]{1,0:T(8,128)(2,1)} %head_ref.3, s32[8,128]{1,0:T(8,128)} %bitcast.8), custom_call_target="tpu_custom_call" | custom-call | flops 536870912 | bytes 4194304 | tf_op jit(solution)/shard_map/pallas_call | solution.py:99
  4.4 1.5 %collective-permute-start = (bf16[528,256]{1,0:T(8,128)(2,1)}, bf16[528,256]{1,0:T(8,128)(2,1)S(1)}, u32[]{:S(2)}, u32[]{:S(2)}) collective-permute-start(bf16[528,256]{1,0:T(8,128)(2,1)} %get-tuple-element.25.refs_0_.refs_2_.refs_3_), channel_id=1, source_target_pairs={{0,1},{1,0},{2,3},{3,2},{4,5},{5,4},{6,7},{7,6},{8,9},{9,8},{10,11... | collective-permute-start | bytes 811016 | tf_op jit(solution)/shard_map/ppermute | solution.py:239
  5.9 0.1 collective-permute-start.1
  6.0 8.5 %collective-permute-start.8 = (bf16[528,256]{1,0:T(8,128)(2,1)}, bf16[528,256]{1,0:T(8,128)(2,1)S(1)}, u32[]{:S(2)}, u32[]{:S(2)}) collective-permute-start(bf16[528,256]{1,0:T(8,128)(2,1)} %get-tuple-element.25.refs_0_.refs_2_.refs_3_), channel_id=1, source_target_pairs={{0,2},{1,127},{2,4},{3,1},{4,6},{5,3},{6,8},{7,5},{8,10},{9,7},{10... | collective-permute-start | bytes 811016 | tf_op jit(solution)/shard_map/ppermute | solution.py:243
  14.5 0.1 collective-permute-start.6
  14.6 0.1 stack.29
  14.7 0.0 copy-start
  14.7 1.0 %copy-done = bf16[528,256]{1,0:T(8,128)(2,1)S(1)} copy-done((bf16[528,256]{1,0:T(8,128)(2,1)S(1)}, bf16[528,256]{1,0:T(8,128)(2,1)}, u32[]{:S(2)}) %copy-start) | copy-done | bytes 270360
  15.7 0.0 copy-start.2
  15.7 1.0 %copy-done.2 = bf16[528,256]{1,0:T(8,128)(2,1)S(1)} copy-done((bf16[528,256]{1,0:T(8,128)(2,1)S(1)}, bf16[528,256]{1,0:T(8,128)(2,1)}, u32[]{:S(2)}) %copy-start.2) | copy-done | bytes 270360
  16.6 1.4 %shard_map.51.refs_4_ = f32[1024,256]{1,0:T(8,128)S(1)} custom-call(bf16[528,256]{1,0:T(8,128)(2,1)S(1)} %copy-done, bf16[528,256]{1,0:T(8,128)(2,1)S(1)} %copy-done.2), custom_call_target="tpu_custom_call" | custom-call | flops 322122560 | bytes 4194304 | tf_op jit(solution)/shard_map/pallas_call | solution.py:276
  18.1 0.0 collective-permute-done.refs_2_.refs_0_
  18.1 0.1 collective-permute-start.4
  18.2 0.0 collective-permute-done.1.refs_3_.refs_1_
  18.2 0.1 broadcast_in_dim.2.first_ref
  18.2 1.6 %shard_map.52 = (f32[1024,256]{1,0:T(8,128)S(1)}, f32[2048,128]{1,0:T(8,128)S(1)}, bf16[528,256]{1,0:T(8,128)(2,1)S(1)}) custom-call(f32[8,128]{1,0:T(8,128)S(1)} %broadcast_in_dim.2.first_ref, bf16[528,256]{1,0:T(8,128)(2,1)S(1)} %copy-done, bf16[528,256]{1,0:T(8,128)(2,1)S(1)} %copy-done.2, bf16[528,256]{1,0:T(8,128)(2,1)S(1)} %collective-permute-done.refs_2_.refs_0_, ...), custom_call_target="tpu_custom_call" | custom-call | flops 322122560 | bytes 4194304 | tf_op jit(solution)/shard_map/pallas_call | solution.py:277
  19.9 0.1 collective-permute-start.2
  20.0 0.0 collective-permute-done.8.cols_ref
  20.0 5.5 %collective-permute-start.9 = (bf16[528,256]{1,0:T(8,128)(2,1)S(1)}, bf16[528,256]{1,0:T(8,128)(2,1)S(1)}, u32[]{:S(2)}, u32[]{:S(2)}) collective-permute-start(bf16[528,256]{1,0:T(8,128)(2,1)S(1)} %collective-permute-done.8.cols_ref), channel_id=1, source_target_pairs={{0,2},{1,127},{2,4},{3,1},{4,6},{5,3},{6,8},{7,5},{8,10},{9,7},{10... | collective-permute-start | bytes 811016 | tf_op jit(solution)/shard_map/ppermute | solution.py:243
  25.5 0.0 collective-permute-done.6.cols_ref
  25.5 2.9 %collective-permute-start.7 = (bf16[528,256]{1,0:T(8,128)(2,1)S(1)}, bf16[528,256]{1,0:T(8,128)(2,1)S(1)}, u32[]{:S(2)}, u32[]{:S(2)}) collective-permute-start(bf16[528,256]{1,0:T(8,128)(2,1)S(1)} %collective-permute-done.6.cols_ref), channel_id=1, source_target_pairs={{0,2},{1,127},{2,4},{3,1},{4,6},{5,3},{6,8},{7,5},{8,10},{9,7},{10... | collective-permute-start | bytes 811016 | tf_op jit(solution)/shard_map/ppermute | solution.py:243
  28.4 1.6 %shard_map.53 = (f32[1024,256]{1,0:T(8,128)S(1)}, f32[1024,256]{1,0:T(8,128)S(1)}) custom-call(f32[8,128]{1,0:T(8,128)S(1)} %broadcast_in_dim.2.first_ref, bf16[528,256]{1,0:T(8,128)(2,1)S(1)} %collective-permute-done.8.cols_ref, f32[2048,128]{1,0:T(8,128)S(1)} %get-tuple-element.28.spread_ref, bf16[528,256]{1,0:T(8,128)(2,1)S(1)} %collective-permute-done.refs_2_.refs_0_, ...), custom_call_target="tpu_custom_call" | custom-call | flops 1073741824 | bytes 4194304 | tf_op jit(solution)/shard_map/pallas_call | solution.py:293
  30.0 0.0 collective-permute-done.4.refs_6_.cols_ref
  30.0 1.2 %collective-permute-start.5 = (bf16[528,256]{1,0:T(8,128)(2,1)S(1)}, bf16[528,256]{1,0:T(8,128)(2,1)S(1)}, u32[]{:S(2)}, u32[]{:S(2)}) collective-permute-start(bf16[528,256]{1,0:T(8,128)(2,1)S(1)} %collective-permute-done.4.refs_6_.cols_ref), channel_id=1, source_target_pairs={{0,2},{1,127},{2,4},{3,1},{4,6},{5,3},{6,8},{7,5},{8,10},{9,7},{10... | collective-permute-start | bytes 811016 | tf_op jit(solution)/shard_map/ppermute | solution.py:243
  31.3 0.0 collective-permute-done.2.refs_6_.cols_ref
  31.3 2.9 %collective-permute-start.3 = (bf16[528,256]{1,0:T(8,128)(2,1)S(1)}, bf16[528,256]{1,0:T(8,128)(2,1)S(1)}, u32[]{:S(2)}, u32[]{:S(2)}) collective-permute-start(bf16[528,256]{1,0:T(8,128)(2,1)S(1)} %collective-permute-done.2.refs_6_.cols_ref), channel_id=1, source_target_pairs={{0,2},{1,127},{2,4},{3,1},{4,6},{5,3},{6,8},{7,5},{8,10},{9,7},{10... | collective-permute-start | bytes 811016 | tf_op jit(solution)/shard_map/ppermute | solution.py:243
  34.2 1.6 %shard_map.54 = (f32[1024,256]{1,0:T(8,128)S(1)}, f32[1024,256]{1,0:T(8,128)S(1)}) custom-call(f32[8,128]{1,0:T(8,128)S(1)} %broadcast_in_dim.2.first_ref, bf16[528,256]{1,0:T(8,128)(2,1)S(1)} %collective-permute-done.6.cols_ref, f32[2048,128]{1,0:T(8,128)S(1)} %get-tuple-element.28.spread_ref, bf16[528,256]{1,0:T(8,128)(2,1)S(1)} %collective-permute-done.refs_2_.refs_0_, ...), custom_call_target="tpu_custom_call" | custom-call | flops 1073741824 | bytes 4194304 | tf_op jit(solution)/shard_map/pallas_call | solution.py:293
  35.8 1.7 %shard_map.55 = (f32[1024,256]{1,0:T(8,128)S(1)}, f32[1024,256]{1,0:T(8,128)S(1)}) custom-call(f32[8,128]{1,0:T(8,128)S(1)} %broadcast_in_dim.2.first_ref, bf16[528,256]{1,0:T(8,128)(2,1)S(1)} %collective-permute-done.4.refs_6_.cols_ref, f32[2048,128]{1,0:T(8,128)S(1)} %get-tuple-element.28.spread_ref, ...), custom_call_target="tpu_custom_call" | custom-call | flops 1073741824 | bytes 4194304 | tf_op jit(solution)/shard_map/pallas_call | solution.py:293
  37.5 1.7 %shard_map.56 = (f32[1024,256]{1,0:T(8,128)S(1)}, f32[1024,256]{1,0:T(8,128)S(1)}) custom-call(f32[8,128]{1,0:T(8,128)S(1)} %broadcast_in_dim.2.first_ref, bf16[528,256]{1,0:T(8,128)(2,1)S(1)} %collective-permute-done.2.refs_6_.cols_ref, f32[2048,128]{1,0:T(8,128)S(1)} %get-tuple-element.28.spread_ref, ...), custom_call_target="tpu_custom_call" | custom-call | flops 1073741824 | bytes 4194304 | tf_op jit(solution)/shard_map/pallas_call | solution.py:293
  39.2 0.0 collective-permute-done.9.cols_ref
  39.2 1.0 %shard_map.57 = (f32[1024,256]{1,0:T(8,128)S(1)}, f32[1024,256]{1,0:T(8,128)S(1)}) custom-call(f32[8,128]{1,0:T(8,128)S(1)} %broadcast_in_dim.2.first_ref, bf16[528,256]{1,0:T(8,128)(2,1)S(1)} %collective-permute-done.9.cols_ref, f32[2048,128]{1,0:T(8,128)S(1)} %get-tuple-element.28.spread_ref, ...), custom_call_target="tpu_custom_call", output_to_operand_aliasing={{1}: (6, {})} | custom-call | flops 536870912 | bytes 4194304 | tf_op jit(solution)/shard_map/pallas_call | solution.py:293
  40.2 0.0 collective-permute-done.7.cols_ref
  40.2 1.0 %shard_map.58 = (f32[1024,256]{1,0:T(8,128)S(1)}, f32[1024,256]{1,0:T(8,128)S(1)}) custom-call(f32[8,128]{1,0:T(8,128)S(1)} %broadcast_in_dim.2.first_ref, bf16[528,256]{1,0:T(8,128)(2,1)S(1)} %collective-permute-done.7.cols_ref, f32[2048,128]{1,0:T(8,128)S(1)} %get-tuple-element.28.spread_ref, ...), custom_call_target="tpu_custom_call", output_to_operand_aliasing={{1}: (6, {})} | custom-call | flops 536870912 | bytes 4194304 | tf_op jit(solution)/shard_map/pallas_call | solution.py:293
  41.2 0.0 collective-permute-done.5.cols_ref
  41.2 1.7 %shard_map.59 = (f32[1024,256]{1,0:T(8,128)S(1)}, f32[1024,256]{1,0:T(8,128)S(1)}) custom-call(f32[8,128]{1,0:T(8,128)S(1)} %broadcast_in_dim.2.first_ref, bf16[528,256]{1,0:T(8,128)(2,1)S(1)} %collective-permute-done.5.cols_ref, f32[2048,128]{1,0:T(8,128)S(1)} %get-tuple-element.28.spread_ref, bf16[528,256]{1,0:T(8,128)(2,1)S(1)} %collective-permute-done.refs_2_.refs_0_, ...), custom_call_target="tpu_custom_call" | custom-call | flops 1073741824 | bytes 4194304 | tf_op jit(solution)/shard_map/pallas_call | solution.py:293
  42.9 0.0 copy-start.1
  42.9 0.0 copy-start.3
  42.9 0.0 collective-permute-done.3.cols_ref
  42.9 1.0 %shard_map.61 = bf16[1024,256]{1,0:T(8,128)(2,1)S(1)} custom-call(f32[8,128]{1,0:T(8,128)S(1)} %broadcast_in_dim.2.first_ref, bf16[528,256]{1,0:T(8,128)(2,1)S(1)} %collective-permute-done.3.cols_ref, f32[2048,128]{1,0:T(8,128)S(1)} %get-tuple-element.28.spread_ref, bf16[528,256]{1,0:T(8,128)(2,1)S(1)} %collective-permute-done.refs_2_.refs_0_, ...), custom_call_target="tpu_custom_call" | custom-call | flops 536870912 | bytes 4194304 | tf_op jit(solution)/shard_map/pallas_call | solution.py:293
  43.9 0.0 copy-start.4
  43.9 0.0 copy-start.6
  43.9 0.1 collective-permute-start.10
  44.0 0.0 copy-done.1
  44.0 0.0 copy-done.3
  44.1 1.0 %shard_map.60.grad_ref = f32[1024,256]{1,0:T(8,128)S(1)} custom-call(f32[8,128]{1,0:T(8,128)S(1)} %broadcast_in_dim.2.first_ref, bf16[528,256]{1,0:T(8,128)(2,1)S(1)} %collective-permute-done.3.cols_ref, f32[2048,128]{1,0:T(8,128)S(1)} %get-tuple-element.28.spread_ref, bf16[528,256]{1,0:T(8,128)(2,1)S(1)} %copy-done.1, bf16[528,256]{1,0:T(8,128)(2,1)S(1)} %copy-done.3, ...), custom_call_target="tpu_custom_call" | custom-call | flops 536870912 | bytes 4194304 | tf_op jit(solution)/shard_map/pallas_call | solution.py:293
  45.0 0.9 %collective-permute-done.10.extra_ref = bf16[1024,256]{1,0:T(8,128)(2,1)S(1)} collective-permute-done((bf16[1024,256]{1,0:T(8,128)(2,1)S(1)}, bf16[1024,256]{1,0:T(8,128)(2,1)S(1)}, u32[]{:S(2)}, u32[]{:S(2)}) %collective-permute-start.10) | collective-permute-done | bytes 524320 | tf_op jit(solution)/shard_map/ppermute | solution.py:239
  45.9 0.0 copy-done.4
  45.9 0.0 copy-done.6
  45.9 0.0 copy-start.5
  45.9 2.0 %shard_map.62 = (bf16[1024,256]{1,0:T(8,128)(2,1)S(1)}, bf16[1024,256]{1,0:T(8,128)(2,1)}) custom-call(bf16[1024,1024]{1,0:T(8,128)(2,1)S(1)} %copy-done.4, f32[1024,256]{1,0:T(8,128)S(1)} %copy-done.6, f32[1024,256]{1,0:T(8,128)S(1)} %shard_map.60.grad_ref, bf16[1024,256]{1,0:T(8,128)(2,1)S(1)} %collective-permute-done.10.extra_ref), custom_call_target="tpu_custom_call" | custom-call | flops 536870912 | bytes 4194304 | tf_op jit(solution)/shard_map/pallas_call | solution.py:321
  48.0 4.1 %all-to-all-start = ((bf16[128,8,256]{2,1,0:T(8,128)(2,1)}), bf16[128,8,256]{2,1,0:T(8,128)(2,1)S(1)}, u32[]{:S(2)}, u32[]{:S(2)}) async-start(bf16[128,8,256]{2,1,0:T(8,128)(2,1)} %bitcast.7), calls=%async_computation | async-start | bytes 1048576 | tf_op jit(solution)/shard_map/all_to_all | solution.py:327
  52.1 0.0 copy-done.5
  52.1 2.1 %shard_map.63 = bf16[1024,1024]{1,0:T(8,128)(2,1)} custom-call(bf16[1024,256]{1,0:T(8,128)(2,1)S(1)} %get-tuple-element.44.raw_grad_ref, bf16[1024,256]{1,0:T(8,128)(2,1)S(1)} %copy-done.5), custom_call_target="tpu_custom_call" | custom-call | flops 536870912 | bytes 4194304 | tf_op jit(solution)/shard_map/pallas_call | solution.py:328
  54.2 11.5 %all-to-all-done = bf16[128,8,256]{2,1,0:T(8,128)(2,1)S(1)} async-done(((bf16[128,8,256]{2,1,0:T(8,128)(2,1)}), bf16[128,8,256]{2,1,0:T(8,128)(2,1)S(1)}, u32[]{:S(2)}, u32[]{:S(2)}) %all-to-all-start) | async-done | bytes 524320 | tf_op jit(solution)/shard_map/all_to_all | solution.py:327
  65.7 0.7 %convert_reduce_fusion = f32[8,256]{1,0:T(8,128)} fusion(bf16[128,8,256]{2,1,0:T(8,128)(2,1)S(1)} %all-to-all-done), kind=kLoop, calls=%fused_computation | loop fusion | flops 522240 | bytes 532480 | tf_op jit(solution)/shard_map/reduce_sum | solution.py:331
  (1 shorter events, 0.0 us)
Async XLA Ops:
  4.4 13.6 %collective-permute-start = (bf16[528,256]{1,0:T(8,128)(2,1)}, bf16[528,256]{1,0:T(8,128)(2,1)S(1)}, u32[]{:S(2)}, u32[]{:S(2)}) collective-permute-start(bf16[528,256]{1,0:T(8,128)(2,1)} %get-tuple-element.25.refs_0_.refs_2_.refs_3_), channel_id=1, source_target_pairs={{0,1},{1,0},{2,3},{3,2},{4,5},{5,4},{6,7},{7,6},{8,9},{9,8},{10,11... | collective-permute-start | bytes 811016 | tf_op jit(solution)/shard_map/ppermute | solution.py:239
  5.9 12.2 %collective-permute-start.1 = (bf16[528,256]{1,0:T(8,128)(2,1)}, bf16[528,256]{1,0:T(8,128)(2,1)S(1)}, u32[]{:S(2)}, u32[]{:S(2)}) collective-permute-start(bf16[528,256]{1,0:T(8,128)(2,1)} %get-tuple-element.26.refs_1_.refs_3_.refs_4_), channel_id=1, source_target_pairs={{0,1},{1,0},{2,3},{3,2},{4,5},{5,4},{6,7},{7,6},{8,9},{9,8},{10,11... | collective-permute-start | bytes 811016 | tf_op jit(solution)/shard_map/ppermute | solution.py:239
  6.0 13.9 %collective-permute-start.8 = (bf16[528,256]{1,0:T(8,128)(2,1)}, bf16[528,256]{1,0:T(8,128)(2,1)S(1)}, u32[]{:S(2)}, u32[]{:S(2)}) collective-permute-start(bf16[528,256]{1,0:T(8,128)(2,1)} %get-tuple-element.25.refs_0_.refs_2_.refs_3_), channel_id=1, source_target_pairs={{0,2},{1,127},{2,4},{3,1},{4,6},{5,3},{6,8},{7,5},{8,10},{9,7},{10... | collective-permute-start | bytes 811016 | tf_op jit(solution)/shard_map/ppermute | solution.py:243
  14.5 11.0 %collective-permute-start.6 = (bf16[528,256]{1,0:T(8,128)(2,1)}, bf16[528,256]{1,0:T(8,128)(2,1)S(1)}, u32[]{:S(2)}, u32[]{:S(2)}) collective-permute-start(bf16[528,256]{1,0:T(8,128)(2,1)} %get-tuple-element.26.refs_1_.refs_3_.refs_4_), channel_id=1, source_target_pairs={{0,2},{1,127},{2,4},{3,1},{4,6},{5,3},{6,8},{7,5},{8,10},{9,7},{10... | collective-permute-start | bytes 811016 | tf_op jit(solution)/shard_map/ppermute | solution.py:243
  14.7 1.0 %copy-start = (bf16[528,256]{1,0:T(8,128)(2,1)S(1)}, bf16[528,256]{1,0:T(8,128)(2,1)}, u32[]{:S(2)}) copy-start(bf16[528,256]{1,0:T(8,128)(2,1)} %get-tuple-element.25.refs_0_.refs_2_.refs_3_) | copy-start | bytes 811012
  15.7 1.0 %copy-start.2 = (bf16[528,256]{1,0:T(8,128)(2,1)S(1)}, bf16[528,256]{1,0:T(8,128)(2,1)}, u32[]{:S(2)}) copy-start(bf16[528,256]{1,0:T(8,128)(2,1)} %get-tuple-element.26.refs_1_.refs_3_.refs_4_) | copy-start | bytes 811012
  18.1 11.9 %collective-permute-start.4 = (bf16[528,256]{1,0:T(8,128)(2,1)S(1)}, bf16[528,256]{1,0:T(8,128)(2,1)S(1)}, u32[]{:S(2)}, u32[]{:S(2)}) collective-permute-start(bf16[528,256]{1,0:T(8,128)(2,1)S(1)} %collective-permute-done.refs_2_.refs_0_), channel_id=1, source_target_pairs={{0,2},{1,127},{2,4},{3,1},{4,6},{5,3},{6,8},{7,5},{8,10},{9,7},{10... | collective-permute-start | bytes 811016 | tf_op jit(solution)/shard_map/ppermute | solution.py:243
  19.9 11.4 %collective-permute-start.2 = (bf16[528,256]{1,0:T(8,128)(2,1)S(1)}, bf16[528,256]{1,0:T(8,128)(2,1)S(1)}, u32[]{:S(2)}, u32[]{:S(2)}) collective-permute-start(bf16[528,256]{1,0:T(8,128)(2,1)S(1)} %get-tuple-element.27), channel_id=1, source_target_pairs={{0,2},{1,127},{2,4},{3,1},{4,6},{5,3},{6,8},{7,5},{8,10},{9,7},{10... | collective-permute-start | bytes 811016 | tf_op jit(solution)/shard_map/ppermute | solution.py:243
  20.0 19.2 %collective-permute-start.9 = (bf16[528,256]{1,0:T(8,128)(2,1)S(1)}, bf16[528,256]{1,0:T(8,128)(2,1)S(1)}, u32[]{:S(2)}, u32[]{:S(2)}) collective-permute-start(bf16[528,256]{1,0:T(8,128)(2,1)S(1)} %collective-permute-done.8.cols_ref), channel_id=1, source_target_pairs={{0,2},{1,127},{2,4},{3,1},{4,6},{5,3},{6,8},{7,5},{8,10},{9,7},{10... | collective-permute-start | bytes 811016 | tf_op jit(solution)/shard_map/ppermute | solution.py:243
  25.5 14.7 %collective-permute-start.7 = (bf16[528,256]{1,0:T(8,128)(2,1)S(1)}, bf16[528,256]{1,0:T(8,128)(2,1)S(1)}, u32[]{:S(2)}, u32[]{:S(2)}) collective-permute-start(bf16[528,256]{1,0:T(8,128)(2,1)S(1)} %collective-permute-done.6.cols_ref), channel_id=1, source_target_pairs={{0,2},{1,127},{2,4},{3,1},{4,6},{5,3},{6,8},{7,5},{8,10},{9,7},{10... | collective-permute-start | bytes 811016 | tf_op jit(solution)/shard_map/ppermute | solution.py:243
  30.0 11.2 %collective-permute-start.5 = (bf16[528,256]{1,0:T(8,128)(2,1)S(1)}, bf16[528,256]{1,0:T(8,128)(2,1)S(1)}, u32[]{:S(2)}, u32[]{:S(2)}) collective-permute-start(bf16[528,256]{1,0:T(8,128)(2,1)S(1)} %collective-permute-done.4.refs_6_.cols_ref), channel_id=1, source_target_pairs={{0,2},{1,127},{2,4},{3,1},{4,6},{5,3},{6,8},{7,5},{8,10},{9,7},{10... | collective-permute-start | bytes 811016 | tf_op jit(solution)/shard_map/ppermute | solution.py:243
  31.3 11.7 %collective-permute-start.3 = (bf16[528,256]{1,0:T(8,128)(2,1)S(1)}, bf16[528,256]{1,0:T(8,128)(2,1)S(1)}, u32[]{:S(2)}, u32[]{:S(2)}) collective-permute-start(bf16[528,256]{1,0:T(8,128)(2,1)S(1)} %collective-permute-done.2.refs_6_.cols_ref), channel_id=1, source_target_pairs={{0,2},{1,127},{2,4},{3,1},{4,6},{5,3},{6,8},{7,5},{8,10},{9,7},{10... | collective-permute-start | bytes 811016 | tf_op jit(solution)/shard_map/ppermute | solution.py:243
  42.9 1.1 %copy-start.1 = (bf16[528,256]{1,0:T(8,128)(2,1)S(1)}, bf16[528,256]{1,0:T(8,128)(2,1)}, u32[]{:S(2)}) copy-start(bf16[528,256]{1,0:T(8,128)(2,1)} %get-tuple-element.25.refs_0_.refs_2_.refs_3_) | copy-start | bytes 811012
  42.9 1.1 %copy-start.3 = (bf16[528,256]{1,0:T(8,128)(2,1)S(1)}, bf16[528,256]{1,0:T(8,128)(2,1)}, u32[]{:S(2)}) copy-start(bf16[528,256]{1,0:T(8,128)(2,1)} %get-tuple-element.26.refs_1_.refs_3_.refs_4_) | copy-start | bytes 811012
  43.9 2.0 %copy-start.4 = (bf16[1024,1024]{1,0:T(8,128)(2,1)S(1)}, bf16[1024,1024]{1,0:T(8,128)(2,1)}, u32[]{:S(2)}) copy-start(bf16[1024,1024]{1,0:T(8,128)(2,1)} %features_ref.3) | copy-start | bytes 6291460
  43.9 2.0 %copy-start.6 = (f32[1024,256]{1,0:T(8,128)S(1)}, f32[1024,256]{1,0:T(8,128)}, u32[]{:S(2)}) copy-start(f32[1024,256]{1,0:T(8,128)} %get-tuple-element.24.raw_ref) | copy-start | bytes 3145732
  43.9 2.0 %collective-permute-start.10 = (bf16[1024,256]{1,0:T(8,128)(2,1)S(1)}, bf16[1024,256]{1,0:T(8,128)(2,1)S(1)}, u32[]{:S(2)}, u32[]{:S(2)}) collective-permute-start(bf16[1024,256]{1,0:T(8,128)(2,1)S(1)} %shard_map.61), channel_id=1, source_target_pairs={{0,1},{1,0},{2,3},{3,2},{4,5},{5,4},{6,7},{7,6},{8,9},{9,8},{10,11... | collective-permute-start | bytes 1572872 | tf_op jit(solution)/shard_map/ppermute | solution.py:239
  45.9 6.1 %copy-start.5 = (bf16[1024,256]{1,0:T(8,128)(2,1)S(1)}, bf16[1024,256]{1,0:T(8,128)(2,1)}, u32[]{:S(2)}) copy-start(bf16[1024,256]{1,0:T(8,128)(2,1)} %head_ref.3) | copy-start | bytes 1572868
  48.0 17.7 %all-to-all-start = ((bf16[128,8,256]{2,1,0:T(8,128)(2,1)}), bf16[128,8,256]{2,1,0:T(8,128)(2,1)S(1)}, u32[]{:S(2)}, u32[]{:S(2)}) async-start(bf16[128,8,256]{2,1,0:T(8,128)(2,1)} %bitcast.7), calls=%async_computation | async-start | bytes 1048576 | tf_op jit(solution)/shard_map/all_to_all | solution.py:327
